TPU v7x, 32 devices: a whole 2x2x4 slice. The times are simulated.
32 devices in a mesh: tm: 16 (over z, y, x), rep: 2 (over core).
Axes of the slice: x: 2, y: 2, z: 4, core: 2. Of those that a mesh axis runs over, the one named last changes fastest.
Arguments:
- table: bfloat16 [2, 4096, 512], P(None, 'tm'), may hold values from -30 to 30
- cotangent: bfloat16 [2, 4096, 512], P(None, 'tm'), may hold values from -6 to 6
- stamps: int32 [2, 4096], P(None, 'tm'), may hold values from 0 to 12288, as said below
- starts: int32 [2, 4096], P(None, 'tm'), may hold values from 0 to 8191, as said below
- w_query: bfloat16 [512, 512], P(None, 'rep'), may hold values from -0.5 to 0.5
- w_key: bfloat16 [512, 512], P(None, 'rep'), may hold values from -0.5 to 0.5
- w_value: bfloat16 [512, 512], P(None, 'rep'), may hold values from -0.25 to 0.25
- w_out: bfloat16 [512, 512], P('rep'), may hold values from -0.25 to 0.25
- decay: float32 [4], P('rep'), may hold values from 0.0002 to 0.02
Outputs:
- mixed: bfloat16 [2, 4096, 512], P(None, 'tm')
- grad_table: bfloat16 [2, 4096, 512], P(None, 'tm')
- grad_query: float32 [512, 512], P(None, 'rep')
- grad_key: float32 [512, 512], P(None, 'rep')
- grad_value: float32 [512, 512], P(None, 'rep')
- grad_out: float32 [512, 512], P('rep')
Inputs may be any that keep to these rules, and one draw needn't show every extreme that they name: In time order the stamps never fall, successive rows differ by 0 to 3, the first row has stamp 0 and the last row has stamp 3 * 4096. For the row r in time order, starts lies between max(0, (r // 256 - 2) * 256) and r; the first row of each block reaches the lower end and the last row of each block starts at itself.
All inputs are finite; a program needn't handle non-finite values.
Results may differ from a plain program's by a relative error of at most 0.0045.
The roundings to bfloat16 on the way count: a program that leaves them out, or rounds other values in their place, can miss the bound.
Values may be sent and summed in bfloat16 or wider, within the bound.
No kernel may reach another device: no remote copies, remote signals or barrier semaphores. Data moves between devices by JAX's collectives and lax.ppermute only.
A program may use at most 64 MiB of HBM per device.

v0:
```python
import math

import jax
import jax.numpy as jnp
from jax import lax
from jax.sharding import PartitionSpec as P

HD = 128


def for_sending(shard):

    def short(part):
        return part.astype(jnp.bfloat16) if part.dtype == jnp.float32 else part

    return jax.tree.map(short, shard)


def passed_along(block, axis, distance):
    devices = range(lax.axis_size(axis))
    route = [(i - distance, i) for i in devices if i - distance in devices]
    return lax.ppermute(block, axis, route)


def attend(q_rows, window, key_times, q_times, q_first, first_blk, decay, grad_attn):
    blk_rows = q_rows.shape[0]
    head_cols = q_rows.shape[1]
    head_count = head_cols // HD
    inv_scale = 1.0 / math.sqrt(HD)
    q_heads = q_rows.reshape(blk_rows, head_count, HD)
    k_heads = window[:, :head_cols].reshape(3 * blk_rows, head_count, HD)
    v_heads = window[:, head_cols:].reshape(3 * blk_rows, head_count, HD)
    g_heads = grad_attn.reshape(blk_rows, head_count, HD)
    q_pos = first_blk * blk_rows + jnp.arange(blk_rows, dtype=jnp.int32)
    k_pos = (first_blk - 2) * blk_rows + jnp.arange(3 * blk_rows, dtype=jnp.int32)
    allowed = (k_pos[None, :] >= q_first[:, None]) & (k_pos[None, :] <= q_pos[:, None])
    time_gap = (q_times[:, None] - key_times[None, :]).astype(jnp.float32)
    scores = (
        jnp.einsum("qhd,khd->hqk", q_heads, k_heads, preferred_element_type=jnp.float32) * inv_scale
    )
    scores = scores - decay[:, None, None] * time_gap[None]
    scores = jnp.where(allowed[None], scores, -1e30)
    row_max = jnp.max(scores, -1, keepdims=True)
    weights = jnp.where(allowed[None], jnp.exp(scores - row_max), 0.0)
    probs = weights / jnp.sum(weights, -1, keepdims=True)
    probs_low = probs.astype(jnp.bfloat16)
    attn = jnp.einsum(
        "hqk,khd->qhd", probs_low, v_heads, preferred_element_type=jnp.float32
    ).astype(jnp.bfloat16)
    d_probs = jnp.einsum("qhd,khd->hqk", g_heads, v_heads, preferred_element_type=jnp.float32)
    delta = jnp.sum(probs * d_probs, -1, keepdims=True)
    d_scores = (probs * (d_probs - delta)).astype(jnp.bfloat16)
    d_query = (
        jnp.einsum("hqk,khd->qhd", d_scores, k_heads, preferred_element_type=jnp.float32)
        * inv_scale
    ).astype(jnp.bfloat16)
    d_key = (
        jnp.einsum("hqk,qhd->khd", d_scores, q_heads, preferred_element_type=jnp.float32)
        * inv_scale
    )
    d_value = jnp.einsum("hqk,qhd->khd", probs_low, g_heads, preferred_element_type=jnp.float32)
    d_window = jnp.concatenate(
        [d_key.reshape(3 * blk_rows, head_cols), d_value.reshape(3 * blk_rows, head_cols)], 1
    )
    return (attn.reshape(blk_rows, head_cols), d_query.reshape(blk_rows, head_cols), d_window)


def shards(table, cotangent, stamps, starts, w_query, w_key, w_value, w_out, decay):
    tm_size = lax.axis_size("tm")
    dev_index = lax.axis_index("tm")
    blk_rows = table.shape[1]
    width = table.shape[2]
    head_cols = w_query.shape[1]
    flat_rows = table.reshape(2 * blk_rows, width)
    flat_grad = cotangent.reshape(2 * blk_rows, width)
    queries = jnp.dot(flat_rows, w_query, preferred_element_type=jnp.float32).astype(jnp.bfloat16)
    key_rows = jnp.dot(flat_rows, w_key, preferred_element_type=jnp.float32).astype(jnp.bfloat16)
    val_rows = jnp.dot(flat_rows, w_value, preferred_element_type=jnp.float32).astype(jnp.bfloat16)
    packed = jnp.concatenate([key_rows, val_rows], 1).reshape(2, blk_rows, 2 * head_cols)
    grad_attn = jnp.dot(flat_grad, w_out.T, preferred_element_type=jnp.float32).astype(jnp.bfloat16)

    def kv_send(offset):
        if offset > 0:
            return (packed[0], stamps[0])
        if offset == -2:
            return (packed[1], stamps[1])
        return (packed, stamps)

    nearby = {}
    for offset in (1, 2, -1, -2):
        nearby[offset] = passed_along(for_sending(kv_send(offset)), "tm", offset)

    def pick(offset, which):
        got = nearby[offset]
        if offset != -1:
            return got
        return (got[0][which], got[1][which])

    low_m2 = pick(2, 0)
    low_m1 = pick(1, 0)
    high_p2 = pick(-2, 1)
    edge_low = pick(-1, 0)
    edge_high = pick(-1, 1)
    top_fold = dev_index <= tm_size - 3
    at_second = dev_index == tm_size - 2
    at_last = dev_index == tm_size - 1
    before_last = dev_index <= tm_size - 2
    low_window = jnp.concatenate([low_m2[0], low_m1[0], packed[0]], 0)
    low_times = jnp.concatenate([low_m2[1], low_m1[1], stamps[0]], 0)
    high_two = jnp.where(top_fold, high_p2[0], jnp.where(at_second, edge_low[0], low_m1[0]))
    high_two_t = jnp.where(top_fold, high_p2[1], jnp.where(at_second, edge_low[1], low_m1[1]))
    high_one = jnp.where(before_last, edge_high[0], packed[0])
    high_one_t = jnp.where(before_last, edge_high[1], stamps[0])
    high_window = jnp.concatenate([high_two, high_one, packed[1]], 0)
    high_times = jnp.concatenate([high_two_t, high_one_t, stamps[1]], 0)
    low_attn, low_dq, low_dwin = attend(
        queries[:blk_rows],
        low_window,
        low_times,
        stamps[0],
        starts[0],
        dev_index,
        decay,
        grad_attn[:blk_rows],
    )
    high_attn, high_dq, high_dwin = attend(
        queries[blk_rows:],
        high_window,
        high_times,
        stamps[1],
        starts[1],
        2 * tm_size - 1 - dev_index,
        decay,
        grad_attn[blk_rows:],
    )
    attn_all = jnp.concatenate([low_attn, high_attn], 0)
    dq_all = jnp.concatenate([low_dq, high_dq], 0)
    partial_out = jnp.dot(attn_all, w_out, preferred_element_type=jnp.float32)
    mixed = lax.psum(partial_out, "rep").astype(jnp.bfloat16).reshape(2, blk_rows, width)
    low_two, low_one, low_own = (
        low_dwin[:blk_rows],
        low_dwin[blk_rows : 2 * blk_rows],
        low_dwin[2 * blk_rows :],
    )
    hi_two, hi_one, hi_own = (
        high_dwin[:blk_rows],
        high_dwin[blk_rows : 2 * blk_rows],
        high_dwin[2 * blk_rows :],
    )
    near_one = low_one + jnp.where(at_last, hi_two, 0.0)
    far_two = jnp.where(top_fold, hi_two, 0.0)
    grad_near = {}
    grad_near[-1] = jnp.stack(
        [jnp.where(at_second, hi_two, 0.0), jnp.where(before_last, hi_one, 0.0)]
    )
    grad_near[2] = low_two
    grad_near[1] = near_one
    grad_near[-2] = far_two
    grad_own = jnp.stack([low_own + jnp.where(at_last, hi_one, 0.0), hi_own])

    def absorb(total, got, offset):
        if offset > 0:
            return total.at[0].add(got)
        if offset == -2:
            return total.at[1].add(got)
        return total + got

    for offset in (1, 2, -1, -2):
        grad_own = absorb(grad_own, passed_along(grad_near[offset], "tm", -offset), offset)
    grad_own = grad_own.reshape(2 * blk_rows, 2 * head_cols)
    dk_all = grad_own[:, :head_cols].astype(jnp.bfloat16)
    dv_all = grad_own[:, head_cols:].astype(jnp.bfloat16)
    partial_in = (
        jnp.dot(dq_all, w_query.T, preferred_element_type=jnp.float32)
        + jnp.dot(dk_all, w_key.T, preferred_element_type=jnp.float32)
        + jnp.dot(dv_all, w_value.T, preferred_element_type=jnp.float32)
    )
    grad_table = lax.psum(partial_in, "rep").astype(jnp.bfloat16).reshape(2, blk_rows, width)
    grad_scale = 1.0 / math.sqrt(2 * blk_rows * tm_size)
    contract = (((0,), (0,)), ((), ()))
    term_query = (
        lax.dot_general(flat_rows, dq_all, contract, preferred_element_type=jnp.float32)
        * grad_scale
    )
    term_key = (
        lax.dot_general(flat_rows, dk_all, contract, preferred_element_type=jnp.float32)
        * grad_scale
    )
    term_value = (
        lax.dot_general(flat_rows, dv_all, contract, preferred_element_type=jnp.float32)
        * grad_scale
    )
    term_out = (
        lax.dot_general(attn_all, flat_grad, contract, preferred_element_type=jnp.float32)
        * grad_scale
    )
    grad_query, grad_key, grad_value, grad_out = lax.psum(
        (term_query, term_key, term_value, term_out), "tm"
    )
    return (mixed, grad_table, grad_query, grad_key, grad_value, grad_out)


def solution(mesh):
    return jax.shard_map(
        shards,
        mesh=mesh,
        in_specs=(
            P(None, "tm", None),
            P(None, "tm", None),
            P(None, "tm"),
            P(None, "tm"),
            P(None, "rep"),
            P(None, "rep"),
            P(None, "rep"),
            P("rep", None),
            P("rep"),
        ),
        out_specs=(
            P(None, "tm", None),
            P(None, "tm", None),
            P(None, "rep"),
            P(None, "rep"),
            P(None, "rep"),
            P("rep", None),
        ),
        check_vma=False,
    )
```

profile of v0, /device:TPU:0, one launch (start us, length us, event | category | flops | bytes accessed | tf_op | source)
XLA Modules:
  0.0 268.5 jit_solution(11343078785372608933)
XLA Ops:
  7.2 1.4 collective-permute-start.7
  9.4 5.4 %collective-permute-start.3 = (s32[256]{0:T(256)S(1)}, s32[256]{0:T(256)S(1)}, u32[]{:S(2)}, u32[]{:S(2)}) collective-permute-start(s32[256]{0:T(256)S(1)} %bitcast.157), channel_id=1, source_target_pairs={{0,2},{2,4},{4,6},{6,8},{8,10},{10,12},{12,14},{14,16},{16,18},{18... | collective-permute-start | bytes 3080 | tf_op jit(solution)/shard_map/ppermute | solution.py:22
  14.9 4.0 %collective-permute-start.2 = (s32[256]{0:T(256)S(1)}, s32[256]{0:T(256)S(1)}, u32[]{:S(2)}, u32[]{:S(2)}) collective-permute-start(s32[256]{0:T(256)S(1)} %bitcast.158), channel_id=1, source_target_pairs={{0,4},{2,6},{4,8},{6,10},{8,12},{10,14},{12,16},{14,18},{16,20},{1... | collective-permute-start | bytes 3080 | tf_op jit(solution)/shard_map/ppermute | solution.py:22
  18.8 1.3 convolution_convert_fusion.2
  20.1 1.3 convolution_convert_fusion.3
  21.6 1.4 collective-permute-start.5
  23.0 1.3 collective-permute-start.6
  28.4 1.0 subtract_convert_fusion.1
  29.4 2.4 collective-permute-done.6
  31.9 6.2 %collective-permute-done.5 = bf16[2,256,512]{1,2,0:T(8,128)(2,1)S(1)} collective-permute-done((bf16[2,256,512]{1,2,0:T(8,128)(2,1)S(1)}, bf16[2,256,512]{1,2,0:T(8,128)(2,1)S(1)}, u32[]{:S(2)}, u32[]{:S(2)}) %collective-permute-start.5) | collective-permute-done | bytes 524320 | tf_op jit(solution)/shard_map/ppermute | solution.py:22
  38.8 1.3 collective-permute-start.4
  40.1 4.6 %collective-permute-start.1 = (bf16[256,512]{0,1:T(8,128)(2,1)}, bf16[256,512]{0,1:T(8,128)(2,1)S(1)}, u32[]{:S(2)}, u32[]{:S(2)}) collective-permute-start(bf16[256,512]{0,1:T(8,128)(2,1)} %get-tuple-element.63), channel_id=1, source_target_pairs={{0,2},{2,4},{4,6},{6,8},{8,10},{10,12},{12,14},{14,16},{16,18},{18... | collective-permute-start | bytes 786440 | tf_op jit(solution)/shard_map/ppermute | solution.py:22
  44.7 1.0 subtract_convert_fusion
  45.7 5.3 %collective-permute-start = (bf16[256,512]{0,1:T(8,128)(2,1)}, bf16[256,512]{0,1:T(8,128)(2,1)}, u32[]{:S(2)}, u32[]{:S(2)}) collective-permute-start(bf16[256,512]{0,1:T(8,128)(2,1)} %get-tuple-element.63), channel_id=1, source_target_pairs={{0,4},{2,6},{4,8},{6,10},{8,12},{10,14},{12,16},{14,18},{16,20},{1... | collective-permute-start | bytes 786440 | tf_op jit(solution)/shard_map/ppermute | solution.py:22
  52.3 2.3 fusion.52
  59.2 1.1 pad_maximum_fusion.2
  61.0 3.4 %fusion.53 = (f32[2,256]{1,0:T(2,128)S(1)}, f32[2,256,768]{2,1,0:T(8,128)}) fusion(bf16[256,2,128]{0,2,1:T(8,128)(2,1)S(1)} %bitcast.145, bf16[768,2,128]{0,2,1:T(8,128)(2,1)S(1)} %bitcast.133, f32[256,768]{1,0:T(8,128)} %subtract_convert_fusion.1, f32[2]{0:T(128)S(1)} %copy-done.23, pred[256,768]{1,0:T(8,128)(4,1)} %compare_and_fusion.1), kind=kOutput, calls=%fused_computation.120 | convolution fusion | flops 103416576 | bytes 3082248 | tf_op jit(solution)/shard_map/sub | solution.py:44
  64.5 2.1 convolution_convert_fusion.5
  69.2 1.3 collective-permute-start.8
  70.5 1.3 collective-permute-start.9
  71.8 5.4 %collective-permute-start.10 = (f32[2,256,512]{1,2,0:T(8,128)S(1)}, f32[2,256,512]{1,2,0:T(8,128)S(1)}, u32[]{:S(2)}, u32[]{:S(2)}) collective-permute-start(f32[2,256,512]{1,2,0:T(8,128)S(1)} %pad_maximum_fusion.1), channel_id=1, source_target_pairs={{0,2},{2,4},{4,6},{6,8},{8,10},{10,12},{12,14},{14,16},{16,18},{18... | collective-permute-start | bytes 3145736 | tf_op jit(solution)/shard_map/ppermute | solution.py:22
  77.2 6.4 %collective-permute-start.11 = (f32[256,512]{0,1:T(8,128)S(1)}, f32[256,512]{0,1:T(8,128)S(1)}, u32[]{:S(2)}, u32[]{:S(2)}) collective-permute-start(f32[256,512]{0,1:T(8,128)S(1)} %get-tuple-element.60), channel_id=1, source_target_pairs={{0,4},{2,6},{4,8},{6,10},{8,12},{10,14},{12,16},{14,18},{16,20},{1... | collective-permute-start | bytes 1572872 | tf_op jit(solution)/shard_map/ppermute | solution.py:22
  83.6 1.1 fusion.6
  84.8 1.1 convolution_multiply_fusion.2
  87.7 18.5 %collective-permute-done.10 = f32[2,256,512]{1,2,0:T(8,128)S(1)} collective-permute-done((f32[2,256,512]{1,2,0:T(8,128)S(1)}, f32[2,256,512]{1,2,0:T(8,128)S(1)}, u32[]{:S(2)}, u32[]{:S(2)}) %collective-permute-start.10) | collective-permute-done | bytes 1048608 | tf_op jit(solution)/shard_map/ppermute | solution.py:22
  106.3 17.7 %collective-permute-done.11 = f32[256,512]{0,1:T(8,128)S(1)} collective-permute-done((f32[256,512]{0,1:T(8,128)S(1)}, f32[256,512]{0,1:T(8,128)S(1)}, u32[]{:S(2)}, u32[]{:S(2)}) %collective-permute-start.11) | collective-permute-done | bytes 524320 | tf_op jit(solution)/shard_map/ppermute | solution.py:22
  124.4 1.1 fusion.5
  125.5 1.1 fusion.4
  129.2 9.3 %all-reduce.6 = (bf16[512,512]{1,0:T(8,128)(2,1)}, bf16[512,512]{1,0:T(8,128)(2,1)}) all-reduce(f32[512,512]{1,0:T(8,128)S(1)} %fusion.33, f32[512,512]{1,0:T(8,128)S(1)} %convolution_add_fusion), channel_id=1, replica_groups=mesh['tm'=16,'rep'=2] {'rep'}, use_global_device_ids=true, to_apply=%region_4.5 | all-reduce | flops 524288 | bytes 3145728 | tf_op jit(solution)/shard_map/psum | solution.py:139
  138.5 117.1 %all-reduce.5.cloned.1.call-done = (f32[512,256]{0,1:T(8,128)}, f32[512,256]{0,1:T(8,128)}, f32[512,256]{0,1:T(8,128)}, f32[256,512]{1,0:T(8,128)}) async-done(((f32[512,256]{0,1:T(8,128)}, f32[512,256]{0,1:T(8,128)}, f32[512,256]{0,1:T(8,128)}, f32[256,512]{1,0:T(8,128)}), (f32[512,256]{0,1:T(8,128)}, f32[512,256]{0,1:T(8,128)}, f32[512,256]{0,1:T(8,128)}, ...) | async-done | bytes 2097168 | tf_op jit(solution)/shard_map/psum | solution.py:197
  255.7 2.1 copy.37
  257.8 2.0 copy.38
  (109 shorter events, 21.4 us)
Async XLA Ops:
  7.2 11.7 %copy-start = (bf16[2,256,512]{2,1,0:T(8,128)(2,1)S(1)}, bf16[2,256,512]{2,1,0:T(8,128)(2,1)}, u32[]{:S(2)}) copy-start(bf16[2,256,512]{2,1,0:T(8,128)(2,1)} %param.15) | copy-start | bytes 1572868
  7.2 248.5 %all-reduce.5.cloned.1.call-start = ((), (), s32[]{:S(2)}) async-start(), calls=%async_computation | async-start | bytes 4194304 | tf_op jit(solution)/shard_map/psum | solution.py:197
  7.2 22.2 %collective-permute-start.7 = (s32[2,256]{1,0:T(2,128)}, s32[2,256]{1,0:T(2,128)S(1)}, u32[]{:S(2)}, u32[]{:S(2)}) collective-permute-start(s32[2,256]{1,0:T(2,128)} %param.17), channel_id=1, source_target_pairs={{2,0},{4,2},{6,4},{8,6},{10,8},{12,10},{14,12},{16,14},{18,16},{20... | collective-permute-start | bytes 6152 | tf_op jit(solution)/shard_map/ppermute | solution.py:22
  9.4 18.9 %collective-permute-start.3 = (s32[256]{0:T(256)S(1)}, s32[256]{0:T(256)S(1)}, u32[]{:S(2)}, u32[]{:S(2)}) collective-permute-start(s32[256]{0:T(256)S(1)} %bitcast.157), channel_id=1, source_target_pairs={{0,2},{2,4},{4,6},{6,8},{8,10},{10,12},{12,14},{14,16},{16,18},{18... | collective-permute-start | bytes 3080 | tf_op jit(solution)/shard_map/ppermute | solution.py:22
  14.9 13.5 %collective-permute-start.2 = (s32[256]{0:T(256)S(1)}, s32[256]{0:T(256)S(1)}, u32[]{:S(2)}, u32[]{:S(2)}) collective-permute-start(s32[256]{0:T(256)S(1)} %bitcast.158), channel_id=1, source_target_pairs={{0,4},{2,6},{4,8},{6,10},{8,12},{10,14},{12,16},{14,18},{16,20},{1... | collective-permute-start | bytes 3080 | tf_op jit(solution)/shard_map/ppermute | solution.py:22
  20.1 4.2 %copy-start.11 = (bf16[512,256]{1,0:T(8,128)(2,1)S(1)}, bf16[512,256]{1,0:T(8,128)(2,1)}, u32[]{:S(2)}) copy-start(bf16[512,256]{1,0:T(8,128)(2,1)} %param.19) | copy-start | bytes 786436
  21.5 3.9 %copy-start.22 = (s32[2,256]{1,0:T(2,128)S(1)}, s32[2,256]{1,0:T(2,128)}, u32[]{:S(2)}) copy-start(s32[2,256]{1,0:T(2,128)} %param.18) | copy-start | bytes 6148
  21.5 3.9 %copy-start.1 = (bf16[2,256,512]{2,1,0:T(8,128)(2,1)S(1)}, bf16[2,256,512]{2,1,0:T(8,128)(2,1)}, u32[]{:S(2)}) copy-start(bf16[2,256,512]{2,1,0:T(8,128)(2,1)} %param.16) | copy-start | bytes 1572868
  21.6 3.9 %copy-start.9 = (bf16[256,512]{1,0:T(8,128)(2,1)S(1)}, bf16[256,512]{1,0:T(8,128)(2,1)}, u32[]{:S(2)}) copy-start(bf16[256,512]{1,0:T(8,128)(2,1)} %param.22) | copy-start | bytes 786436
  21.6 16.4 %collective-permute-start.5 = (bf16[2,256,512]{1,2,0:T(8,128)(2,1)S(1)}, bf16[2,256,512]{1,2,0:T(8,128)(2,1)S(1)}, u32[]{:S(2)}, u32[]{:S(2)}) collective-permute-start(bf16[2,256,512]{1,2,0:T(8,128)(2,1)S(1)} %bitcast.144), channel_id=1, source_target_pairs={{2,0},{4,2},{6,4},{8,6},{10,8},{12,10},{14,12},{16,14},{18,16},{20... | collective-permute-start | bytes 1572872 | tf_op jit(solution)/shard_map/ppermute | solution.py:22
  23.0 8.8 %collective-permute-start.6 = (s32[256]{0:T(256)S(1)}, s32[256]{0:T(256)S(1)}, u32[]{:S(2)}, u32[]{:S(2)}) collective-permute-start(s32[256]{0:T(256)S(1)} %bitcast.162), channel_id=1, source_target_pairs={{4,0},{6,2},{8,4},{10,6},{12,8},{14,10},{16,12},{18,14},{20,16},{2... | collective-permute-start | bytes 3080 | tf_op jit(solution)/shard_map/ppermute | solution.py:22
  25.4 26.4 %copy-start.17 = (bf16[256,256]{0,1:T(8,128)(2,1)}, bf16[256,256]{0,1:T(8,128)(2,1)S(1)}, u32[]{:S(2)}) copy-start(bf16[256,256]{0,1:T(8,128)(2,1)S(1)} %get-tuple-element.78) | copy-start | bytes 393220
  38.8 12.2 %collective-permute-start.4 = (bf16[256,512]{0,1:T(8,128)(2,1)S(1)}, bf16[256,512]{0,1:T(8,128)(2,1)S(1)}, u32[]{:S(2)}, u32[]{:S(2)}) collective-permute-start(bf16[256,512]{0,1:T(8,128)(2,1)S(1)} %get-tuple-element.74), channel_id=1, source_target_pairs={{4,0},{6,2},{8,4},{10,6},{12,8},{14,10},{16,12},{18,14},{20,16},{2... | collective-permute-start | bytes 786440 | tf_op jit(solution)/shard_map/ppermute | solution.py:22
  40.1 10.9 %collective-permute-start.1 = (bf16[256,512]{0,1:T(8,128)(2,1)}, bf16[256,512]{0,1:T(8,128)(2,1)S(1)}, u32[]{:S(2)}, u32[]{:S(2)}) collective-permute-start(bf16[256,512]{0,1:T(8,128)(2,1)} %get-tuple-element.63), channel_id=1, source_target_pairs={{0,2},{2,4},{4,6},{6,8},{8,10},{10,12},{12,14},{14,16},{16,18},{18... | collective-permute-start | bytes 786440 | tf_op jit(solution)/shard_map/ppermute | solution.py:22
  45.7 13.5 %collective-permute-start = (bf16[256,512]{0,1:T(8,128)(2,1)}, bf16[256,512]{0,1:T(8,128)(2,1)}, u32[]{:S(2)}, u32[]{:S(2)}) collective-permute-start(bf16[256,512]{0,1:T(8,128)(2,1)} %get-tuple-element.63), channel_id=1, source_target_pairs={{0,4},{2,6},{4,8},{6,10},{8,12},{10,14},{12,16},{14,18},{16,20},{1... | collective-permute-start | bytes 786440 | tf_op jit(solution)/shard_map/ppermute | solution.py:22
  51.8 2.9 %copy-start.3 = (bf16[768,256]{0,1:T(8,128)(2,1)}, bf16[768,256]{0,1:T(8,128)(2,1)S(1)}, u32[]{:S(2)}) copy-start(bf16[768,256]{0,1:T(8,128)(2,1)S(1)} %get-tuple-element.71) | copy-start | bytes 1179652
  57.3 1.0 copy-start.4
  57.3 1.8 copy-start.8
  58.7 2.3 copy-start.15
  64.5 2.2 copy-start.2
  64.5 2.2 copy-start.19
  64.5 2.2 copy-start.20
  69.2 17.5 %collective-permute-start.8 = (f32[256,512]{0,1:T(8,128)S(1)}, f32[256,512]{0,1:T(8,128)S(1)}, u32[]{:S(2)}, u32[]{:S(2)}) collective-permute-start(f32[256,512]{0,1:T(8,128)S(1)} %get-tuple-element.67), channel_id=1, source_target_pairs={{2,0},{4,2},{6,4},{8,6},{10,8},{12,10},{14,12},{16,14},{18,16},{20... | collective-permute-start | bytes 1572872 | tf_op jit(solution)/shard_map/ppermute | solution.py:22
  70.5 17.1 %collective-permute-start.9 = (f32[256,512]{0,1:T(8,128)S(1)}, f32[256,512]{0,1:T(8,128)S(1)}, u32[]{:S(2)}, u32[]{:S(2)}) collective-permute-start(f32[256,512]{0,1:T(8,128)S(1)} %get-tuple-element.66), channel_id=1, source_target_pairs={{4,0},{6,2},{8,4},{10,6},{12,8},{14,10},{16,12},{18,14},{20,16},{2... | collective-permute-start | bytes 1572872 | tf_op jit(solution)/shard_map/ppermute | solution.py:22
  71.8 34.3 %collective-permute-start.10 = (f32[2,256,512]{1,2,0:T(8,128)S(1)}, f32[2,256,512]{1,2,0:T(8,128)S(1)}, u32[]{:S(2)}, u32[]{:S(2)}) collective-permute-start(f32[2,256,512]{1,2,0:T(8,128)S(1)} %pad_maximum_fusion.1), channel_id=1, source_target_pairs={{0,2},{2,4},{4,6},{6,8},{8,10},{10,12},{12,14},{14,16},{16,18},{18... | collective-permute-start | bytes 3145736 | tf_op jit(solution)/shard_map/ppermute | solution.py:22
  77.2 46.8 %collective-permute-start.11 = (f32[256,512]{0,1:T(8,128)S(1)}, f32[256,512]{0,1:T(8,128)S(1)}, u32[]{:S(2)}, u32[]{:S(2)}) collective-permute-start(f32[256,512]{0,1:T(8,128)S(1)} %get-tuple-element.60), channel_id=1, source_target_pairs={{0,4},{2,6},{4,8},{6,10},{8,12},{10,14},{12,16},{14,18},{16,20},{1... | collective-permute-start | bytes 1572872 | tf_op jit(solution)/shard_map/ppermute | solution.py:22
  125.5 1.1 copy-start.10
  126.6 0.9 copy-start.12
  126.7 1.3 copy-start.5
  128.0 1.0 copy-start.6
  255.7 4.2 %copy-start.14 = (f32[512,256]{0,1:T(8,128)S(1)}, f32[512,256]{0,1:T(8,128)}, u32[]{:S(2)}) copy-start(f32[512,256]{0,1:T(8,128)} %get-tuple-element.56) | copy-start | bytes 1572868
  255.7 5.2 %copy-start.13 = (f32[256,512]{1,0:T(8,128)S(1)}, f32[256,512]{1,0:T(8,128)}, u32[]{:S(2)}) copy-start(f32[256,512]{1,0:T(8,128)} %get-tuple-element.98) | copy-start | bytes 1572868
  (5 other events, 4.1 us)
Sparse Core Ops, SparseCore 0:
  126.8 128.8 all-reduce.4
where the time goes:
time: 269 us; the launch traced here: 268 us
  waiting for transfers between devices  164 us (61%)
  starting transfers between devices  39 us (14%)
  matrix products  20.5 us (8%)
  between operations  14.6 us (5%)
  local copies, waits for them, and re-layouts  13.6 us (5%)
  blocking collectives  9.29 us (3%)
  other arithmetic  7.53 us (3%)
    psum x1, waiting for transfers between devices, shards(): lax.psum((term_query, term_key, term_value, term_out), 'tm')  117 us
    ppermute x12, waiting for transfers between devices, passed_along(): return lax.ppermute(block, axis, route)  46.8 us
    ppermute x12, starting transfers between devices, passed_along(): return lax.ppermute(block, axis, route)  39 us
    unnamed x52, local copies, waits for them, and re-layouts  10.3 us
    psum x1, blocking collectives, shards(): lax.psum(partial_out, 'rep').astype(jnp.bfloat16)  9.29 us
    sub x2, matrix products, attend(): weights = jnp.where(allowed[None], jnp.exp(scores - row_max), 0.0)  5.74 us
  transfers between devices with their start and end apart: 13, of which 8 were waited for; matrix products, arithmetic and copies ran while one was open for 7% of the time, Pallas kernels for 0%

commit v1 on v0

v1 whole, which is shorter than its diff:
```python
import functools
import math

import jax
import jax.numpy as jnp
from jax import lax
from jax.experimental import pallas as pl
from jax.experimental.pallas import tpu as pltpu
from jax.sharding import PartitionSpec as P

HD = 128
BF = jnp.bfloat16
F32 = jnp.float32
AXES = ("tm", "rep")
LOG2E = math.log2(math.e)


def dot(a, b, dims=((1,), (0,))):
    return lax.dot_general(a, b, (dims, ((), ())), preferred_element_type=F32)


def swap_cores(x):
    return lax.ppermute(x, "rep", [(0, 1), (1, 0)])


def shift_blocks(x, distance):
    n = lax.axis_size("tm")

    def worker(b):
        return 2 * b if b < n else 2 * (2 * n - 1 - b) + 1

    route = [(worker(b), worker((b + distance) % (2 * n))) for b in range(2 * n)]
    return lax.ppermute(x, AXES, route)


def bit_orders():
    bits = lax.axis_size("tm").bit_length() - 1
    count = min(3, bits)
    first = list(range(count))
    return first, first[-1:] + first[:-1], list(range(count, bits))


def partners(bit0, bit1):
    n = lax.axis_size("tm")
    pairs = []
    for i in range(n):
        pairs += [(2 * i, 2 * (i ^ (1 << bit0))), (2 * i + 1, 2 * (i ^ (1 << bit1)) + 1)]
    return pairs


def my_bit(bit0, bit1):
    index = lax.axis_index("tm")
    return jnp.where(lax.axis_index("rep") == 0, (index >> bit0) & 1, (index >> bit1) & 1)


def sum_over_tm(total):
    order0, order1, rest = bit_orders()
    for bit0, bit1 in zip(order0, order1):
        mine = my_bit(bit0, bit1)
        half = total.shape[0] // 2
        send = lax.dynamic_slice_in_dim(total, (1 - mine) * half, half, 0).astype(BF)
        keep = lax.dynamic_slice_in_dim(total, mine * half, half, 0)
        total = keep + lax.ppermute(send, AXES, partners(bit0, bit1)).astype(F32)
    for bit in rest:
        own = total.astype(BF)
        total = own.astype(F32) + lax.ppermute(own, AXES, partners(bit, bit)).astype(F32)
    whole = total.astype(BF)
    for bit0, bit1 in zip(order0[::-1], order1[::-1]):
        got = lax.ppermute(whole, AXES, partners(bit0, bit1))
        mine = my_bit(bit0, bit1)
        whole = jnp.where(
            mine == 1, jnp.concatenate([got, whole], 0), jnp.concatenate([whole, got], 0)
        )
    return whole


def attend_kernel(decay_ref, q_ref, k_ref, v_ref, g_ref, gap_ref, first_ref, o_ref, dq_ref, dk_ref, dv_ref):
    head = pl.program_id(0)
    rows, keys = q_ref.shape[0], k_ref.shape[0]
    inv_scale = 1.0 / math.sqrt(HD)
    q, k, v, g = q_ref[...], k_ref[...], v_ref[...], g_ref[...]
    at_key = lax.broadcasted_iota(jnp.int32, (rows, keys), 1)
    at_row = lax.broadcasted_iota(jnp.int32, (rows, keys), 0) + (keys - rows)
    allowed = (at_key >= first_ref[...]) & (at_key <= at_row)
    bias = gap_ref[...] * (decay_ref[head] * LOG2E)
    scores = dot(q, k, ((1,), (1,))) * (inv_scale * LOG2E) - bias
    scores = jnp.where(allowed, scores, -1e30)
    weights = jnp.exp2(scores - jnp.max(scores, -1, keepdims=True))
    probs = weights * (1.0 / jnp.sum(weights, -1, keepdims=True))
    low = probs.astype(BF)
    o_ref[...] = dot(low, v).astype(BF)
    dv_ref[...] = dot(low, g, ((0,), (0,))).astype(BF)
    d_probs = dot(g, v, ((1,), (1,)))
    delta = jnp.sum(probs * d_probs, -1, keepdims=True)
    d_scores = (probs * (d_probs - delta)).astype(BF)
    dq_ref[...] = (dot(d_scores, k) * inv_scale).astype(BF)
    dk_ref[...] = (dot(d_scores, q, ((0,), (0,))) * inv_scale).astype(BF)


def attend(q, k, v, g, gap, first, decay):
    rows, width = q.shape
    keys = k.shape[0]
    near = pl.BlockSpec((rows, HD), lambda h: (0, h))
    wide = pl.BlockSpec((keys, HD), lambda h: (0, h))
    return pl.pallas_call(
        attend_kernel,
        grid=(width // HD,),
        in_specs=[
            pl.BlockSpec(memory_space=pltpu.SMEM),
            near,
            wide,
            wide,
            near,
            pl.BlockSpec((1, keys), lambda h: (0, 0)),
            pl.BlockSpec((rows, 1), lambda h: (0, 0)),
        ],
        out_specs=[near, near, wide, wide],
        out_shape=[
            jax.ShapeDtypeStruct((rows, width), BF),
            jax.ShapeDtypeStruct((rows, width), BF),
            jax.ShapeDtypeStruct((keys, width), BF),
            jax.ShapeDtypeStruct((keys, width), BF),
        ],
        compiler_params=pltpu.CompilerParams(vmem_limit_bytes=40 * 1024 * 1024),
        name="attend",
    )(decay, q, k, v, g, gap, first)


def shards(table, cotangent, stamps, starts, w_query, w_key, w_value, w_out, decay):
    n = lax.axis_size("tm")
    index = lax.axis_index("tm")
    core = lax.axis_index("rep")
    blk = table.shape[1]
    width = table.shape[2]
    cols = w_query.shape[1]
    block = jnp.where(core == 0, index, 2 * n - 1 - index)

    x_own = lax.dynamic_index_in_dim(table, core, 0, False)
    g_own = lax.dynamic_index_in_dim(cotangent, core, 0, False)
    t_own = lax.dynamic_index_in_dim(stamps, core, 0, False)
    first = lax.dynamic_index_in_dim(starts, core, 0, False)
    pieces = jnp.stack([t_own & 255, (t_own >> 8) & 255, t_own >> 16]).astype(BF)
    pieces = jnp.pad(pieces, ((0, 13), (0, width - blk)))
    parcel = jnp.concatenate([x_own, pieces], 0)
    back_one = shift_blocks(parcel, 1)
    back_two = shift_blocks(parcel, 2)

    w_all = jnp.concatenate([w_query, w_key, w_value], 1)
    w_all_other = swap_cores(w_all)
    w_out_other = swap_cores(w_out)
    decay_here = jnp.concatenate([decay, swap_cores(decay)])

    def joined(which):
        return jnp.concatenate(
            [w[:, which * cols : (which + 1) * cols] for w in (w_all, w_all_other)], 1
        )

    wq, wk, wv = joined(0), joined(1), joined(2)
    wo = jnp.concatenate([w_out, w_out_other], 0)

    q = dot(x_own, wq).astype(BF)
    g_attn = dot(g_own, wo, ((1,), (1,))).astype(BF)

    x_win = jnp.concatenate([back_two[:blk], back_one[:blk], x_own], 0)

    def times(parcel):
        p = parcel[blk : blk + 3, :blk].astype(F32)
        return p[0] + 256.0 * p[1] + 65536.0 * p[2]

    t_self = t_own.astype(F32)
    t_win = jnp.concatenate([times(back_two), times(back_one), t_self])
    gap = (t_self[-1] - t_win)[None]
    first_local = (first - (block - 2) * blk)[:, None]

    k_win = dot(x_win, wk).astype(BF)
    v_win = dot(x_win, wv).astype(BF)
    attn, dq, dk, dv = attend(q, k_win, v_win, g_attn, gap, first_local, decay_here)

    scale = 1.0 / math.sqrt(2 * blk * n)
    contract = ((0,), (0,))
    term_out = dot(attn, g_own, contract) * scale
    term_value = dot(x_win, dv, contract) * scale
    term_query = dot(x_own, dq, contract) * scale
    term_key = dot(x_win, dk, contract) * scale

    def both_cores(columns, rows=None):
        away = [m[:, cols:] for m in columns]
        here = [m[:, :cols] for m in columns]
        if rows is not None:
            away += [rows[cols:, :cols], rows[cols:, cols:]]
            here += [rows[:cols, :cols], rows[:cols, cols:]]
        return jnp.concatenate(here, 0) + swap_cores(jnp.concatenate(away, 0))

    sum_a = sum_over_tm(both_cores([term_value], term_out))
    sum_b = sum_over_tm(both_cores([term_query, term_key]))

    mixed_own = dot(attn, wo).astype(BF)

    def into_rows(dk_part, dv_part):
        return dot(dk_part, wk, ((1,), (1,))) + dot(dv_part, wv, ((1,), (1,)))

    to_two = into_rows(dk[:blk], dv[:blk]).astype(BF)
    to_one = into_rows(dk[blk : 2 * blk], dv[blk : 2 * blk]).astype(BF)
    to_self = dot(dq, wq, ((1,), (1,))) + into_rows(dk[2 * blk :], dv[2 * blk :])
    grad_own = (
        to_self
        + shift_blocks(to_one, -1).astype(F32)
        + shift_blocks(to_two, -2).astype(F32)
    ).astype(BF)

    def both_blocks(own):
        other = swap_cores(own)
        return jnp.where(core == 0, jnp.stack([own, other]), jnp.stack([other, own]))

    mixed = both_blocks(mixed_own)
    grad_table = both_blocks(grad_own)
    wide = width // 2
    grad_value = sum_a[:width].astype(F32)
    grad_out = jnp.concatenate(
        [sum_a[width : width + cols], sum_a[width + cols :]], 1
    ).astype(F32)
    grad_query = sum_b[:width].astype(F32)
    grad_key = sum_b[width:].astype(F32)
    return (mixed, grad_table, grad_query, grad_key, grad_value, grad_out)


def solution(mesh):
    return jax.shard_map(
        shards,
        mesh=mesh,
        in_specs=(
            P(None, "tm", None),
            P(None, "tm", None),
            P(None, "tm"),
            P(None, "tm"),
            P(None, "rep"),
            P(None, "rep"),
            P(None, "rep"),
            P("rep", None),
            P("rep"),
        ),
        out_specs=(
            P(None, "tm", None),
            P(None, "tm", None),
            P(None, "rep"),
            P(None, "rep"),
            P(None, "rep"),
            P("rep", None),
        ),
        check_vma=False,
    )
```

time: 269 us -> 86.4 us (0.32)
  waiting for transfers between devices: 164 us -> 28.1 us
  matrix products: 20.5 us -> 6.26 us
  between operations: 14.6 us -> 1.14 us
  starting transfers between devices: 39 us -> 26.9 us
  blocking collectives: 9.29 us -> 0 us
  Pallas kernels: 0 us -> 7.34 us
  local copies, waits for them, and re-layouts: 13.6 us -> 6.32 us
    psum x1 -> x0, waiting for transfers between devices: 117 us -> none  [shards(): lax.psum((term_query, term_key, term_value, term_out), 'tm')]
    ppermute x12 -> x25, waiting for transfers between devices: 46.8 us -> 28.1 us  [the longest x6 15 us: sum_over_tm(): total = keep + lax.ppermute(send, AXES, partners(bit0, bit1)).astype(F32)]
    ppermute x12 -> x25, starting transfers between devices: 39 us -> 26.9 us  [the longest x6 7.65 us: sum_over_tm(): total = keep + lax.ppermute(send, AXES, partners(bit0, bit1)).astype(F32)]
    unnamed x52 -> x19, local copies, waits for them, and re-layouts: 10.3 us -> 0.43 us
    psum x1 -> x0, blocking collectives: 9.29 us -> none  [shards(): lax.psum(partial_out, 'rep').astype(jnp.bfloat16)]
    dot_general x22 -> x16, matrix products: 14.7 us -> 6.26 us  [dot(): return lax.dot_general(a, b, (dims, ((), ())), preferred_element_type=F32)]
    pallas_call x0 -> x1, Pallas kernels: none -> 7.34 us  [attend(): pl.pallas_call(attend_kernel, grid=(width // HD,), in_specs=[pl.BlockSpec...]
    sub x2 -> x0, matrix products: 5.74 us -> none  [attend(): weights = jnp.where(allowed[None], jnp.exp(scores - row_max), 0.0)]
  transfers between devices with their start and end apart: 13 -> 25, of which waited for: 8 -> 15; matrix products, arithmetic and copies ran while one was open for 7% -> 18% of each run, Pallas kernels for 0% -> 0%
where the time goes in v1:
time: 86.4 us; the launch traced here: 86 us
  waiting for transfers between devices  28.1 us (33%)
  starting transfers between devices  26.9 us (31%)
  other arithmetic  9.98 us (12%)
  Pallas kernels  7.34 us (8%)
  local copies, waits for them, and re-layouts  6.32 us (7%)
  matrix products  6.26 us (7%)
  between operations  1.14 us (1%)
    ppermute x6, waiting for transfers between devices, sum_over_tm(): total = keep + lax.ppermute(send, AXES, partners(bit0, bit1)).astype(F32)  15 us
    ppermute x6, starting transfers between devices, sum_over_tm(): total = keep + lax.ppermute(send, AXES, partners(bit0, bit1)).astype(F32)  7.65 us
    ppermute x4, starting transfers between devices, shift_blocks(): return lax.ppermute(x, AXES, route)  7.4 us
    pallas_call x1, Pallas kernels, attend(): pl.pallas_call(attend_kernel, grid=(width // HD,), in_specs=[pl.BlockSpec...  7.34 us
    ppermute x6, waiting for transfers between devices, sum_over_tm(): got = lax.ppermute(whole, AXES, partners(bit0, bit1))  7.19 us
    ppermute x6, starting transfers between devices, sum_over_tm(): got = lax.ppermute(whole, AXES, partners(bit0, bit1))  6.29 us
    dot_general x16, matrix products, dot(): return lax.dot_general(a, b, (dims, ((), ())), preferred_element_type=F32)  6.26 us
    ppermute x2, starting transfers between devices, sum_over_tm(): lax.ppermute(own, AXES, partners(bit, bit)).astype(F32)  4.04 us
  transfers between devices with their start and end apart: 25, of which 15 were waited for; matrix products, arithmetic and copies ran while one was open for 18% of the time, Pallas kernels for 0%

profile of v1, /device:TPU:0, one launch (start us, length us, event | category | flops | bytes accessed | tf_op | source)
XLA Modules:
  0.0 86.0 jit_solution(5629597698619065871)
XLA Ops:
  0.7 1.1 %dynamic-slice_bitcast_fusion = bf16[256,512]{1,0:T(8,128)(2,1)S(1)} fusion(bf16[2,256,512]{2,1,0:T(8,128)(2,1)} %param.9, s32[]{:T(128)S(6)} %select_n.103), kind=kLoop, calls=%fused_computation.57 | loop fusion | bytes 524292 | tf_op jit(solution)/shard_map/jit(dynamic_index_in_dim)/squeeze | solution.py:138
  2.5 3.0 %collective-permute-start.3 = (bf16[272,512]{1,0:T(8,128)(2,1)S(1)}, bf16[272,512]{1,0:T(8,128)(2,1)}, u32[]{:S(2)}, u32[]{:S(2)}) collective-permute-start(bf16[272,512]{1,0:T(8,128)(2,1)S(1)} %pad_maximum_fusion.9), channel_id=1, source_target_pairs={{0,2},{2,4},{4,6},{6,8},{8,10},{10,12},{12,14},{14,16},{16,18},{18... | collective-permute-start | bytes 835592 | tf_op jit(solution)/shard_map/ppermute | solution.py:33
  5.5 1.5 %collective-permute-start.2 = (bf16[272,512]{1,0:T(8,128)(2,1)S(1)}, bf16[272,512]{1,0:T(8,128)(2,1)}, u32[]{:S(2)}, u32[]{:S(2)}) collective-permute-start(bf16[272,512]{1,0:T(8,128)(2,1)S(1)} %pad_maximum_fusion.9), channel_id=1, source_target_pairs={{0,4},{2,6},{4,8},{6,10},{8,12},{10,14},{12,16},{14,18},{16,20},{1... | collective-permute-start | bytes 835592 | tf_op jit(solution)/shard_map/ppermute | solution.py:33
  8.9 0.8 copy.15.first_ref
  10.5 1.0 %constant_dynamic-update-slice_fusion = bf16[512,512]{1,0:T(8,128)(2,1)S(1)} fusion(bf16[512,512]{1,0:T(8,128)(2,1)S(1)} %constant_dynamic-update-slice_fusion.1, bf16[256,512]{1,0:T(8,128)(2,1)} %collective-permute-done.4), kind=kLoop, calls=%fused_computation.79 | loop fusion | bytes 524288 | tf_op jit(solution)/shard_map/concatenate | solution.py:159
  11.9 2.9 %collective-permute-done.3 = bf16[272,512]{1,0:T(8,128)(2,1)} collective-permute-done((bf16[272,512]{1,0:T(8,128)(2,1)S(1)}, bf16[272,512]{1,0:T(8,128)(2,1)}, u32[]{:S(2)}, u32[]{:S(2)}) %collective-permute-start.3) | collective-permute-done | bytes 278560 | tf_op jit(solution)/shard_map/ppermute | solution.py:33
  15.4 1.0 %slice.143 = bf16[256,512]{1,0:T(8,128)(2,1)S(1)} slice(bf16[272,512]{1,0:T(8,128)(2,1)} %collective-permute-done.3), slice={[0:256], [0:512]} | slice | bytes 524288 | tf_op jit(solution)/shard_map/slice | solution.py:164
  16.8 1.0 %slice.142 = bf16[256,512]{1,0:T(8,128)(2,1)S(1)} slice(bf16[272,512]{1,0:T(8,128)(2,1)} %collective-permute-done.2), slice={[0:256], [0:512]} | slice | bytes 524288 | tf_op jit(solution)/shard_map/slice | solution.py:164
  21.1 7.3 %attend.1 = (bf16[256,512]{1,0:T(8,128)(2,1)S(1)}, bf16[256,512]{1,0:T(8,128)(2,1)S(1)}, bf16[768,512]{1,0:T(8,128)(2,1)S(1)}, bf16[768,512]{1,0:T(8,128)(2,1)S(1)}) custom-call(f32[4]{0:T(128)S(1)} %pad_maximum_fusion.10.decay_ref, bf16[256,512]{1,0:T(8,128)(2,1)S(1)} %convolution_convert_fusion.4.q_ref, ...), custom_call_target="tpu_custom_call" | custom-call | tf_op jit(solution)/shard_map/attend/pallas_call | solution.py:105
  31.0 2.3 %collective-permute-start.7 = (bf16[256,512]{1,0:T(8,128)(2,1)S(1)}, bf16[256,512]{1,0:T(8,128)(2,1)S(1)}, u32[]{:S(2)}, u32[]{:S(2)}) collective-permute-start(bf16[256,512]{1,0:T(8,128)(2,1)S(1)} %fusion.4), channel_id=1, source_target_pairs={{0,3},{2,1},{4,0},{6,2},{8,4},{10,6},{12,8},{14,10},{16,12},{18,14... | collective-permute-start | bytes 786440 | tf_op jit(solution)/shard_map/ppermute | solution.py:33
  37.2 1.4 %collective-permute-start.18 = (bf16[512,256]{1,0:T(8,128)(2,1)S(1)}, bf16[512,256]{1,0:T(8,128)(2,1)S(1)}, u32[]{:S(2)}, u32[]{:S(2)}) collective-permute-start(bf16[512,256]{1,0:T(8,128)(2,1)S(1)} %dynamic-slice_convert_fusion), channel_id=1, source_target_pairs={{0,2},{1,9},{2,0},{3,11},{4,6},{5,13},{6,4},{7,15},{8,10},{9,1},{1... | collective-permute-start | bytes 786440 | tf_op jit(solution)/shard_map/ppermute | solution.py:63
  38.7 0.8 collective-permute-start.10
  39.5 7.6 %collective-permute-done.18 = bf16[512,256]{1,0:T(8,128)(2,1)S(1)} collective-permute-done((bf16[512,256]{1,0:T(8,128)(2,1)S(1)}, bf16[512,256]{1,0:T(8,128)(2,1)S(1)}, u32[]{:S(2)}, u32[]{:S(2)}) %collective-permute-start.18) | collective-permute-done | bytes 262176 | tf_op jit(solution)/shard_map/ppermute | solution.py:63
  47.2 4.0 %collective-permute-done.10 = bf16[512,256]{1,0:T(8,128)(2,1)S(1)} collective-permute-done((bf16[512,256]{1,0:T(8,128)(2,1)S(1)}, bf16[512,256]{1,0:T(8,128)(2,1)S(1)}, u32[]{:S(2)}, u32[]{:S(2)}) %collective-permute-start.10) | collective-permute-done | bytes 262176 | tf_op jit(solution)/shard_map/ppermute | solution.py:63
  52.2 3.0 %collective-permute-start.20 = (bf16[128,256]{1,0:T(8,128)(2,1)S(1)}, bf16[128,256]{1,0:T(8,128)(2,1)S(1)}, u32[]{:S(2)}, u32[]{:S(2)}) collective-permute-start(bf16[128,256]{1,0:T(8,128)(2,1)S(1)} %dynamic-slice_convert_fusion.4), channel_id=1, source_target_pairs={{0,8},{1,5},{2,10},{3,7},{4,12},{5,1},{6,14},{7,3},{8,0},{9,13},{1... | collective-permute-start | bytes 196616 | tf_op jit(solution)/shard_map/ppermute | solution.py:63
  55.3 1.9 %collective-permute-done.11 = bf16[256,256]{1,0:T(8,128)(2,1)S(1)} collective-permute-done((bf16[256,256]{1,0:T(8,128)(2,1)S(1)}, bf16[256,256]{1,0:T(8,128)(2,1)S(1)}, u32[]{:S(2)}, u32[]{:S(2)}) %collective-permute-start.11) | collective-permute-done | bytes 131104 | tf_op jit(solution)/shard_map/ppermute | solution.py:63
  57.2 2.4 %collective-permute-start.12 = (bf16[128,256]{1,0:T(8,128)(2,1)S(1)}, bf16[128,256]{1,0:T(8,128)(2,1)S(1)}, u32[]{:S(2)}, u32[]{:S(2)}) collective-permute-start(bf16[128,256]{1,0:T(8,128)(2,1)S(1)} %dynamic-slice_convert_fusion.5), channel_id=1, source_target_pairs={{0,8},{1,5},{2,10},{3,7},{4,12},{5,1},{6,14},{7,3},{8,0},{9,13},{1... | collective-permute-start | bytes 196616 | tf_op jit(solution)/shard_map/ppermute | solution.py:63
  59.5 1.9 %collective-permute-start.21 = (bf16[128,256]{1,0:T(8,128)(2,1)S(1)}, bf16[128,256]{1,0:T(8,128)(2,1)S(1)}, u32[]{:S(2)}, u32[]{:S(2)}) collective-permute-start(bf16[128,256]{1,0:T(8,128)(2,1)S(1)} %add_convert_fusion.1), channel_id=1, source_target_pairs={{0,16},{1,17},{2,18},{3,19},{4,20},{5,21},{6,22},{7,23},{8,24},{9,... | collective-permute-start | bytes 196616 | tf_op jit(solution)/shard_map/ppermute | solution.py:66
  61.5 0.8 collective-permute-done.12
  62.3 2.1 %collective-permute-start.13 = (bf16[128,256]{1,0:T(8,128)(2,1)S(1)}, bf16[128,256]{1,0:T(8,128)(2,1)S(1)}, u32[]{:S(2)}, u32[]{:S(2)}) collective-permute-start(bf16[128,256]{1,0:T(8,128)(2,1)S(1)} %add_convert_fusion.3), channel_id=1, source_target_pairs={{0,16},{1,17},{2,18},{3,19},{4,20},{5,21},{6,22},{7,23},{8,24},{9,... | collective-permute-start | bytes 196616 | tf_op jit(solution)/shard_map/ppermute | solution.py:66
  65.8 1.7 %collective-permute-done.13 = bf16[128,256]{1,0:T(8,128)(2,1)S(1)} collective-permute-done((bf16[128,256]{1,0:T(8,128)(2,1)S(1)}, bf16[128,256]{1,0:T(8,128)(2,1)S(1)}, u32[]{:S(2)}, u32[]{:S(2)}) %collective-permute-start.13) | collective-permute-done | bytes 65568 | tf_op jit(solution)/shard_map/ppermute | solution.py:66
  67.5 1.6 %collective-permute-start.14 = (bf16[128,256]{1,0:T(8,128)(2,1)S(1)}, bf16[128,256]{1,0:T(8,128)(2,1)S(1)}, u32[]{:S(2)}, u32[]{:S(2)}) collective-permute-start(bf16[128,256]{1,0:T(8,128)(2,1)S(1)} %add_convert_fusion.2), channel_id=1, source_target_pairs={{0,8},{1,5},{2,10},{3,7},{4,12},{5,1},{6,14},{7,3},{8,0},{9,13},{1... | collective-permute-start | bytes 196616 | tf_op jit(solution)/shard_map/ppermute | solution.py:69
  69.5 1.1 %collective-permute-start.23 = (bf16[256,256]{1,0:T(8,128)(2,1)S(1)}, bf16[256,256]{1,0:T(8,128)(2,1)S(1)}, u32[]{:S(2)}, u32[]{:S(2)}) collective-permute-start(bf16[256,256]{1,0:T(8,128)(2,1)S(1)} %maximum_select_fusion.7), channel_id=1, source_target_pairs={{0,4},{1,3},{2,6},{3,1},{4,0},{5,7},{6,2},{7,5},{8,12},{9,11},{10,... | collective-permute-start | bytes 393224 | tf_op jit(solution)/shard_map/ppermute | solution.py:69
  72.6 1.9 %collective-permute-done.23 = bf16[256,256]{1,0:T(8,128)(2,1)S(1)} collective-permute-done((bf16[256,256]{1,0:T(8,128)(2,1)S(1)}, bf16[256,256]{1,0:T(8,128)(2,1)S(1)}, u32[]{:S(2)}, u32[]{:S(2)}) %collective-permute-start.23) | collective-permute-done | bytes 131104 | tf_op jit(solution)/shard_map/ppermute | solution.py:69
  75.4 0.9 %maximum_select_fusion = bf16[2,256,512]{2,1,0:T(8,128)(2,1)} fusion(bf16[1,256,512]{2,1,0:T(8,128)(2,1)S(1)} %bitcast.26, bf16[1,256,512]{2,1,0:T(8,128)(2,1)S(1)} %bitcast.24, pred[]{:T(512)S(6)} %eq.8), kind=kLoop, calls=%fused_computation.27 | loop fusion | flops 786432 | bytes 1048577 | tf_op jit(solution)/shard_map/jit(_where)/select_n | solution.py:213
  76.3 0.9 %maximum_select_fusion.1 = bf16[2,256,512]{2,1,0:T(8,128)(2,1)} fusion(bf16[1,256,512]{2,1,0:T(8,128)(2,1)S(1)} %bitcast.27, bf16[1,256,512]{2,1,0:T(8,128)(2,1)S(1)} %bitcast.25, pred[]{:T(512)S(6)} %eq.8), kind=kLoop, calls=%fused_computation.28 | loop fusion | flops 786432 | bytes 1048577 | tf_op jit(solution)/shard_map/jit(_where)/select_n | solution.py:213
  77.2 1.4 %collective-permute-start.16 = (bf16[512,256]{1,0:T(8,128)(2,1)S(1)}, bf16[512,256]{1,0:T(8,128)(2,1)S(1)}, u32[]{:S(2)}, u32[]{:S(2)}) collective-permute-start(bf16[512,256]{1,0:T(8,128)(2,1)S(1)} %maximum_select_fusion.4), channel_id=1, source_target_pairs={{0,2},{1,9},{2,0},{3,11},{4,6},{5,13},{6,4},{7,15},{8,10},{9,1},{1... | collective-permute-start | bytes 786440 | tf_op jit(solution)/shard_map/ppermute | solution.py:69
  78.7 2.4 %collective-permute-done.24 = bf16[512,256]{1,0:T(8,128)(2,1)S(1)} collective-permute-done((bf16[512,256]{1,0:T(8,128)(2,1)S(1)}, bf16[512,256]{1,0:T(8,128)(2,1)S(1)}, u32[]{:S(2)}, u32[]{:S(2)}) %collective-permute-start.24) | collective-permute-done | bytes 262176 | tf_op jit(solution)/shard_map/ppermute | solution.py:69
  81.4 0.8 slice_convert_fusion
  82.2 1.7 %collective-permute-done.16 = bf16[512,256]{1,0:T(8,128)(2,1)S(1)} collective-permute-done((bf16[512,256]{1,0:T(8,128)(2,1)S(1)}, bf16[512,256]{1,0:T(8,128)(2,1)S(1)}, u32[]{:S(2)}, u32[]{:S(2)}) %collective-permute-start.16) | collective-permute-done | bytes 262176 | tf_op jit(solution)/shard_map/ppermute | solution.py:69
  84.1 1.0 %slice_convert_fusion.1 = (f32[512,256]{1,0:T(8,128)}, f32[512,256]{1,0:T(8,128)}) fusion(bf16[1024,256]{1,0:T(8,128)(2,1)S(1)} %maximum_select_fusion.2), kind=kLoop, calls=%fused_computation.37 | loop fusion | flops 262144 | bytes 1572864 | tf_op jit(solution)/shard_map/convert_element_type | solution.py:223
  85.2 0.9 maximum_convert_fusion
  (106 shorter events, 20.9 us)
Async XLA Ops:
  0.6 10.9 %copy-start = (bf16[2,256,512]{2,1,0:T(8,128)(2,1)S(1)}, bf16[2,256,512]{2,1,0:T(8,128)(2,1)}, u32[]{:S(2)}) copy-start(bf16[2,256,512]{2,1,0:T(8,128)(2,1)} %param.10) | copy-start | bytes 1572868
  0.6 6.5 %copy-start.4 = (bf16[512,256]{1,0:T(8,128)(2,1)S(1)}, bf16[512,256]{1,0:T(8,128)(2,1)}, u32[]{:S(2)}) copy-start(bf16[512,256]{1,0:T(8,128)(2,1)} %param.15) | copy-start | bytes 786436
  0.7 6.5 %copy-start.1 = (bf16[512,256]{1,0:T(8,128)(2,1)S(1)}, bf16[512,256]{1,0:T(8,128)(2,1)}, u32[]{:S(2)}) copy-start(bf16[512,256]{1,0:T(8,128)(2,1)} %param.14) | copy-start | bytes 786436
  0.7 6.5 %copy-start.2 = (bf16[512,256]{1,0:T(8,128)(2,1)S(1)}, bf16[512,256]{1,0:T(8,128)(2,1)}, u32[]{:S(2)}) copy-start(bf16[512,256]{1,0:T(8,128)(2,1)} %param.13) | copy-start | bytes 786436
  2.5 5.9 %copy-start.6 = (f32[1,256]{1,0:T(1,128)}, f32[1,256]{1,0:T(1,128)S(1)}, u32[]{:S(2)}) copy-start(f32[1,256]{1,0:T(1,128)S(1)} %get-tuple-element.31) | copy-start | bytes 3076
  2.5 5.3 %copy-start.8 = (s32[2,256]{1,0:T(2,128)S(1)}, s32[2,256]{1,0:T(2,128)}, u32[]{:S(2)}) copy-start(s32[2,256]{1,0:T(2,128)} %param.12) | copy-start | bytes 6148
  2.5 12.2 %collective-permute-start.3 = (bf16[272,512]{1,0:T(8,128)(2,1)S(1)}, bf16[272,512]{1,0:T(8,128)(2,1)}, u32[]{:S(2)}, u32[]{:S(2)}) collective-permute-start(bf16[272,512]{1,0:T(8,128)(2,1)S(1)} %pad_maximum_fusion.9), channel_id=1, source_target_pairs={{0,2},{2,4},{4,6},{6,8},{8,10},{10,12},{12,14},{14,16},{16,18},{18... | collective-permute-start | bytes 835592 | tf_op jit(solution)/shard_map/ppermute | solution.py:33
  5.5 11.3 %collective-permute-start.2 = (bf16[272,512]{1,0:T(8,128)(2,1)S(1)}, bf16[272,512]{1,0:T(8,128)(2,1)}, u32[]{:S(2)}, u32[]{:S(2)}) collective-permute-start(bf16[272,512]{1,0:T(8,128)(2,1)S(1)} %pad_maximum_fusion.9), channel_id=1, source_target_pairs={{0,4},{2,6},{4,8},{6,10},{8,12},{10,14},{12,16},{14,18},{16,20},{1... | collective-permute-start | bytes 835592 | tf_op jit(solution)/shard_map/ppermute | solution.py:33
  7.0 2.7 %collective-permute-start = (f32[2]{0:T(128)}, f32[2]{0:T(128)}, u32[]{:S(2)}, u32[]{:S(2)}) collective-permute-start(f32[2]{0:T(128)} %param.17), channel_id=1, source_target_pairs={{0,1},{1,0},{2,3},{3,2},{4,5},{5,4},{6,7},{7,6},{8,9},{9,8},{10,11... | collective-permute-start | bytes 32 | tf_op jit(solution)/shard_map/ppermute | solution.py:23
  7.2 12.0 %collective-permute-start.1 = (bf16[512,768]{1,0:T(8,128)(2,1)S(1)}, bf16[512,768]{1,0:T(8,128)(2,1)S(1)}, u32[]{:S(2)}, u32[]{:S(2)}) collective-permute-start(bf16[512,768]{1,0:T(8,128)(2,1)S(1)} %pad_maximum_fusion.2), channel_id=1, source_target_pairs={{0,1},{1,0},{2,3},{3,2},{4,5},{5,4},{6,7},{7,6},{8,9},{9,8},{10,11... | collective-permute-start | bytes 2359304 | tf_op jit(solution)/shard_map/ppermute | solution.py:23
  7.7 2.8 %collective-permute-start.4 = (bf16[256,512]{1,0:T(8,128)(2,1)S(1)}, bf16[256,512]{1,0:T(8,128)(2,1)}, u32[]{:S(2)}, u32[]{:S(2)}) collective-permute-start(bf16[256,512]{1,0:T(8,128)(2,1)S(1)} %copy-done.3), channel_id=1, source_target_pairs={{0,1},{1,0},{2,3},{3,2},{4,5},{5,4},{6,7},{7,6},{8,9},{9,8},{10,11... | collective-permute-start | bytes 786440 | tf_op jit(solution)/shard_map/ppermute | solution.py:23
  11.5 7.0 %copy-start.7 = (f32[1,256]{1,0:T(1,128)S(1)}, f32[1,256]{1,0:T(1,128)}, u32[]{:S(2)}) copy-start(f32[1,256]{1,0:T(1,128)} %copy-done.6) | copy-start | bytes 3076
  30.0 45.4 %collective-permute-start.5 = (bf16[256,512]{1,0:T(8,128)(2,1)S(1)}, bf16[256,512]{1,0:T(8,128)(2,1)S(1)}, u32[]{:S(2)}, u32[]{:S(2)}) collective-permute-start(bf16[256,512]{1,0:T(8,128)(2,1)S(1)} %convolution_convert_fusion.2), channel_id=1, source_target_pairs={{0,1},{1,0},{2,3},{3,2},{4,5},{5,4},{6,7},{7,6},{8,9},{9,8},{10,11... | collective-permute-start | bytes 786440 | tf_op jit(solution)/shard_map/ppermute | solution.py:23
  31.0 39.6 %collective-permute-start.7 = (bf16[256,512]{1,0:T(8,128)(2,1)S(1)}, bf16[256,512]{1,0:T(8,128)(2,1)S(1)}, u32[]{:S(2)}, u32[]{:S(2)}) collective-permute-start(bf16[256,512]{1,0:T(8,128)(2,1)S(1)} %fusion.4), channel_id=1, source_target_pairs={{0,3},{2,1},{4,0},{6,2},{8,4},{10,6},{12,8},{14,10},{16,12},{18,14... | collective-permute-start | bytes 786440 | tf_op jit(solution)/shard_map/ppermute | solution.py:33
  34.1 2.9 %collective-permute-start.17 = (f32[1024,256]{1,0:T(8,128)S(1)}, f32[1024,256]{1,0:T(8,128)S(1)}, u32[]{:S(2)}, u32[]{:S(2)}) collective-permute-start(f32[1024,256]{1,0:T(8,128)S(1)} %pad_maximum_fusion.1), channel_id=1, source_target_pairs={{0,1},{1,0},{2,3},{3,2},{4,5},{5,4},{6,7},{7,6},{8,9},{9,8},{10,11... | collective-permute-start | bytes 3145736 | tf_op jit(solution)/shard_map/ppermute | solution.py:23
  34.8 3.8 %collective-permute-start.9 = (f32[1024,256]{1,0:T(8,128)S(1)}, f32[1024,256]{1,0:T(8,128)S(1)}, u32[]{:S(2)}, u32[]{:S(2)}) collective-permute-start(f32[1024,256]{1,0:T(8,128)S(1)} %pad_maximum_fusion), channel_id=1, source_target_pairs={{0,1},{1,0},{2,3},{3,2},{4,5},{5,4},{6,7},{7,6},{8,9},{9,8},{10,11... | collective-permute-start | bytes 3145736 | tf_op jit(solution)/shard_map/ppermute | solution.py:23
  35.5 35.1 %collective-permute-start.6 = (bf16[256,512]{1,0:T(8,128)(2,1)S(1)}, bf16[256,512]{1,0:T(8,128)(2,1)S(1)}, u32[]{:S(2)}, u32[]{:S(2)}) collective-permute-start(bf16[256,512]{1,0:T(8,128)(2,1)S(1)} %fusion.3), channel_id=1, source_target_pairs={{0,1},{2,0},{4,2},{6,4},{8,6},{10,8},{12,10},{14,12},{16,14},{18,1... | collective-permute-start | bytes 786440 | tf_op jit(solution)/shard_map/ppermute | solution.py:33
  37.2 9.9 %collective-permute-start.18 = (bf16[512,256]{1,0:T(8,128)(2,1)S(1)}, bf16[512,256]{1,0:T(8,128)(2,1)S(1)}, u32[]{:S(2)}, u32[]{:S(2)}) collective-permute-start(bf16[512,256]{1,0:T(8,128)(2,1)S(1)} %dynamic-slice_convert_fusion), channel_id=1, source_target_pairs={{0,2},{1,9},{2,0},{3,11},{4,6},{5,13},{6,4},{7,15},{8,10},{9,1},{1... | collective-permute-start | bytes 786440 | tf_op jit(solution)/shard_map/ppermute | solution.py:63
  38.7 12.5 %collective-permute-start.10 = (bf16[512,256]{1,0:T(8,128)(2,1)S(1)}, bf16[512,256]{1,0:T(8,128)(2,1)S(1)}, u32[]{:S(2)}, u32[]{:S(2)}) collective-permute-start(bf16[512,256]{1,0:T(8,128)(2,1)S(1)} %dynamic-slice_convert_fusion.1), channel_id=1, source_target_pairs={{0,2},{1,9},{2,0},{3,11},{4,6},{5,13},{6,4},{7,15},{8,10},{9,1},{1... | collective-permute-start | bytes 786440 | tf_op jit(solution)/shard_map/ppermute | solution.py:63
  47.2 5.0 %collective-permute-start.19 = (bf16[256,256]{1,0:T(8,128)(2,1)S(1)}, bf16[256,256]{1,0:T(8,128)(2,1)S(1)}, u32[]{:S(2)}, u32[]{:S(2)}) collective-permute-start(bf16[256,256]{1,0:T(8,128)(2,1)S(1)} %dynamic-slice_convert_fusion.2), channel_id=1, source_target_pairs={{0,4},{1,3},{2,6},{3,1},{4,0},{5,7},{6,2},{7,5},{8,12},{9,11},{10,... | collective-permute-start | bytes 393224 | tf_op jit(solution)/shard_map/ppermute | solution.py:63
  51.4 5.7 %collective-permute-start.11 = (bf16[256,256]{1,0:T(8,128)(2,1)S(1)}, bf16[256,256]{1,0:T(8,128)(2,1)S(1)}, u32[]{:S(2)}, u32[]{:S(2)}) collective-permute-start(bf16[256,256]{1,0:T(8,128)(2,1)S(1)} %dynamic-slice_convert_fusion.3), channel_id=1, source_target_pairs={{0,4},{1,3},{2,6},{3,1},{4,0},{5,7},{6,2},{7,5},{8,12},{9,11},{10,... | collective-permute-start | bytes 393224 | tf_op jit(solution)/shard_map/ppermute | solution.py:63
  52.2 7.3 %collective-permute-start.20 = (bf16[128,256]{1,0:T(8,128)(2,1)S(1)}, bf16[128,256]{1,0:T(8,128)(2,1)S(1)}, u32[]{:S(2)}, u32[]{:S(2)}) collective-permute-start(bf16[128,256]{1,0:T(8,128)(2,1)S(1)} %dynamic-slice_convert_fusion.4), channel_id=1, source_target_pairs={{0,8},{1,5},{2,10},{3,7},{4,12},{5,1},{6,14},{7,3},{8,0},{9,13},{1... | collective-permute-start | bytes 196616 | tf_op jit(solution)/shard_map/ppermute | solution.py:63
  57.2 5.1 %collective-permute-start.12 = (bf16[128,256]{1,0:T(8,128)(2,1)S(1)}, bf16[128,256]{1,0:T(8,128)(2,1)S(1)}, u32[]{:S(2)}, u32[]{:S(2)}) collective-permute-start(bf16[128,256]{1,0:T(8,128)(2,1)S(1)} %dynamic-slice_convert_fusion.5), channel_id=1, source_target_pairs={{0,8},{1,5},{2,10},{3,7},{4,12},{5,1},{6,14},{7,3},{8,0},{9,13},{1... | collective-permute-start | bytes 196616 | tf_op jit(solution)/shard_map/ppermute | solution.py:63
  59.5 5.6 %collective-permute-start.21 = (bf16[128,256]{1,0:T(8,128)(2,1)S(1)}, bf16[128,256]{1,0:T(8,128)(2,1)S(1)}, u32[]{:S(2)}, u32[]{:S(2)}) collective-permute-start(bf16[128,256]{1,0:T(8,128)(2,1)S(1)} %add_convert_fusion.1), channel_id=1, source_target_pairs={{0,16},{1,17},{2,18},{3,19},{4,20},{5,21},{6,22},{7,23},{8,24},{9,... | collective-permute-start | bytes 196616 | tf_op jit(solution)/shard_map/ppermute | solution.py:66
  62.3 5.2 %collective-permute-start.13 = (bf16[128,256]{1,0:T(8,128)(2,1)S(1)}, bf16[128,256]{1,0:T(8,128)(2,1)S(1)}, u32[]{:S(2)}, u32[]{:S(2)}) collective-permute-start(bf16[128,256]{1,0:T(8,128)(2,1)S(1)} %add_convert_fusion.3), channel_id=1, source_target_pairs={{0,16},{1,17},{2,18},{3,19},{4,20},{5,21},{6,22},{7,23},{8,24},{9,... | collective-permute-start | bytes 196616 | tf_op jit(solution)/shard_map/ppermute | solution.py:66
  65.2 4.3 %collective-permute-start.22 = (bf16[128,256]{1,0:T(8,128)(2,1)S(1)}, bf16[128,256]{1,0:T(8,128)(2,1)S(1)}, u32[]{:S(2)}, u32[]{:S(2)}) collective-permute-start(bf16[128,256]{1,0:T(8,128)(2,1)S(1)} %add_convert_fusion), channel_id=1, source_target_pairs={{0,8},{1,5},{2,10},{3,7},{4,12},{5,1},{6,14},{7,3},{8,0},{9,13},{1... | collective-permute-start | bytes 196616 | tf_op jit(solution)/shard_map/ppermute | solution.py:69
  67.5 4.3 %collective-permute-start.14 = (bf16[128,256]{1,0:T(8,128)(2,1)S(1)}, bf16[128,256]{1,0:T(8,128)(2,1)S(1)}, u32[]{:S(2)}, u32[]{:S(2)}) collective-permute-start(bf16[128,256]{1,0:T(8,128)(2,1)S(1)} %add_convert_fusion.2), channel_id=1, source_target_pairs={{0,8},{1,5},{2,10},{3,7},{4,12},{5,1},{6,14},{7,3},{8,0},{9,13},{1... | collective-permute-start | bytes 196616 | tf_op jit(solution)/shard_map/ppermute | solution.py:69
  69.5 5.0 %collective-permute-start.23 = (bf16[256,256]{1,0:T(8,128)(2,1)S(1)}, bf16[256,256]{1,0:T(8,128)(2,1)S(1)}, u32[]{:S(2)}, u32[]{:S(2)}) collective-permute-start(bf16[256,256]{1,0:T(8,128)(2,1)S(1)} %maximum_select_fusion.7), channel_id=1, source_target_pairs={{0,4},{1,3},{2,6},{3,1},{4,0},{5,7},{6,2},{7,5},{8,12},{9,11},{10,... | collective-permute-start | bytes 393224 | tf_op jit(solution)/shard_map/ppermute | solution.py:69
  71.0 5.3 %collective-permute-start.8 = (bf16[256,512]{1,0:T(8,128)(2,1)S(1)}, bf16[256,512]{1,0:T(8,128)(2,1)S(1)}, u32[]{:S(2)}, u32[]{:S(2)}) collective-permute-start(bf16[256,512]{1,0:T(8,128)(2,1)S(1)} %fusion.2), channel_id=1, source_target_pairs={{0,1},{1,0},{2,3},{3,2},{4,5},{5,4},{6,7},{7,6},{8,9},{9,8},{10,11... | collective-permute-start | bytes 786440 | tf_op jit(solution)/shard_map/ppermute | solution.py:23
  71.9 5.3 %collective-permute-start.15 = (bf16[256,256]{1,0:T(8,128)(2,1)S(1)}, bf16[256,256]{1,0:T(8,128)(2,1)S(1)}, u32[]{:S(2)}, u32[]{:S(2)}) collective-permute-start(bf16[256,256]{1,0:T(8,128)(2,1)S(1)} %maximum_select_fusion.6), channel_id=1, source_target_pairs={{0,4},{1,3},{2,6},{3,1},{4,0},{5,7},{6,2},{7,5},{8,12},{9,11},{10,... | collective-permute-start | bytes 393224 | tf_op jit(solution)/shard_map/ppermute | solution.py:69
  74.7 6.4 %collective-permute-start.24 = (bf16[512,256]{1,0:T(8,128)(2,1)S(1)}, bf16[512,256]{1,0:T(8,128)(2,1)S(1)}, u32[]{:S(2)}, u32[]{:S(2)}) collective-permute-start(bf16[512,256]{1,0:T(8,128)(2,1)S(1)} %maximum_select_fusion.5), channel_id=1, source_target_pairs={{0,2},{1,9},{2,0},{3,11},{4,6},{5,13},{6,4},{7,15},{8,10},{9,1},{1... | collective-permute-start | bytes 786440 | tf_op jit(solution)/shard_map/ppermute | solution.py:69
  77.2 6.7 %collective-permute-start.16 = (bf16[512,256]{1,0:T(8,128)(2,1)S(1)}, bf16[512,256]{1,0:T(8,128)(2,1)S(1)}, u32[]{:S(2)}, u32[]{:S(2)}) collective-permute-start(bf16[512,256]{1,0:T(8,128)(2,1)S(1)} %maximum_select_fusion.4), channel_id=1, source_target_pairs={{0,2},{1,9},{2,0},{3,11},{4,6},{5,13},{6,4},{7,15},{8,10},{9,1},{1... | collective-permute-start | bytes 786440 | tf_op jit(solution)/shard_map/ppermute | solution.py:69
  (2 other events, 6.2 us)

commit v2 on v1

v2 whole, which is shorter than its diff:
```python
import functools
import math

import jax
import jax.numpy as jnp
from jax import lax
from jax.experimental import pallas as pl
from jax.experimental.pallas import tpu as pltpu
from jax.sharding import PartitionSpec as P

HD = 128
BF = jnp.bfloat16
F32 = jnp.float32
AXES = ("tm", "rep")
LOG2E = math.log2(math.e)
DOWN = ((0,), (0,))
ACROSS = ((1,), (1,))


def dot(a, b, dims=((1,), (0,))):
    return lax.dot_general(a, b, (dims, ((), ())), preferred_element_type=F32)


def swap_cores(x):
    return lax.ppermute(x, "rep", [(0, 1), (1, 0)])


def shift_blocks(x, distance):
    n = lax.axis_size("tm")

    def worker(b):
        return 2 * b if b < n else 2 * (2 * n - 1 - b) + 1

    route = [(worker(b), worker((b + distance) % (2 * n))) for b in range(2 * n)]
    return lax.ppermute(x, AXES, route)


def bit_orders():
    bits = lax.axis_size("tm").bit_length() - 1
    count = min(3, bits)
    first = list(range(count))
    return first, first[-1:] + first[:-1], list(range(count, bits))


def partners(bit0, bit1):
    n = lax.axis_size("tm")
    pairs = []
    for i in range(n):
        pairs += [(2 * i, 2 * (i ^ (1 << bit0))), (2 * i + 1, 2 * (i ^ (1 << bit1)) + 1)]
    return pairs


def my_bits(orders):
    index = lax.axis_index("tm")
    on_first = lax.axis_index("rep") == 0
    return [jnp.where(on_first, (index >> a) & 1, (index >> b) & 1) for a, b in zip(*orders[:2])]


def tied(x, *others):
    return lax.optimization_barrier((x, *others))[0]


def call(kernel, name, outs, args, smem=1, far_in=0, scratch=(), limit=20, work=1):
    spaces = [pltpu.SMEM] * smem + [pl.ANY] * far_in + [pltpu.VMEM] * (len(args) - smem - far_in)
    return pl.pallas_call(
        kernel,
        in_specs=[pl.BlockSpec(memory_space=space) for space in spaces],
        out_specs=[pl.BlockSpec(memory_space=pltpu.VMEM)] * len(outs),
        out_shape=[jax.ShapeDtypeStruct(shape, dtype) for shape, dtype in outs],
        scratch_shapes=[pltpu.VMEM(shape, dtype) for shape, dtype in scratch]
        + ([pltpu.SemaphoreType.DMA((far_in,))] if far_in else []),
        compiler_params=pltpu.CompilerParams(vmem_limit_bytes=limit << 20),
        cost_estimate=pl.CostEstimate(flops=work << 27, bytes_accessed=work << 17, transcendentals=0),
        name=name,
    )(*args[:smem], *(pltpu.with_memory_space_constraint(x, pltpu.HBM) for x in args[smem : smem + far_in]), *args[smem + far_in :])


CORE, WINDOW, BITS = 0, 1, 2


def places_kernel(info, starts_ref, parcel_ref, first_ref, masks_ref):
    del parcel_ref
    blk = first_ref.shape[0]
    core = info[CORE]
    first = jnp.where(core == 0, starts_ref[0:1], starts_ref[1:2]) - info[WINDOW]
    first_ref[...] = jnp.transpose(jnp.broadcast_to(first, (8, blk)))[:, :1]
    at = lax.broadcasted_iota(jnp.int32, masks_ref.shape, 0)
    masks = jnp.where(at == 0, core, 0)
    for step in range(info.shape[0] - BITS):
        masks = jnp.where(at == step + 1, info[BITS + step], masks)
    masks_ref[...] = masks


def before_kernel(
    info, wq_ref, wk_ref, wv_ref, wo_ref, cotangent_ref, wq_other_ref, wk_other_ref, wv_other_ref, wo_other_ref, x_ref,
    q_ref, k_ref, v_ref, g_attn_ref, g_ref, wq_all_ref, wk_all_ref, wv_all_ref, wo_all_ref, sems,
):
    blk, width = q_ref.shape
    cols = width // 2
    core = info[CORE]
    moves = [
        (wq_ref, wq_all_ref.at[:, :cols]),
        (wk_ref, wk_all_ref.at[:, :cols]),
        (wv_ref, wv_all_ref.at[:, :cols]),
        (wo_ref, wo_all_ref.at[:cols]),
        (cotangent_ref.at[core], g_ref),
    ]
    copies = [pltpu.make_async_copy(a, b, sems.at[i]) for i, (a, b) in enumerate(moves)]
    for copy in copies:
        copy.start()
    wq_all_ref[:, cols:] = wq_other_ref[...]
    wk_all_ref[:, cols:] = wk_other_ref[...]
    wv_all_ref[:, cols:] = wv_other_ref[...]
    wo_all_ref[cols:] = wo_other_ref[...]
    for i, (all_ref, out_ref) in enumerate(((wq_all_ref, q_ref), (wk_all_ref, k_ref), (wv_all_ref, v_ref))):
        copies[i].wait()
        out_ref[...] = dot(x_ref[:blk], all_ref[...]).astype(BF)
    for copy in copies[3:]:
        copy.wait()
    g_attn_ref[...] = dot(g_ref[...], wo_all_ref[...], ACROSS).astype(BF)


def softmax_parts(scores):
    weights = jnp.exp2(scores - jnp.max(scores, -1, keepdims=True))
    return weights * (1.0 / jnp.sum(weights, -1, keepdims=True))


def stamps_of(parcel_ref, blk):
    pieces = parcel_ref[blk:, :blk].astype(F32)
    at = lax.broadcasted_iota(jnp.int32, pieces.shape, 0)
    unit = jnp.where(at == 0, 1.0, jnp.where(at == 1, 256.0, jnp.where(at == 2, 65536.0, 0.0)))
    return jnp.sum(pieces * unit, 0, keepdims=True)


def window_terms(xs, ref, columns, scale):
    blk = ref.shape[0] // len(xs)
    parts = [dot(x[:blk], ref[i * blk : (i + 1) * blk, columns], DOWN) for i, x in enumerate(xs)]
    return functools.reduce(jnp.add, parts) * scale


def forward_kernel(
    scale, decay_ref, decay_other_ref, x_ref, one_ref, two_ref, q_ref, k_ref, v_ref, g_attn_ref, g_ref, wk_ref, wv_ref, first_ref,
    probs_ref, k_win_ref, v_win_ref, away_ref, here_ref, o_ref, dv_ref, shut_ref,
):
    blk, width = q_ref.shape
    cols = width // 2
    k_win_ref[2 * blk :] = k_ref[...]
    v_win_ref[2 * blk :] = v_ref[...]
    at_key = lax.broadcasted_iota(jnp.int32, shut_ref.shape, 1)
    at_row = lax.broadcasted_iota(jnp.int32, shut_ref.shape, 0) + 2 * blk
    allowed = (at_key >= first_ref[...]) & (at_key <= at_row)
    shut_ref[...] = jnp.where(allowed, 0.0, -1e30)
    xs = (two_ref, one_ref, x_ref)
    for i, ref in enumerate(xs[:2]):
        rows = slice(i * blk, (i + 1) * blk)
        k_win_ref[rows] = dot(ref[:blk], wk_ref[...]).astype(BF)
        v_win_ref[rows] = dot(ref[:blk], wv_ref[...]).astype(BF)
    times = [stamps_of(x, blk) for x in xs]
    gap = (times[2][:, blk - 1 :] - jnp.concatenate(times, 1)) * LOG2E
    heads = width // HD
    for head in range(heads):
        c = slice(head * HD, (head + 1) * HD)
        decay = decay_ref[head] if head < heads // 2 else decay_other_ref[head - heads // 2]
        scores = dot(q_ref[:, c], k_win_ref[:, c], ACROSS) * (LOG2E / math.sqrt(HD))
        probs = softmax_parts(scores + (shut_ref[...] - gap * decay))
        probs_ref[head] = probs
        low = probs.astype(BF)
        o_ref[:, c] = dot(low, v_win_ref[:, c]).astype(BF)
        dv_ref[:, c] = dot(low, g_attn_ref[:, c], DOWN).astype(BF)
    for out_ref, lo in ((here_ref, 0), (away_ref, cols)):
        c = slice(lo, lo + cols)
        out_ref[:width] = window_terms(xs, dv_ref, c, scale)
        out_ref[width : width + cols] = dot(o_ref[:, c], g_ref[:, :cols], DOWN) * scale
        out_ref[width + cols :] = dot(o_ref[:, c], g_ref[:, cols:], DOWN) * scale


def backward_kernel(
    scale, x_ref, one_ref, two_ref, q_ref, k_win_ref, v_win_ref, g_attn_ref, probs_ref,
    away_ref, here_ref, dq_ref, dk_ref,
):
    width = q_ref.shape[1]
    cols = width // 2
    inv_scale = 1.0 / math.sqrt(HD)
    for head in range(width // HD):
        c = slice(head * HD, (head + 1) * HD)
        probs = probs_ref[head]
        d_probs = dot(g_attn_ref[:, c], v_win_ref[:, c], ACROSS)
        delta = jnp.sum(probs * d_probs, -1, keepdims=True)
        d_scores = (probs * (d_probs - delta)).astype(BF)
        dq_ref[:, c] = (dot(d_scores, k_win_ref[:, c]) * inv_scale).astype(BF)
        dk_ref[:, c] = (dot(d_scores, q_ref[:, c], DOWN) * inv_scale).astype(BF)
    for out_ref, lo in ((here_ref, 0), (away_ref, cols)):
        c = slice(lo, lo + cols)
        out_ref[:width] = window_terms((x_ref,), dq_ref, c, scale)
        out_ref[width:] = window_terms((two_ref, one_ref, x_ref), dk_ref, c, scale)


def tail_kernel(
    dk_ref, wk_ref, dv_ref, wv_ref, dq_ref, wq_ref, o_ref, wo_ref, two_ref, one_ref, own_ref, mixed_ref
):
    blk = o_ref.shape[0]
    for i, out_ref in enumerate((two_ref, one_ref, own_ref)):
        rows = slice(i * blk, (i + 1) * blk)
        part = dot(dk_ref[rows], wk_ref[...], ACROSS) + dot(dv_ref[rows], wv_ref[...], ACROSS)
        if out_ref is own_ref:
            part += dot(dq_ref[...], wq_ref[...], ACROSS)
        out_ref[...] = part.astype(out_ref.dtype)
    mixed_ref[...] = dot(o_ref[...], wo_ref[...]).astype(BF)


class Summed:
    def __init__(self, masks, orders, here, away):
        self.masks = masks
        self.orders, self.rest = orders[:2], orders[2]
        self.keep, self.got = here, swap_cores(away)

    def passed(self, step, x):
        return lax.ppermute(x, AXES, partners(*(order[step] for order in self.orders)))

    def halve(self, step, *after):
        self.got = tied(self.got, *after)
        half = self.keep.shape[0] // 2
        second = self.masks[step, : self.keep.shape[1]][None] == 1

        def total(rows):
            return self.keep[rows] + self.got[rows].astype(F32)

        lower, upper = total(slice(None, half)), total(slice(half, None))
        self.keep = jnp.where(second, upper, lower)
        self.send = jnp.where(second, lower, upper).astype(BF)
        self.got = self.passed(step, self.send)

    def exchange(self, *after):
        total = self.keep + tied(self.got, *after).astype(F32)
        for bit in self.rest:
            self.send = total.astype(BF)
            got = lax.ppermute(self.send, AXES, partners(bit, bit))
            total = self.send.astype(F32) + got.astype(F32)
        self.whole = total.astype(BF)

    def gather(self, step, *after):
        self.send = self.whole = tied(self.whole, *after)
        self.got = self.passed(step, self.whole)

    def placed(self, step, *after):
        got = tied(self.got, *after)
        second = self.masks[step, : self.keep.shape[1]][None] == 1
        self.parts = jnp.where(second, got, self.whole), jnp.where(second, self.whole, got)
        self.whole = jnp.concatenate(self.parts, 0)


def shards(table, cotangent, stamps, starts, w_query, w_key, w_value, w_out, decay):
    n = lax.axis_size("tm")
    index = lax.axis_index("tm")
    core = lax.axis_index("rep")
    blk = table.shape[1]
    width = table.shape[2]
    cols = w_query.shape[1]
    block = jnp.where(core == 0, index, 2 * n - 1 - index)
    orders = bit_orders()
    info = jnp.stack([core, (block - 2) * blk, *my_bits(orders)]).astype(jnp.int32)

    x_own = lax.dynamic_index_in_dim(table, core, 0, False)
    t_own = lax.dynamic_index_in_dim(stamps, core, 0, False)
    pieces = jnp.stack([t_own & 255, (t_own >> 8) & 255, t_own >> 16]).astype(BF)
    pieces = jnp.pad(pieces, ((0, 13), (0, width - blk)))
    parcel = jnp.concatenate([x_own, pieces], 0)
    back_one = shift_blocks(parcel, 1)
    back_two = shift_blocks(parcel, 2)


    rows = ((blk, width), BF)
    window = ((3 * blk, width), BF)
    square = ((width, width), BF)
    pair = ((2 * width, cols), F32)
    heads = ((width // HD, blk, 3 * blk), F32)
    scale = 1.0 / math.sqrt(2 * blk * n)

    first, masks = call(
        places_kernel, "places", [((blk, 1), jnp.int32), ((8, width), jnp.int32)], (info, starts, parcel), work=0
    )
    others = [swap_cores(tied(x, parcel)) for x in (w_query, w_key, w_value, w_out, decay)]
    decay_other = others.pop()
    q, k_own, v_own, g_attn, g_own, wq, wk, wv, wo = call(
        before_kernel,
        "before",
        [rows, rows, rows, rows, rows, square, square, square, square],
        (info, w_query, w_key, w_value, w_out, cotangent, *others, parcel),
        far_in=5,
        work=0,
    )
    probs, k_win, v_win, away_a, here_a, attn, dv = call(
        functools.partial(forward_kernel, scale),
        "forward",
        [heads, window, window, pair, pair, rows, window],
        (decay, decay_other, parcel, back_one, back_two, q, k_own, v_own, g_attn, g_own, wk, wv, first),
        smem=2,
        scratch=[((blk, 3 * blk), F32)],
        work=32,
    )
    sum_a = Summed(masks[1:], orders, here_a, away_a)
    away_b, here_b, dq, dk = call(
        functools.partial(backward_kernel, scale),
        "backward",
        [pair, pair, rows, window],
        (parcel, back_one, back_two, q, k_win, v_win, g_attn, probs),
        smem=0,
        work=24,
    )
    sum_b = Summed(masks[1:], orders, here_b, away_b)
    to_two, to_one, to_self, mixed_own = call(
        tail_kernel, "tail", [rows, rows, ((blk, width), F32), rows], (dk, wk, dv, wv, dq, wq, attn, wo), smem=0, work=8
    )
    steps = len(orders[0])
    halos = []

    def start_halos(*after):
        halos.append(shift_blocks(tied(to_one, *after), -1))
        halos.append(shift_blocks(tied(to_two, *after), -2))

    def end_halos():
        return (to_self + halos[0].astype(F32) + halos[1].astype(F32)).astype(BF)

    sum_a.halve(0)
    sum_b.halve(0, sum_a.send)
    sum_a.halve(1, sum_b.send)
    sum_b.halve(1, sum_a.send)
    sum_a.halve(2, sum_b.send)
    sum_b.halve(2, sum_a.send)
    start_halos(sum_b.send)
    sum_a.exchange(sum_b.send)
    sum_b.exchange(sum_a.send)
    sum_a.gather(2, sum_b.send)
    sum_b.gather(2, sum_a.send)
    sum_a.placed(2)
    sum_b.placed(2, sum_a.whole)
    sum_a.gather(1, sum_b.send)
    sum_b.gather(1, sum_a.send)
    sum_a.placed(1)
    sum_b.placed(1, sum_a.whole)
    sum_a.gather(0, sum_b.send)
    sum_b.gather(0, sum_a.send)
    sum_a.placed(0)
    grad_own = end_halos()
    on_second = masks[0][None, None] == 1

    def both_blocks(own):
        other = swap_cores(own)
        return jnp.where(on_second, jnp.stack([other, own]), jnp.stack([own, other]))

    mixed = both_blocks(mixed_own)
    grad_table = both_blocks(grad_own)
    grad_value, lines = (part.astype(F32) for part in sum_a.parts)
    grad_out = jnp.concatenate([lines[:cols], lines[cols:]], 1)
    sum_b.placed(0, grad_value, grad_out)
    grad_query, grad_key = (part.astype(F32) for part in sum_b.parts)
    return (mixed, grad_table, grad_query, grad_key, grad_value, grad_out)


def solution(mesh):
    return jax.shard_map(
        shards,
        mesh=mesh,
        in_specs=(
            P(None, "tm", None),
            P(None, "tm", None),
            P(None, "tm"),
            P(None, "tm"),
            P(None, "rep"),
            P(None, "rep"),
            P(None, "rep"),
            P("rep", None),
            P("rep"),
        ),
        out_specs=(
            P(None, "tm", None),
            P(None, "tm", None),
            P(None, "rep"),
            P(None, "rep"),
            P(None, "rep"),
            P("rep", None),
        ),
        check_vma=False,
    )
```

time: 86.4 us -> 75.2 us (0.87)
  matrix products: 6.26 us -> 0 us
  local copies, waits for them, and re-layouts: 6.32 us -> 1.11 us
  Pallas kernels: 7.34 us -> 12.5 us
  other arithmetic: 9.98 us -> 5.65 us
  waiting for transfers between devices: 28.1 us -> 24.7 us
  starting transfers between devices: 26.9 us -> 30.1 us
    dot_general x16 -> x0, matrix products: 6.26 us -> none  [dot(): return lax.dot_general(a, b, (dims, ((), ())), preferred_element_type=F32)]
    pallas_call x1 -> x5, Pallas kernels: 7.34 us -> 12.5 us  [call(): pl.pallas_call(kernel, in_specs=[pl.BlockSpec(memory_space=space) for spa...]
    ppermute x14, waiting for transfers between devices: 24.6 us -> 19.6 us  [the longest x12 12.4 us: passed(): lax.ppermute(x, AXES, partners(*(order[step] for order in self.orders)))]
    ppermute x14, starting transfers between devices: 18 us -> 22.5 us  [the longest x12 16.9 us: passed(): lax.ppermute(x, AXES, partners(*(order[step] for order in self.orders)))]
    ppermute x4, starting transfers between devices: 7.4 us -> 4.08 us  [shift_blocks(): return lax.ppermute(x, AXES, route)]
    slice x9 -> x1, local copies, waits for them, and re-layouts: 2.89 us -> 0.03 us  [shards(): grad_out = jnp.concatenate([lines[:cols], lines[cols:]], 1)]
    convert_element_type x10 -> x11, other arithmetic: 4.85 us -> 2.42 us  [the longest x1 1.04 us: shards(): grad_query, grad_key = (part.astype(F32) for part in sum_b.parts)]
    ppermute x7 -> x9, starting transfers between devices: 1.48 us -> 3.53 us  [swap_cores(): return lax.ppermute(x, 'rep', [(0, 1), (1, 0)])]
  transfers between devices with their start and end apart: 25 -> 27, of which waited for: 15 -> 13; matrix products, arithmetic and copies ran while one was open for 18% -> 5% of each run, Pallas kernels for 0% -> 10%
where the time goes in v2:
time: 75.2 us; the launch traced here: 75 us
  starting transfers between devices  30.1 us (40%)
  waiting for transfers between devices  24.7 us (33%)
  Pallas kernels  12.5 us (17%)
  other arithmetic  5.65 us (8%)
  local copies, waits for them, and re-layouts  1.11 us (1%)
  between operations  0.88 us (1%)
    ppermute x12, starting transfers between devices, passed(): lax.ppermute(x, AXES, partners(*(order[step] for order in self.orders)))  16.9 us
    pallas_call x5, Pallas kernels, call(): pl.pallas_call(kernel, in_specs=[pl.BlockSpec(memory_space=space) for spa...  12.5 us
    ppermute x12, waiting for transfers between devices, passed(): lax.ppermute(x, AXES, partners(*(order[step] for order in self.orders)))  12.4 us
    ppermute x2, waiting for transfers between devices, exchange(): got = lax.ppermute(self.send, AXES, partners(bit, bit))  7.19 us
    ppermute x2, starting transfers between devices, exchange(): got = lax.ppermute(self.send, AXES, partners(bit, bit))  5.57 us
    ppermute x4, waiting for transfers between devices, shift_blocks(): return lax.ppermute(x, AXES, route)  4.42 us
    ppermute x4, starting transfers between devices, shift_blocks(): return lax.ppermute(x, AXES, route)  4.08 us
    ppermute x9, starting transfers between devices, swap_cores(): return lax.ppermute(x, 'rep', [(0, 1), (1, 0)])  3.53 us
  transfers between devices with their start and end apart: 27, of which 13 were waited for; matrix products, arithmetic and copies ran while one was open for 5% of the time, Pallas kernels for 10%

profile of v2, /device:TPU:0, one launch (start us, length us, event | category | flops | bytes accessed | tf_op | source)
XLA Modules:
  0.0 75.0 jit_solution(4404734589313371621)
XLA Ops:
  0.7 0.7 and_convert_fusion.1
  2.3 2.6 %collective-permute-start = (bf16[272,512]{1,0:T(8,128)(2,1)S(1)}, bf16[272,512]{1,0:T(8,128)(2,1)S(1)}, u32[]{:S(2)}, u32[]{:S(2)}) collective-permute-start(bf16[272,512]{1,0:T(8,128)(2,1)S(1)} %pad_maximum_fusion.1.parcel_ref.x_ref), channel_id=1, source_target_pairs={{0,2},{2,4},{4,6},{6,8},{8,10},{10,12},{12,14},{14,16},{16,18},{18... | collective-permute-start | bytes 835592 | tf_op jit(solution)/shard_map/ppermute | solution.py:35
  4.8 1.5 %collective-permute-start.1 = (bf16[272,512]{1,0:T(8,128)(2,1)S(1)}, bf16[272,512]{1,0:T(8,128)(2,1)S(1)}, u32[]{:S(2)}, u32[]{:S(2)}) collective-permute-start(bf16[272,512]{1,0:T(8,128)(2,1)S(1)} %pad_maximum_fusion.1.parcel_ref.x_ref), channel_id=1, source_target_pairs={{0,4},{2,6},{4,8},{6,10},{8,12},{10,14},{12,16},{14,18},{16,20},{1... | collective-permute-start | bytes 835592 | tf_op jit(solution)/shard_map/ppermute | solution.py:35
  8.9 2.8 %before.1 = (bf16[256,512]{1,0:T(8,128)(2,1)S(1)}, bf16[256,512]{1,0:T(8,128)(2,1)S(1)}, bf16[256,512]{1,0:T(8,128)(2,1)S(1)}, bf16[256,512]{1,0:T(8,128)(2,1)S(...) custom-call(s32[5]{0:T(128)S(1)} %stack.58.info, ...), custom_call_target="tpu_custom_call" | custom-call | tf_op jit(solution)/shard_map/before/pallas_call | solution.py:65
  11.7 2.3 %collective-permute-done.one_ref = bf16[272,512]{1,0:T(8,128)(2,1)S(1)} collective-permute-done((bf16[272,512]{1,0:T(8,128)(2,1)S(1)}, bf16[272,512]{1,0:T(8,128)(2,1)S(1)}, u32[]{:S(2)}, u32[]{:S(2)}) %collective-permute-start) | collective-permute-done | bytes 278560 | tf_op jit(solution)/shard_map/ppermute | solution.py:35
  14.0 2.2 %collective-permute-done.1.two_ref = bf16[272,512]{1,0:T(8,128)(2,1)S(1)} collective-permute-done((bf16[272,512]{1,0:T(8,128)(2,1)S(1)}, bf16[272,512]{1,0:T(8,128)(2,1)S(1)}, u32[]{:S(2)}, u32[]{:S(2)}) %collective-permute-start.1) | collective-permute-done | bytes 278560 | tf_op jit(solution)/shard_map/ppermute | solution.py:35
  16.1 4.8 %forward.1 = (f32[4,256,768]{2,1,0:T(8,128)S(1)}, bf16[768,512]{1,0:T(8,128)(2,1)S(1)}, bf16[768,512]{1,0:T(8,128)(2,1)S(1)}, f32[1024,256]{1,0:T(8,128)S(1)}, f...) custom-call(f32[2]{0:T(128)S(1)} %copy-done.2, ...), custom_call_target="tpu_custom_call" | custom-call | flops 4294967296 | bytes 4194304 | tf_op jit(solution)/shard_map/forward/pallas_call | solution.py:65
  21.0 3.0 %backward.1 = (f32[1024,256]{1,0:T(8,128)S(1)}, f32[1024,256]{1,0:T(8,128)S(1)}, bf16[256,512]{1,0:T(8,128)(2,1)S(1)}, bf16[768,512]{1,0:T(8,128)(2,1)S(1)}) custom-call(bf16[272,512]{1,0:T(8,128)(2,1)S(1)} %pad_maximum_fusion.1.parcel_ref.x_ref, bf16[272,512]{1,0:T(8,128)(2,1)S(1)} %collective-permute-done.one_ref, ...), custom_call_target="tpu_custom_call" | custom-call | flops 3221225472 | bytes 3145728 | tf_op jit(solution)/shard_map/backward/pallas_call | solution.py:65
  24.8 1.3 %collective-permute-start.11 = (bf16[512,256]{1,0:T(8,128)(2,1)S(1)}, bf16[512,256]{1,0:T(8,128)(2,1)S(1)}, u32[]{:S(2)}, u32[]{:S(2)}) collective-permute-start(bf16[512,256]{1,0:T(8,128)(2,1)S(1)} %get-tuple-element.108), channel_id=1, source_target_pairs={{0,2},{1,9},{2,0},{3,11},{4,6},{5,13},{6,4},{7,15},{8,10},{9,1},{1... | collective-permute-start | bytes 786440 | tf_op jit(solution)/shard_map/ppermute | solution.py:218
  27.0 1.3 %collective-permute-start.10 = (bf16[512,256]{1,0:T(8,128)(2,1)S(1)}, bf16[512,256]{1,0:T(8,128)(2,1)S(1)}, u32[]{:S(2)}, u32[]{:S(2)}) collective-permute-start(bf16[512,256]{1,0:T(8,128)(2,1)S(1)} %get-tuple-element.109), channel_id=1, source_target_pairs={{0,2},{1,9},{2,0},{3,11},{4,6},{5,13},{6,4},{7,15},{8,10},{9,1},{1... | collective-permute-start | bytes 786440 | tf_op jit(solution)/shard_map/ppermute | solution.py:218
  28.3 1.3 %tail.1 = (bf16[256,512]{1,0:T(8,128)(2,1)S(1)}, bf16[256,512]{1,0:T(8,128)(2,1)S(1)}, f32[256,512]{1,0:T(8,128)S(1)}, bf16[256,512]{1,0:T(8,128)(2,1)S(1)}) custom-call(bf16[768,512]{1,0:T(8,128)(2,1)S(1)} %get-tuple-element.72.dk_ref, bf16[512,512]{1,0:T(8,128)(2,1)S(1)} %get-tuple-element.66.wk_ref, bf16[768,512]{1,0:T(8,128)(2,1)S(1)} %get-tuple-element.73.dv_ref, ...), custom_call_target="tpu_custom_call" | custom-call | flops 1073741824 | bytes 1048576 | tf_op jit(solution)/shard_map/tail/pallas_call | solution.py:65
  29.6 1.2 %collective-permute-start.7 = (bf16[256,512]{1,0:T(8,128)(2,1)S(1)}, bf16[256,512]{1,0:T(8,128)(2,1)S(1)}, u32[]{:S(2)}, u32[]{:S(2)}) collective-permute-start(bf16[256,512]{1,0:T(8,128)(2,1)S(1)} %get-tuple-element.78), channel_id=1, source_target_pairs={{0,1},{1,0},{2,3},{3,2},{4,5},{5,4},{6,7},{7,6},{8,9},{9,8},{10,11... | collective-permute-start | bytes 786440 | tf_op jit(solution)/shard_map/ppermute | solution.py:25
  31.3 2.5 %collective-permute-start.13 = (bf16[256,256]{1,0:T(8,128)(2,1)S(1)}, bf16[256,256]{1,0:T(8,128)(2,1)S(1)}, u32[]{:S(2)}, u32[]{:S(2)}) collective-permute-start(bf16[256,256]{1,0:T(8,128)(2,1)S(1)} %get-tuple-element.112), channel_id=1, source_target_pairs={{0,4},{1,3},{2,6},{3,1},{4,0},{5,7},{6,2},{7,5},{8,12},{9,11},{10,... | collective-permute-start | bytes 393224 | tf_op jit(solution)/shard_map/ppermute | solution.py:218
  34.2 3.4 %collective-permute-start.12 = (bf16[256,256]{1,0:T(8,128)(2,1)S(1)}, bf16[256,256]{1,0:T(8,128)(2,1)S(1)}, u32[]{:S(2)}, u32[]{:S(2)}) collective-permute-start(bf16[256,256]{1,0:T(8,128)(2,1)S(1)} %get-tuple-element.113), channel_id=1, source_target_pairs={{0,4},{1,3},{2,6},{3,1},{4,0},{5,7},{6,2},{7,5},{8,12},{9,11},{10,... | collective-permute-start | bytes 393224 | tf_op jit(solution)/shard_map/ppermute | solution.py:218
  37.6 1.6 %collective-permute-start.18 = (bf16[128,256]{1,0:T(8,128)(2,1)S(1)}, bf16[128,256]{1,0:T(8,128)(2,1)S(1)}, u32[]{:S(2)}, u32[]{:S(2)}) collective-permute-start(bf16[128,256]{1,0:T(8,128)(2,1)S(1)} %select_convert_fusion.9), channel_id=1, source_target_pairs={{0,8},{1,5},{2,10},{3,7},{4,12},{5,1},{6,14},{7,3},{8,0},{9,13},{1... | collective-permute-start | bytes 196616 | tf_op jit(solution)/shard_map/ppermute | solution.py:218
  39.2 2.2 %collective-permute-done.12 = bf16[256,256]{1,0:T(8,128)(2,1)S(1)} collective-permute-done((bf16[256,256]{1,0:T(8,128)(2,1)S(1)}, bf16[256,256]{1,0:T(8,128)(2,1)S(1)}, u32[]{:S(2)}, u32[]{:S(2)}) %collective-permute-start.12) | collective-permute-done | bytes 131104 | tf_op jit(solution)/shard_map/ppermute | solution.py:218
  41.4 1.5 %collective-permute-start.17 = (bf16[128,256]{1,0:T(8,128)(2,1)S(1)}, bf16[128,256]{1,0:T(8,128)(2,1)S(1)}, u32[]{:S(2)}, u32[]{:S(2)}) collective-permute-start(bf16[128,256]{1,0:T(8,128)(2,1)S(1)} %select_convert_fusion.8), channel_id=1, source_target_pairs={{0,8},{1,5},{2,10},{3,7},{4,12},{5,1},{6,14},{7,3},{8,0},{9,13},{1... | collective-permute-start | bytes 196616 | tf_op jit(solution)/shard_map/ppermute | solution.py:218
  43.0 4.1 %collective-permute-start.20 = (bf16[128,256]{1,0:T(8,128)(2,1)S(1)}, bf16[128,256]{1,0:T(8,128)(2,1)S(1)}, u32[]{:S(2)}, u32[]{:S(2)}) collective-permute-start(bf16[128,256]{1,0:T(8,128)(2,1)S(1)} %add_convert_fusion.4), channel_id=1, source_target_pairs={{0,16},{1,17},{2,18},{3,19},{4,20},{5,21},{6,22},{7,23},{8,24},{9,... | collective-permute-start | bytes 196616 | tf_op jit(solution)/shard_map/ppermute | solution.py:237
  47.1 1.5 %collective-permute-start.19 = (bf16[128,256]{1,0:T(8,128)(2,1)S(1)}, bf16[128,256]{1,0:T(8,128)(2,1)S(1)}, u32[]{:S(2)}, u32[]{:S(2)}) collective-permute-start(bf16[128,256]{1,0:T(8,128)(2,1)S(1)} %add_convert_fusion.3), channel_id=1, source_target_pairs={{0,16},{1,17},{2,18},{3,19},{4,20},{5,21},{6,22},{7,23},{8,24},{9,... | collective-permute-start | bytes 196616 | tf_op jit(solution)/shard_map/ppermute | solution.py:237
  48.6 6.5 %collective-permute-done.20 = bf16[128,256]{1,0:T(8,128)(2,1)S(1)} collective-permute-done((bf16[128,256]{1,0:T(8,128)(2,1)S(1)}, bf16[128,256]{1,0:T(8,128)(2,1)S(1)}, u32[]{:S(2)}, u32[]{:S(2)}) %collective-permute-start.20) | collective-permute-done | bytes 65568 | tf_op jit(solution)/shard_map/ppermute | solution.py:237
  55.1 1.3 %collective-permute-start.22 = (bf16[128,256]{1,0:T(8,128)(2,1)S(1)}, bf16[128,256]{1,0:T(8,128)(2,1)S(1)}, u32[]{:S(2)}, u32[]{:S(2)}) collective-permute-start(bf16[128,256]{1,0:T(8,128)(2,1)S(1)} %add_convert_fusion.1), channel_id=1, source_target_pairs={{0,8},{1,5},{2,10},{3,7},{4,12},{5,1},{6,14},{7,3},{8,0},{9,13},{1... | collective-permute-start | bytes 196616 | tf_op jit(solution)/shard_map/ppermute | solution.py:218
  57.3 2.1 %collective-permute-done.22 = bf16[128,256]{1,0:T(8,128)(2,1)S(1)} collective-permute-done((bf16[128,256]{1,0:T(8,128)(2,1)S(1)}, bf16[128,256]{1,0:T(8,128)(2,1)S(1)}, u32[]{:S(2)}, u32[]{:S(2)}) %collective-permute-start.22) | collective-permute-done | bytes 65568 | tf_op jit(solution)/shard_map/ppermute | solution.py:218
  59.6 1.9 %collective-permute-done.21 = bf16[128,256]{1,0:T(8,128)(2,1)S(1)} collective-permute-done((bf16[128,256]{1,0:T(8,128)(2,1)S(1)}, bf16[128,256]{1,0:T(8,128)(2,1)S(1)}, u32[]{:S(2)}, u32[]{:S(2)}) %collective-permute-start.21) | collective-permute-done | bytes 65568 | tf_op jit(solution)/shard_map/ppermute | solution.py:218
  61.9 2.6 %collective-permute-done.24 = bf16[256,256]{1,0:T(8,128)(2,1)S(1)} collective-permute-done((bf16[256,256]{1,0:T(8,128)(2,1)S(1)}, bf16[256,256]{1,0:T(8,128)(2,1)S(1)}, u32[]{:S(2)}, u32[]{:S(2)}) %collective-permute-start.24) | collective-permute-done | bytes 131104 | tf_op jit(solution)/shard_map/ppermute | solution.py:218
  64.6 2.2 %collective-permute-start.26 = (bf16[512,256]{1,0:T(8,128)(2,1)S(1)}, bf16[512,256]{1,0:T(8,128)(2,1)S(1)}, u32[]{:S(2)}, u32[]{:S(2)}) collective-permute-start(bf16[512,256]{1,0:T(8,128)(2,1)S(1)} %pad_maximum_fusion.2), channel_id=1, source_target_pairs={{0,2},{1,9},{2,0},{3,11},{4,6},{5,13},{6,4},{7,15},{8,10},{9,1},{1... | collective-permute-start | bytes 786440 | tf_op jit(solution)/shard_map/ppermute | solution.py:218
  66.8 1.3 %collective-permute-start.25 = (bf16[512,256]{1,0:T(8,128)(2,1)S(1)}, bf16[512,256]{1,0:T(8,128)(2,1)S(1)}, u32[]{:S(2)}, u32[]{:S(2)}) collective-permute-start(bf16[512,256]{1,0:T(8,128)(2,1)S(1)} %pad_maximum_fusion.3), channel_id=1, source_target_pairs={{0,2},{1,9},{2,0},{3,11},{4,6},{5,13},{6,4},{7,15},{8,10},{9,1},{1... | collective-permute-start | bytes 786440 | tf_op jit(solution)/shard_map/ppermute | solution.py:218
  68.2 1.1 %maximum_select_fusion.1 = (bf16[2,256,512]{2,1,0:T(8,128)(2,1)}, bf16[2,256,512]{2,1,0:T(8,128)(2,1)}) fusion(bf16[1,256,512]{2,1,0:T(8,128)(2,1)S(1)} %bitcast.12, bf16[1,256,512]{2,1,0:T(8,128)(2,1)S(1)} %bitcast.14, pred[512]{0:T(512)(128)(4,1)S(1)} %compare_reduce_fusion, bf16[1,256,512]{2,1,0:T(8,128)(2,1)S(1)} %bitcast.13, ...), kind=kLoop, calls=%fused_computation.3 | loop fusion | flops 1572864 | bytes 2097664 | tf_op jit(solution)/shard_map/jit(_where)/select_n | solution.py:349
  69.3 1.8 %collective-permute-done.26 = bf16[512,256]{1,0:T(8,128)(2,1)S(1)} collective-permute-done((bf16[512,256]{1,0:T(8,128)(2,1)S(1)}, bf16[512,256]{1,0:T(8,128)(2,1)S(1)}, u32[]{:S(2)}, u32[]{:S(2)}) %collective-permute-start.26) | collective-permute-done | bytes 262176 | tf_op jit(solution)/shard_map/ppermute | solution.py:218
  71.1 0.9 %select_convert_fusion.4 = (f32[512,256]{1,0:T(8,128)S(1)}, f32[512,256]{1,0:T(8,128)}) fusion(bf16[512,256]{1,0:T(8,128)(2,1)S(1)} %pad_maximum_fusion.2, bf16[512,256]{1,0:T(8,128)(2,1)S(1)} %collective-permute-done.26, pred[256]{0:T(512)(128)(4,1)S(1)} %get-tuple-element.105), kind=kLoop, calls=%fused_computation.19 | loop fusion | flops 524288 | bytes 1573120 | tf_op jit(solution)/shard_map/convert_element_type | solution.py:353
  72.0 0.9 %pad_maximum_fusion = f32[256,512]{1,0:T(8,128)} fusion(f32[256,256]{1,0:T(8,128)S(1)} %get-tuple-element.120, f32[256,256]{1,0:T(8,128)S(1)} %get-tuple-element.119), kind=kLoop, calls=%fused_computation.4 | loop fusion | flops 131072 | bytes 1048576 | tf_op jit(solution)/shard_map/concatenate | solution.py:354
  72.9 1.0 %collective-permute-done.25 = bf16[512,256]{1,0:T(8,128)(2,1)S(1)} collective-permute-done((bf16[512,256]{1,0:T(8,128)(2,1)S(1)}, bf16[512,256]{1,0:T(8,128)(2,1)S(1)}, u32[]{:S(2)}, u32[]{:S(2)}) %collective-permute-start.25) | collective-permute-done | bytes 262176 | tf_op jit(solution)/shard_map/ppermute | solution.py:218
  73.9 1.0 %select_convert_fusion.2 = (f32[512,256]{1,0:T(8,128)}, f32[512,256]{1,0:T(8,128)}) fusion(bf16[512,256]{1,0:T(8,128)(2,1)S(1)} %pad_maximum_fusion.3, bf16[512,256]{1,0:T(8,128)(2,1)S(1)} %collective-permute-done.25, pred[256]{0:T(512)(128)(4,1)S(1)} %get-tuple-element.105), kind=kLoop, calls=%fused_computation.17 | loop fusion | flops 524288 | bytes 1573120 | tf_op jit(solution)/shard_map/convert_element_type | solution.py:356
  (64 shorter events, 7.6 us)
Async XLA Ops:
  0.6 1.1 %copy-start = (bf16[2,256,512]{2,1,0:T(8,128)(2,1)S(1)}, bf16[2,256,512]{2,1,0:T(8,128)(2,1)}, u32[]{:S(2)}) copy-start(bf16[2,256,512]{2,1,0:T(8,128)(2,1)} %param.9) | copy-start | bytes 1572868
  0.6 15.5 %copy-start.2 = (f32[2]{0:T(128)S(1)}, f32[2]{0:T(128)}, u32[]{:S(2)}) copy-start(f32[2]{0:T(128)} %decay_ref.1) | copy-start | bytes 28
  1.8 5.1 %collective-permute-start.2 = (bf16[512,256]{1,0:T(8,128)(2,1)}, bf16[512,256]{1,0:T(8,128)(2,1)S(1)}, u32[]{:S(2)}, u32[]{:S(2)}) collective-permute-start(bf16[512,256]{1,0:T(8,128)(2,1)} %wq_ref.1), channel_id=1, source_target_pairs={{0,1},{1,0},{2,3},{3,2},{4,5},{5,4},{6,7},{7,6},{8,9},{9,8},{10,11... | collective-permute-start | bytes 786440 | tf_op jit(solution)/shard_map/ppermute | solution.py:25
  2.3 11.7 %collective-permute-start = (bf16[272,512]{1,0:T(8,128)(2,1)S(1)}, bf16[272,512]{1,0:T(8,128)(2,1)S(1)}, u32[]{:S(2)}, u32[]{:S(2)}) collective-permute-start(bf16[272,512]{1,0:T(8,128)(2,1)S(1)} %pad_maximum_fusion.1.parcel_ref.x_ref), channel_id=1, source_target_pairs={{0,2},{2,4},{4,6},{6,8},{8,10},{10,12},{12,14},{14,16},{16,18},{18... | collective-permute-start | bytes 835592 | tf_op jit(solution)/shard_map/ppermute | solution.py:35
  4.8 11.3 %collective-permute-start.1 = (bf16[272,512]{1,0:T(8,128)(2,1)S(1)}, bf16[272,512]{1,0:T(8,128)(2,1)S(1)}, u32[]{:S(2)}, u32[]{:S(2)}) collective-permute-start(bf16[272,512]{1,0:T(8,128)(2,1)S(1)} %pad_maximum_fusion.1.parcel_ref.x_ref), channel_id=1, source_target_pairs={{0,4},{2,6},{4,8},{6,10},{8,12},{10,14},{12,16},{14,18},{16,20},{1... | collective-permute-start | bytes 835592 | tf_op jit(solution)/shard_map/ppermute | solution.py:35
  6.4 2.0 %collective-permute-start.3 = (bf16[512,256]{1,0:T(8,128)(2,1)}, bf16[512,256]{1,0:T(8,128)(2,1)S(1)}, u32[]{:S(2)}, u32[]{:S(2)}) collective-permute-start(bf16[512,256]{1,0:T(8,128)(2,1)} %wk_ref.1), channel_id=1, source_target_pairs={{0,1},{1,0},{2,3},{3,2},{4,5},{5,4},{6,7},{7,6},{8,9},{9,8},{10,11... | collective-permute-start | bytes 786440 | tf_op jit(solution)/shard_map/ppermute | solution.py:25
  6.4 2.5 %collective-permute-start.4 = (bf16[512,256]{1,0:T(8,128)(2,1)}, bf16[512,256]{1,0:T(8,128)(2,1)S(1)}, u32[]{:S(2)}, u32[]{:S(2)}) collective-permute-start(bf16[512,256]{1,0:T(8,128)(2,1)} %wv_ref.1), channel_id=1, source_target_pairs={{0,1},{1,0},{2,3},{3,2},{4,5},{5,4},{6,7},{7,6},{8,9},{9,8},{10,11... | collective-permute-start | bytes 786440 | tf_op jit(solution)/shard_map/ppermute | solution.py:25
  6.9 2.0 %collective-permute-start.5 = (bf16[256,512]{1,0:T(8,128)(2,1)}, bf16[256,512]{1,0:T(8,128)(2,1)S(1)}, u32[]{:S(2)}, u32[]{:S(2)}) collective-permute-start(bf16[256,512]{1,0:T(8,128)(2,1)} %wo_ref.1), channel_id=1, source_target_pairs={{0,1},{1,0},{2,3},{3,2},{4,5},{5,4},{6,7},{7,6},{8,9},{9,8},{10,11... | collective-permute-start | bytes 786440 | tf_op jit(solution)/shard_map/ppermute | solution.py:25
  7.0 0.7 copy-start.1
  8.4 3.3 %collective-permute-start.6 = (f32[2]{0:T(128)}, f32[2]{0:T(128)S(1)}, u32[]{:S(2)}, u32[]{:S(2)}) collective-permute-start(f32[2]{0:T(128)} %decay_ref.1), channel_id=1, source_target_pairs={{0,1},{1,0},{2,3},{3,2},{4,5},{5,4},{6,7},{7,6},{8,9},{9,8},{10,11... | collective-permute-start | bytes 32 | tf_op jit(solution)/shard_map/ppermute | solution.py:25
  20.9 3.7 %collective-permute-start.9 = (f32[1024,256]{1,0:T(8,128)S(1)}, f32[1024,256]{1,0:T(8,128)S(1)}, u32[]{:S(2)}, u32[]{:S(2)}) collective-permute-start(f32[1024,256]{1,0:T(8,128)S(1)} %get-tuple-element.84), channel_id=1, source_target_pairs={{0,1},{1,0},{2,3},{3,2},{4,5},{5,4},{6,7},{7,6},{8,9},{9,8},{10,11... | collective-permute-start | bytes 3145736 | tf_op jit(solution)/shard_map/ppermute | solution.py:25
  24.0 2.8 %collective-permute-start.8 = (f32[1024,256]{1,0:T(8,128)S(1)}, f32[1024,256]{1,0:T(8,128)S(1)}, u32[]{:S(2)}, u32[]{:S(2)}) collective-permute-start(f32[1024,256]{1,0:T(8,128)S(1)} %get-tuple-element.82), channel_id=1, source_target_pairs={{0,1},{1,0},{2,3},{3,2},{4,5},{5,4},{6,7},{7,6},{8,9},{9,8},{10,11... | collective-permute-start | bytes 3145736 | tf_op jit(solution)/shard_map/ppermute | solution.py:25
  24.8 6.4 %collective-permute-start.11 = (bf16[512,256]{1,0:T(8,128)(2,1)S(1)}, bf16[512,256]{1,0:T(8,128)(2,1)S(1)}, u32[]{:S(2)}, u32[]{:S(2)}) collective-permute-start(bf16[512,256]{1,0:T(8,128)(2,1)S(1)} %get-tuple-element.108), channel_id=1, source_target_pairs={{0,2},{1,9},{2,0},{3,11},{4,6},{5,13},{6,4},{7,15},{8,10},{9,1},{1... | collective-permute-start | bytes 786440 | tf_op jit(solution)/shard_map/ppermute | solution.py:218
  27.0 7.1 %collective-permute-start.10 = (bf16[512,256]{1,0:T(8,128)(2,1)S(1)}, bf16[512,256]{1,0:T(8,128)(2,1)S(1)}, u32[]{:S(2)}, u32[]{:S(2)}) collective-permute-start(bf16[512,256]{1,0:T(8,128)(2,1)S(1)} %get-tuple-element.109), channel_id=1, source_target_pairs={{0,2},{1,9},{2,0},{3,11},{4,6},{5,13},{6,4},{7,15},{8,10},{9,1},{1... | collective-permute-start | bytes 786440 | tf_op jit(solution)/shard_map/ppermute | solution.py:218
  29.6 38.6 %collective-permute-start.7 = (bf16[256,512]{1,0:T(8,128)(2,1)S(1)}, bf16[256,512]{1,0:T(8,128)(2,1)S(1)}, u32[]{:S(2)}, u32[]{:S(2)}) collective-permute-start(bf16[256,512]{1,0:T(8,128)(2,1)S(1)} %get-tuple-element.78), channel_id=1, source_target_pairs={{0,1},{1,0},{2,3},{3,2},{4,5},{5,4},{6,7},{7,6},{8,9},{9,8},{10,11... | collective-permute-start | bytes 786440 | tf_op jit(solution)/shard_map/ppermute | solution.py:25
  31.3 6.2 %collective-permute-start.13 = (bf16[256,256]{1,0:T(8,128)(2,1)S(1)}, bf16[256,256]{1,0:T(8,128)(2,1)S(1)}, u32[]{:S(2)}, u32[]{:S(2)}) collective-permute-start(bf16[256,256]{1,0:T(8,128)(2,1)S(1)} %get-tuple-element.112), channel_id=1, source_target_pairs={{0,4},{1,3},{2,6},{3,1},{4,0},{5,7},{6,2},{7,5},{8,12},{9,11},{10,... | collective-permute-start | bytes 393224 | tf_op jit(solution)/shard_map/ppermute | solution.py:218
  34.2 7.2 %collective-permute-start.12 = (bf16[256,256]{1,0:T(8,128)(2,1)S(1)}, bf16[256,256]{1,0:T(8,128)(2,1)S(1)}, u32[]{:S(2)}, u32[]{:S(2)}) collective-permute-start(bf16[256,256]{1,0:T(8,128)(2,1)S(1)} %get-tuple-element.113), channel_id=1, source_target_pairs={{0,4},{1,3},{2,6},{3,1},{4,0},{5,7},{6,2},{7,5},{8,12},{9,11},{10,... | collective-permute-start | bytes 393224 | tf_op jit(solution)/shard_map/ppermute | solution.py:218
  37.6 5.3 %collective-permute-start.18 = (bf16[128,256]{1,0:T(8,128)(2,1)S(1)}, bf16[128,256]{1,0:T(8,128)(2,1)S(1)}, u32[]{:S(2)}, u32[]{:S(2)}) collective-permute-start(bf16[128,256]{1,0:T(8,128)(2,1)S(1)} %select_convert_fusion.9), channel_id=1, source_target_pairs={{0,8},{1,5},{2,10},{3,7},{4,12},{5,1},{6,14},{7,3},{8,0},{9,13},{1... | collective-permute-start | bytes 196616 | tf_op jit(solution)/shard_map/ppermute | solution.py:218
  41.4 5.6 %collective-permute-start.17 = (bf16[128,256]{1,0:T(8,128)(2,1)S(1)}, bf16[128,256]{1,0:T(8,128)(2,1)S(1)}, u32[]{:S(2)}, u32[]{:S(2)}) collective-permute-start(bf16[128,256]{1,0:T(8,128)(2,1)S(1)} %select_convert_fusion.8), channel_id=1, source_target_pairs={{0,8},{1,5},{2,10},{3,7},{4,12},{5,1},{6,14},{7,3},{8,0},{9,13},{1... | collective-permute-start | bytes 196616 | tf_op jit(solution)/shard_map/ppermute | solution.py:218
  42.9 18.8 %collective-permute-start.14 = (bf16[256,512]{1,0:T(8,128)(2,1)S(1)}, bf16[256,512]{1,0:T(8,128)(2,1)S(1)}, u32[]{:S(2)}, u32[]{:S(2)}) collective-permute-start(bf16[256,512]{1,0:T(8,128)(2,1)S(1)} %get-tuple-element.90), channel_id=1, source_target_pairs={{0,1},{2,0},{4,2},{6,4},{8,6},{10,8},{12,10},{14,12},{16,14},{18,1... | collective-permute-start | bytes 786440 | tf_op jit(solution)/shard_map/ppermute | solution.py:35
  42.9 18.8 %collective-permute-start.15 = (bf16[256,512]{1,0:T(8,128)(2,1)S(1)}, bf16[256,512]{1,0:T(8,128)(2,1)S(1)}, u32[]{:S(2)}, u32[]{:S(2)}) collective-permute-start(bf16[256,512]{1,0:T(8,128)(2,1)S(1)} %get-tuple-element.92), channel_id=1, source_target_pairs={{0,3},{2,1},{4,0},{6,2},{8,4},{10,6},{12,8},{14,10},{16,12},{18,14... | collective-permute-start | bytes 786440 | tf_op jit(solution)/shard_map/ppermute | solution.py:35
  43.0 12.2 %collective-permute-start.20 = (bf16[128,256]{1,0:T(8,128)(2,1)S(1)}, bf16[128,256]{1,0:T(8,128)(2,1)S(1)}, u32[]{:S(2)}, u32[]{:S(2)}) collective-permute-start(bf16[128,256]{1,0:T(8,128)(2,1)S(1)} %add_convert_fusion.4), channel_id=1, source_target_pairs={{0,16},{1,17},{2,18},{3,19},{4,20},{5,21},{6,22},{7,23},{8,24},{9,... | collective-permute-start | bytes 196616 | tf_op jit(solution)/shard_map/ppermute | solution.py:237
  47.1 10.1 %collective-permute-start.19 = (bf16[128,256]{1,0:T(8,128)(2,1)S(1)}, bf16[128,256]{1,0:T(8,128)(2,1)S(1)}, u32[]{:S(2)}, u32[]{:S(2)}) collective-permute-start(bf16[128,256]{1,0:T(8,128)(2,1)S(1)} %add_convert_fusion.3), channel_id=1, source_target_pairs={{0,16},{1,17},{2,18},{3,19},{4,20},{5,21},{6,22},{7,23},{8,24},{9,... | collective-permute-start | bytes 196616 | tf_op jit(solution)/shard_map/ppermute | solution.py:237
  55.1 4.3 %collective-permute-start.22 = (bf16[128,256]{1,0:T(8,128)(2,1)S(1)}, bf16[128,256]{1,0:T(8,128)(2,1)S(1)}, u32[]{:S(2)}, u32[]{:S(2)}) collective-permute-start(bf16[128,256]{1,0:T(8,128)(2,1)S(1)} %add_convert_fusion.1), channel_id=1, source_target_pairs={{0,8},{1,5},{2,10},{3,7},{4,12},{5,1},{6,14},{7,3},{8,0},{9,13},{1... | collective-permute-start | bytes 196616 | tf_op jit(solution)/shard_map/ppermute | solution.py:218
  57.2 4.3 %collective-permute-start.21 = (bf16[128,256]{1,0:T(8,128)(2,1)S(1)}, bf16[128,256]{1,0:T(8,128)(2,1)S(1)}, u32[]{:S(2)}, u32[]{:S(2)}) collective-permute-start(bf16[128,256]{1,0:T(8,128)(2,1)S(1)} %add_convert_fusion.2), channel_id=1, source_target_pairs={{0,8},{1,5},{2,10},{3,7},{4,12},{5,1},{6,14},{7,3},{8,0},{9,13},{1... | collective-permute-start | bytes 196616 | tf_op jit(solution)/shard_map/ppermute | solution.py:218
  59.5 5.0 %collective-permute-start.24 = (bf16[256,256]{1,0:T(8,128)(2,1)S(1)}, bf16[256,256]{1,0:T(8,128)(2,1)S(1)}, u32[]{:S(2)}, u32[]{:S(2)}) collective-permute-start(bf16[256,256]{1,0:T(8,128)(2,1)S(1)} %pad_maximum_fusion.4), channel_id=1, source_target_pairs={{0,4},{1,3},{2,6},{3,1},{4,0},{5,7},{6,2},{7,5},{8,12},{9,11},{10,... | collective-permute-start | bytes 393224 | tf_op jit(solution)/shard_map/ppermute | solution.py:218
  61.5 5.3 %collective-permute-start.23 = (bf16[256,256]{1,0:T(8,128)(2,1)S(1)}, bf16[256,256]{1,0:T(8,128)(2,1)S(1)}, u32[]{:S(2)}, u32[]{:S(2)}) collective-permute-start(bf16[256,256]{1,0:T(8,128)(2,1)S(1)} %pad_maximum_fusion.5), channel_id=1, source_target_pairs={{0,4},{1,3},{2,6},{3,1},{4,0},{5,7},{6,2},{7,5},{8,12},{9,11},{10,... | collective-permute-start | bytes 393224 | tf_op jit(solution)/shard_map/ppermute | solution.py:218
  61.8 6.4 %collective-permute-start.16 = (bf16[256,512]{1,0:T(8,128)(2,1)S(1)}, bf16[256,512]{1,0:T(8,128)(2,1)S(1)}, u32[]{:S(2)}, u32[]{:S(2)}) collective-permute-start(bf16[256,512]{1,0:T(8,128)(2,1)S(1)} %add_convert_fusion), channel_id=1, source_target_pairs={{0,1},{1,0},{2,3},{3,2},{4,5},{5,4},{6,7},{7,6},{8,9},{9,8},{10,11... | collective-permute-start | bytes 786440 | tf_op jit(solution)/shard_map/ppermute | solution.py:25
  64.6 6.5 %collective-permute-start.26 = (bf16[512,256]{1,0:T(8,128)(2,1)S(1)}, bf16[512,256]{1,0:T(8,128)(2,1)S(1)}, u32[]{:S(2)}, u32[]{:S(2)}) collective-permute-start(bf16[512,256]{1,0:T(8,128)(2,1)S(1)} %pad_maximum_fusion.2), channel_id=1, source_target_pairs={{0,2},{1,9},{2,0},{3,11},{4,6},{5,13},{6,4},{7,15},{8,10},{9,1},{1... | collective-permute-start | bytes 786440 | tf_op jit(solution)/shard_map/ppermute | solution.py:218
  66.8 7.1 %collective-permute-start.25 = (bf16[512,256]{1,0:T(8,128)(2,1)S(1)}, bf16[512,256]{1,0:T(8,128)(2,1)S(1)}, u32[]{:S(2)}, u32[]{:S(2)}) collective-permute-start(bf16[512,256]{1,0:T(8,128)(2,1)S(1)} %pad_maximum_fusion.3), channel_id=1, source_target_pairs={{0,2},{1,9},{2,0},{3,11},{4,6},{5,13},{6,4},{7,15},{8,10},{9,1},{1... | collective-permute-start | bytes 786440 | tf_op jit(solution)/shard_map/ppermute | solution.py:218

commit v3 on v2

--- a/solution.py
+++ b/solution.py
@@ -39,7 +39,7 @@
     bits = lax.axis_size("tm").bit_length() - 1
     count = min(3, bits)
     first = list(range(count))
-    return first, first[-1:] + first[:-1], list(range(count, bits))
+    return first[-1:] + first[:-1], first, list(range(count, bits))
 
 
 def partners(bit0, bit1):
@@ -78,12 +78,15 @@
 CORE, WINDOW, BITS = 0, 1, 2
 
 
-def places_kernel(info, starts_ref, parcel_ref, first_ref, masks_ref):
+def places_kernel(info, starts_ref, parcel_ref, shut_ref, masks_ref):
     del parcel_ref
-    blk = first_ref.shape[0]
+    blk, keys = shut_ref.shape
     core = info[CORE]
     first = jnp.where(core == 0, starts_ref[0:1], starts_ref[1:2]) - info[WINDOW]
-    first_ref[...] = jnp.transpose(jnp.broadcast_to(first, (8, blk)))[:, :1]
+    first = jnp.transpose(jnp.broadcast_to(first, (8, blk)))[:, :1]
+    at_key = lax.broadcasted_iota(jnp.int32, (blk, keys), 1)
+    at_row = lax.broadcasted_iota(jnp.int32, (blk, keys), 0) + (keys - blk)
+    shut_ref[...] = jnp.where((at_key >= first) & (at_key <= at_row), 0.0, -1e30)
     at = lax.broadcasted_iota(jnp.int32, masks_ref.shape, 0)
     masks = jnp.where(at == 0, core, 0)
     for step in range(info.shape[0] - BITS):
@@ -139,17 +142,13 @@
 
 
 def forward_kernel(
-    scale, decay_ref, decay_other_ref, x_ref, one_ref, two_ref, q_ref, k_ref, v_ref, g_attn_ref, g_ref, wk_ref, wv_ref, first_ref,
-    probs_ref, k_win_ref, v_win_ref, away_ref, here_ref, o_ref, dv_ref, shut_ref,
+    scale, decay_ref, decay_other_ref, x_ref, one_ref, two_ref, q_ref, k_ref, v_ref, g_attn_ref, g_ref, wk_ref, wv_ref, shut_ref,
+    probs_ref, k_win_ref, v_win_ref, away_ref, here_ref, o_ref, dv_ref,
 ):
     blk, width = q_ref.shape
     cols = width // 2
     k_win_ref[2 * blk :] = k_ref[...]
     v_win_ref[2 * blk :] = v_ref[...]
-    at_key = lax.broadcasted_iota(jnp.int32, shut_ref.shape, 1)
-    at_row = lax.broadcasted_iota(jnp.int32, shut_ref.shape, 0) + 2 * blk
-    allowed = (at_key >= first_ref[...]) & (at_key <= at_row)
-    shut_ref[...] = jnp.where(allowed, 0.0, -1e30)
     xs = (two_ref, one_ref, x_ref)
     for i, ref in enumerate(xs[:2]):
         rows = slice(i * blk, (i + 1) * blk)
@@ -158,15 +157,28 @@
     times = [stamps_of(x, blk) for x in xs]
     gap = (times[2][:, blk - 1 :] - jnp.concatenate(times, 1)) * LOG2E
     heads = width // HD
-    for head in range(heads):
-        c = slice(head * HD, (head + 1) * HD)
-        decay = decay_ref[head] if head < heads // 2 else decay_other_ref[head - heads // 2]
-        scores = dot(q_ref[:, c], k_win_ref[:, c], ACROSS) * (LOG2E / math.sqrt(HD))
-        probs = softmax_parts(scores + (shut_ref[...] - gap * decay))
-        probs_ref[head] = probs
-        low = probs.astype(BF)
-        o_ref[:, c] = dot(low, v_win_ref[:, c]).astype(BF)
-        dv_ref[:, c] = dot(low, g_attn_ref[:, c], DOWN).astype(BF)
+    lanes = [slice(head * HD, (head + 1) * HD) for head in range(heads)]
+
+    def scores_of(head):
+        c = lanes[head]
+        return dot(q_ref[:, c], k_win_ref[:, c], ACROSS)
+
+    ahead = scores_of(0)
+    low = None
+    for head in range(heads + 1):
+        scores = ahead
+        if head + 1 < heads:
+            ahead = scores_of(head + 1)
+        before = low
+        if head < heads:
+            decay = decay_ref[head] if head < heads // 2 else decay_other_ref[head - heads // 2]
+            probs = softmax_parts(scores * (LOG2E / math.sqrt(HD)) + (shut_ref[...] - gap * decay))
+            probs_ref[head] = probs
+            low = probs.astype(BF)
+        if head:
+            c = lanes[head - 1]
+            o_ref[:, c] = dot(before, v_win_ref[:, c]).astype(BF)
+            dv_ref[:, c] = dot(before, g_attn_ref[:, c], DOWN).astype(BF)
     for out_ref, lo in ((here_ref, 0), (away_ref, cols)):
         c = slice(lo, lo + cols)
         out_ref[:width] = window_terms(xs, dv_ref, c, scale)
@@ -181,14 +193,26 @@
     width = q_ref.shape[1]
     cols = width // 2
     inv_scale = 1.0 / math.sqrt(HD)
-    for head in range(width // HD):
-        c = slice(head * HD, (head + 1) * HD)
-        probs = probs_ref[head]
-        d_probs = dot(g_attn_ref[:, c], v_win_ref[:, c], ACROSS)
-        delta = jnp.sum(probs * d_probs, -1, keepdims=True)
-        d_scores = (probs * (d_probs - delta)).astype(BF)
-        dq_ref[:, c] = (dot(d_scores, k_win_ref[:, c]) * inv_scale).astype(BF)
-        dk_ref[:, c] = (dot(d_scores, q_ref[:, c], DOWN) * inv_scale).astype(BF)
+    heads = width // HD
+    lanes = [slice(head * HD, (head + 1) * HD) for head in range(heads)]
+
+    def d_probs_of(head):
+        return dot(g_attn_ref[:, lanes[head]], v_win_ref[:, lanes[head]], ACROSS)
+
+    ahead = d_probs_of(0)
+    d_scores = None
+    for head in range(heads + 1):
+        d_probs = ahead
+        if head + 1 < heads:
+            ahead = d_probs_of(head + 1)
+        if head:
+            c = lanes[head - 1]
+            dq_ref[:, c] = (dot(d_scores, k_win_ref[:, c]) * inv_scale).astype(BF)
+            dk_ref[:, c] = (dot(d_scores, q_ref[:, c], DOWN) * inv_scale).astype(BF)
+        if head < heads:
+            probs = probs_ref[head]
+            delta = jnp.sum(probs * d_probs, -1, keepdims=True)
+            d_scores = (probs * (d_probs - delta)).astype(BF)
     for out_ref, lo in ((here_ref, 0), (away_ref, cols)):
         c = slice(lo, lo + cols)
         out_ref[:width] = window_terms((x_ref,), dq_ref, c, scale)
@@ -276,8 +300,8 @@
     heads = ((width // HD, blk, 3 * blk), F32)
     scale = 1.0 / math.sqrt(2 * blk * n)
 
-    first, masks = call(
-        places_kernel, "places", [((blk, 1), jnp.int32), ((8, width), jnp.int32)], (info, starts, parcel), work=0
+    shut, masks = call(
+        places_kernel, "places", [((blk, 3 * blk), F32), ((8, width), jnp.int32)], (info, starts, parcel), work=0
     )
     others = [swap_cores(tied(x, parcel)) for x in (w_query, w_key, w_value, w_out, decay)]
     decay_other = others.pop()
@@ -293,9 +317,8 @@
         functools.partial(forward_kernel, scale),
         "forward",
         [heads, window, window, pair, pair, rows, window],
-        (decay, decay_other, parcel, back_one, back_two, q, k_own, v_own, g_attn, g_own, wk, wv, first),
+        (decay, decay_other, parcel, back_one, back_two, q, k_own, v_own, g_attn, g_own, wk, wv, shut),
         smem=2,
-        scratch=[((blk, 3 * blk), F32)],
         work=32,
     )
     sum_a = Summed(masks[1:], orders, here_a, away_a)
@@ -312,36 +335,20 @@
         tail_kernel, "tail", [rows, rows, ((blk, width), F32), rows], (dk, wk, dv, wv, dq, wq, attn, wo), smem=0, work=8
     )
     steps = len(orders[0])
-    halos = []
-
-    def start_halos(*after):
-        halos.append(shift_blocks(tied(to_one, *after), -1))
-        halos.append(shift_blocks(tied(to_two, *after), -2))
-
-    def end_halos():
-        return (to_self + halos[0].astype(F32) + halos[1].astype(F32)).astype(BF)
-
-    sum_a.halve(0)
-    sum_b.halve(0, sum_a.send)
-    sum_a.halve(1, sum_b.send)
-    sum_b.halve(1, sum_a.send)
-    sum_a.halve(2, sum_b.send)
-    sum_b.halve(2, sum_a.send)
-    start_halos(sum_b.send)
+    for step in range(steps):
+        sum_a.halve(step, *([sum_b.send] if step else []))
+        sum_b.halve(step, sum_a.send)
+    halo_one = shift_blocks(tied(to_one, sum_b.send), -1)
+    halo_two = shift_blocks(tied(to_two, sum_b.send), -2)
     sum_a.exchange(sum_b.send)
     sum_b.exchange(sum_a.send)
-    sum_a.gather(2, sum_b.send)
-    sum_b.gather(2, sum_a.send)
-    sum_a.placed(2)
-    sum_b.placed(2, sum_a.whole)
-    sum_a.gather(1, sum_b.send)
-    sum_b.gather(1, sum_a.send)
-    sum_a.placed(1)
-    sum_b.placed(1, sum_a.whole)
-    sum_a.gather(0, sum_b.send)
-    sum_b.gather(0, sum_a.send)
-    sum_a.placed(0)
-    grad_own = end_halos()
+    for step in reversed(range(steps)):
+        sum_a.gather(step, sum_b.send)
+        sum_b.gather(step, sum_a.send)
+        sum_a.placed(step)
+        if step:
+            sum_b.placed(step, sum_a.whole)
+    grad_own = (to_self + halo_one.astype(F32) + halo_two.astype(F32)).astype(BF)
     on_second = masks[0][None, None] == 1
 
     def both_blocks(own):

time: 75.2 us -> 72.8 us (0.968)
  waiting for transfers between devices: 24.7 us -> 16.3 us
  starting transfers between devices: 30.1 us -> 37.4 us
  Pallas kernels: 12.5 us -> 11.4 us
    ppermute x2, starting transfers between devices: 5.57 us -> 10.5 us  [exchange(): got = lax.ppermute(self.send, AXES, partners(bit, bit))]
    ppermute x2, waiting for transfers between devices: 7.19 us -> 2.27 us  [exchange(): got = lax.ppermute(self.send, AXES, partners(bit, bit))]
    ppermute x12, starting transfers between devices: 16.9 us -> 20.3 us  [passed(): lax.ppermute(x, AXES, partners(*(order[step] for order in self.orders)))]
    ppermute x12, waiting for transfers between devices: 12.4 us -> 9.71 us  [passed(): lax.ppermute(x, AXES, partners(*(order[step] for order in self.orders)))]
    ppermute x9, starting transfers between devices: 3.53 us -> 2.37 us  [swap_cores(): return lax.ppermute(x, 'rep', [(0, 1), (1, 0)])]
    pallas_call x5, Pallas kernels: 12.5 us -> 11.4 us  [call(): pl.pallas_call(kernel, in_specs=[pl.BlockSpec(memory_space=space) for spa...]
  transfers between devices with their start and end apart: 27 -> 27, of which waited for: 13 -> 12; matrix products, arithmetic and copies ran while one was open for 5% -> 5% of each run, Pallas kernels for 10% -> 10%
where the time goes in v3:
time: 72.8 us; the launch traced here: 72.6 us
  starting transfers between devices  37.4 us (51%)
  waiting for transfers between devices  16.3 us (22%)
  Pallas kernels  11.4 us (16%)
  other arithmetic  5.64 us (8%)
  local copies, waits for them, and re-layouts  1.11 us (2%)
  between operations  0.88 us (1%)
    ppermute x12, starting transfers between devices, passed(): lax.ppermute(x, AXES, partners(*(order[step] for order in self.orders)))  20.3 us
    pallas_call x5, Pallas kernels, call(): pl.pallas_call(kernel, in_specs=[pl.BlockSpec(memory_space=space) for spa...  11.4 us
    ppermute x2, starting transfers between devices, exchange(): got = lax.ppermute(self.send, AXES, partners(bit, bit))  10.5 us
    ppermute x12, waiting for transfers between devices, passed(): lax.ppermute(x, AXES, partners(*(order[step] for order in self.orders)))  9.71 us
    ppermute x4, waiting for transfers between devices, shift_blocks(): return lax.ppermute(x, AXES, route)  4.29 us
    ppermute x4, starting transfers between devices, shift_blocks(): return lax.ppermute(x, AXES, route)  4.16 us
    ppermute x9, starting transfers between devices, swap_cores(): return lax.ppermute(x, 'rep', [(0, 1), (1, 0)])  2.37 us
    ppermute x2, waiting for transfers between devices, exchange(): got = lax.ppermute(self.send, AXES, partners(bit, bit))  2.27 us
  transfers between devices with their start and end apart: 27, of which 12 were waited for; matrix products, arithmetic and copies ran while one was open for 5% of the time, Pallas kernels for 10%

profile of v3, /device:TPU:0, one launch (start us, length us, event | category | flops | bytes accessed | tf_op | source)
XLA Modules:
  0.0 72.6 jit_solution(472725944624041746)
XLA Ops:
  2.3 2.6 %collective-permute-start = (bf16[272,512]{1,0:T(8,128)(2,1)S(1)}, bf16[272,512]{1,0:T(8,128)(2,1)S(1)}, u32[]{:S(2)}, u32[]{:S(2)}) collective-permute-start(bf16[272,512]{1,0:T(8,128)(2,1)S(1)} %pad_maximum_fusion.1.parcel_ref.x_ref), channel_id=1, source_target_pairs={{0,2},{2,4},{4,6},{6,8},{8,10},{10,12},{12,14},{14,16},{16,18},{18... | collective-permute-start | bytes 835592 | tf_op jit(solution)/shard_map/ppermute | solution.py:35
  4.8 1.5 %collective-permute-start.1 = (bf16[272,512]{1,0:T(8,128)(2,1)S(1)}, bf16[272,512]{1,0:T(8,128)(2,1)S(1)}, u32[]{:S(2)}, u32[]{:S(2)}) collective-permute-start(bf16[272,512]{1,0:T(8,128)(2,1)S(1)} %pad_maximum_fusion.1.parcel_ref.x_ref), channel_id=1, source_target_pairs={{0,4},{2,6},{4,8},{6,10},{8,12},{10,14},{12,16},{14,18},{16,20},{1... | collective-permute-start | bytes 835592 | tf_op jit(solution)/shard_map/ppermute | solution.py:35
  9.0 2.8 %before.1 = (bf16[256,512]{1,0:T(8,128)(2,1)S(1)}, bf16[256,512]{1,0:T(8,128)(2,1)S(1)}, bf16[256,512]{1,0:T(8,128)(2,1)S(1)}, bf16[256,512]{1,0:T(8,128)(2,1)S(...) custom-call(s32[5]{0:T(128)S(1)} %stack.58.info, ...), custom_call_target="tpu_custom_call" | custom-call | tf_op jit(solution)/shard_map/before/pallas_call | solution.py:65
  11.8 2.1 %collective-permute-done.one_ref = bf16[272,512]{1,0:T(8,128)(2,1)S(1)} collective-permute-done((bf16[272,512]{1,0:T(8,128)(2,1)S(1)}, bf16[272,512]{1,0:T(8,128)(2,1)S(1)}, u32[]{:S(2)}, u32[]{:S(2)}) %collective-permute-start) | collective-permute-done | bytes 278560 | tf_op jit(solution)/shard_map/ppermute | solution.py:35
  14.0 2.2 %collective-permute-done.1.two_ref = bf16[272,512]{1,0:T(8,128)(2,1)S(1)} collective-permute-done((bf16[272,512]{1,0:T(8,128)(2,1)S(1)}, bf16[272,512]{1,0:T(8,128)(2,1)S(1)}, u32[]{:S(2)}, u32[]{:S(2)}) %collective-permute-start.1) | collective-permute-done | bytes 278560 | tf_op jit(solution)/shard_map/ppermute | solution.py:35
  16.1 4.0 %forward.1 = (f32[4,256,768]{2,1,0:T(8,128)S(1)}, bf16[768,512]{1,0:T(8,128)(2,1)S(1)}, bf16[768,512]{1,0:T(8,128)(2,1)S(1)}, f32[1024,256]{1,0:T(8,128)S(1)}, f...) custom-call(f32[2]{0:T(128)S(1)} %copy-done.2, ...), custom_call_target="tpu_custom_call" | custom-call | flops 4294967296 | bytes 4194304 | tf_op jit(solution)/shard_map/forward/pallas_call | solution.py:65
  20.2 2.5 %backward.1 = (f32[1024,256]{1,0:T(8,128)S(1)}, f32[1024,256]{1,0:T(8,128)S(1)}, bf16[256,512]{1,0:T(8,128)(2,1)S(1)}, bf16[768,512]{1,0:T(8,128)(2,1)S(1)}) custom-call(bf16[272,512]{1,0:T(8,128)(2,1)S(1)} %pad_maximum_fusion.1.parcel_ref.x_ref, bf16[272,512]{1,0:T(8,128)(2,1)S(1)} %collective-permute-done.one_ref, ...), custom_call_target="tpu_custom_call" | custom-call | flops 3221225472 | bytes 3145728 | tf_op jit(solution)/shard_map/backward/pallas_call | solution.py:65
  23.6 2.2 %collective-permute-start.11 = (bf16[512,256]{1,0:T(8,128)(2,1)S(1)}, bf16[512,256]{1,0:T(8,128)(2,1)S(1)}, u32[]{:S(2)}, u32[]{:S(2)}) collective-permute-start(bf16[512,256]{1,0:T(8,128)(2,1)S(1)} %get-tuple-element.108), channel_id=1, source_target_pairs={{0,8},{1,3},{2,10},{3,1},{4,12},{5,7},{6,14},{7,5},{8,0},{9,11},{1... | collective-permute-start | bytes 786440 | tf_op jit(solution)/shard_map/ppermute | solution.py:242
  25.9 2.4 %collective-permute-start.10 = (bf16[512,256]{1,0:T(8,128)(2,1)S(1)}, bf16[512,256]{1,0:T(8,128)(2,1)S(1)}, u32[]{:S(2)}, u32[]{:S(2)}) collective-permute-start(bf16[512,256]{1,0:T(8,128)(2,1)S(1)} %get-tuple-element.109), channel_id=1, source_target_pairs={{0,8},{1,3},{2,10},{3,1},{4,12},{5,7},{6,14},{7,5},{8,0},{9,11},{1... | collective-permute-start | bytes 786440 | tf_op jit(solution)/shard_map/ppermute | solution.py:242
  28.3 1.3 %tail.1 = (bf16[256,512]{1,0:T(8,128)(2,1)S(1)}, bf16[256,512]{1,0:T(8,128)(2,1)S(1)}, f32[256,512]{1,0:T(8,128)S(1)}, bf16[256,512]{1,0:T(8,128)(2,1)S(1)}) custom-call(bf16[768,512]{1,0:T(8,128)(2,1)S(1)} %get-tuple-element.72.dk_ref, bf16[512,512]{1,0:T(8,128)(2,1)S(1)} %get-tuple-element.66.wk_ref, bf16[768,512]{1,0:T(8,128)(2,1)S(1)} %get-tuple-element.73.dv_ref, ...), custom_call_target="tpu_custom_call" | custom-call | flops 1073741824 | bytes 1048576 | tf_op jit(solution)/shard_map/tail/pallas_call | solution.py:65
  30.2 1.2 %collective-permute-start.13 = (bf16[256,256]{1,0:T(8,128)(2,1)S(1)}, bf16[256,256]{1,0:T(8,128)(2,1)S(1)}, u32[]{:S(2)}, u32[]{:S(2)}) collective-permute-start(bf16[256,256]{1,0:T(8,128)(2,1)S(1)} %get-tuple-element.112), channel_id=1, source_target_pairs={{0,2},{1,5},{2,0},{3,7},{4,6},{5,1},{6,4},{7,3},{8,10},{9,13},{10,... | collective-permute-start | bytes 393224 | tf_op jit(solution)/shard_map/ppermute | solution.py:242
  31.4 1.6 %collective-permute-done.10 = bf16[512,256]{1,0:T(8,128)(2,1)S(1)} collective-permute-done((bf16[512,256]{1,0:T(8,128)(2,1)S(1)}, bf16[512,256]{1,0:T(8,128)(2,1)S(1)}, u32[]{:S(2)}, u32[]{:S(2)}) %collective-permute-start.10) | collective-permute-done | bytes 262176 | tf_op jit(solution)/shard_map/ppermute | solution.py:242
  33.0 1.2 %collective-permute-start.12 = (bf16[256,256]{1,0:T(8,128)(2,1)S(1)}, bf16[256,256]{1,0:T(8,128)(2,1)S(1)}, u32[]{:S(2)}, u32[]{:S(2)}) collective-permute-start(bf16[256,256]{1,0:T(8,128)(2,1)S(1)} %get-tuple-element.113), channel_id=1, source_target_pairs={{0,2},{1,5},{2,0},{3,7},{4,6},{5,1},{6,4},{7,3},{8,10},{9,13},{10,... | collective-permute-start | bytes 393224 | tf_op jit(solution)/shard_map/ppermute | solution.py:242
  34.2 1.1 %collective-permute-done.13 = bf16[256,256]{1,0:T(8,128)(2,1)S(1)} collective-permute-done((bf16[256,256]{1,0:T(8,128)(2,1)S(1)}, bf16[256,256]{1,0:T(8,128)(2,1)S(1)}, u32[]{:S(2)}, u32[]{:S(2)}) %collective-permute-start.13) | collective-permute-done | bytes 131104 | tf_op jit(solution)/shard_map/ppermute | solution.py:242
  35.3 2.4 %collective-permute-start.18 = (bf16[128,256]{1,0:T(8,128)(2,1)S(1)}, bf16[128,256]{1,0:T(8,128)(2,1)S(1)}, u32[]{:S(2)}, u32[]{:S(2)}) collective-permute-start(bf16[128,256]{1,0:T(8,128)(2,1)S(1)} %select_convert_fusion.9), channel_id=1, source_target_pairs={{0,4},{1,9},{2,6},{3,11},{4,0},{5,13},{6,2},{7,15},{8,12},{9,1},{1... | collective-permute-start | bytes 196616 | tf_op jit(solution)/shard_map/ppermute | solution.py:242
  38.1 2.4 %collective-permute-start.17 = (bf16[128,256]{1,0:T(8,128)(2,1)S(1)}, bf16[128,256]{1,0:T(8,128)(2,1)S(1)}, u32[]{:S(2)}, u32[]{:S(2)}) collective-permute-start(bf16[128,256]{1,0:T(8,128)(2,1)S(1)} %select_convert_fusion.8), channel_id=1, source_target_pairs={{0,4},{1,9},{2,6},{3,11},{4,0},{5,13},{6,2},{7,15},{8,12},{9,1},{1... | collective-permute-start | bytes 196616 | tf_op jit(solution)/shard_map/ppermute | solution.py:242
  40.6 4.8 %collective-permute-start.20 = (bf16[128,256]{1,0:T(8,128)(2,1)S(1)}, bf16[128,256]{1,0:T(8,128)(2,1)S(1)}, u32[]{:S(2)}, u32[]{:S(2)}) collective-permute-start(bf16[128,256]{1,0:T(8,128)(2,1)S(1)} %add_convert_fusion.4), channel_id=1, source_target_pairs={{0,16},{1,17},{2,18},{3,19},{4,20},{5,21},{6,22},{7,23},{8,24},{9,... | collective-permute-start | bytes 196616 | tf_op jit(solution)/shard_map/ppermute | solution.py:261
  45.5 5.7 %collective-permute-start.19 = (bf16[128,256]{1,0:T(8,128)(2,1)S(1)}, bf16[128,256]{1,0:T(8,128)(2,1)S(1)}, u32[]{:S(2)}, u32[]{:S(2)}) collective-permute-start(bf16[128,256]{1,0:T(8,128)(2,1)S(1)} %add_convert_fusion.3), channel_id=1, source_target_pairs={{0,16},{1,17},{2,18},{3,19},{4,20},{5,21},{6,22},{7,23},{8,24},{9,... | collective-permute-start | bytes 196616 | tf_op jit(solution)/shard_map/ppermute | solution.py:261
  51.2 1.7 %collective-permute-done.20 = bf16[128,256]{1,0:T(8,128)(2,1)S(1)} collective-permute-done((bf16[128,256]{1,0:T(8,128)(2,1)S(1)}, bf16[128,256]{1,0:T(8,128)(2,1)S(1)}, u32[]{:S(2)}, u32[]{:S(2)}) %collective-permute-start.20) | collective-permute-done | bytes 65568 | tf_op jit(solution)/shard_map/ppermute | solution.py:261
  53.6 1.5 %collective-permute-start.21 = (bf16[128,256]{1,0:T(8,128)(2,1)S(1)}, bf16[128,256]{1,0:T(8,128)(2,1)S(1)}, u32[]{:S(2)}, u32[]{:S(2)}) collective-permute-start(bf16[128,256]{1,0:T(8,128)(2,1)S(1)} %add_convert_fusion.2), channel_id=1, source_target_pairs={{0,4},{1,9},{2,6},{3,11},{4,0},{5,13},{6,2},{7,15},{8,12},{9,1},{1... | collective-permute-start | bytes 196616 | tf_op jit(solution)/shard_map/ppermute | solution.py:242
  55.0 2.1 %collective-permute-done.22 = bf16[128,256]{1,0:T(8,128)(2,1)S(1)} collective-permute-done((bf16[128,256]{1,0:T(8,128)(2,1)S(1)}, bf16[128,256]{1,0:T(8,128)(2,1)S(1)}, u32[]{:S(2)}, u32[]{:S(2)}) %collective-permute-start.22) | collective-permute-done | bytes 65568 | tf_op jit(solution)/shard_map/ppermute | solution.py:242
  57.2 0.9 %collective-permute-start.24 = (bf16[256,256]{1,0:T(8,128)(2,1)S(1)}, bf16[256,256]{1,0:T(8,128)(2,1)S(1)}, u32[]{:S(2)}, u32[]{:S(2)}) collective-permute-start(bf16[256,256]{1,0:T(8,128)(2,1)S(1)} %pad_maximum_fusion.4), channel_id=1, source_target_pairs={{0,2},{1,5},{2,0},{3,7},{4,6},{5,1},{6,4},{7,3},{8,10},{9,13},{10,... | collective-permute-start | bytes 393224 | tf_op jit(solution)/shard_map/ppermute | solution.py:242
  58.2 1.9 %collective-permute-start.23 = (bf16[256,256]{1,0:T(8,128)(2,1)S(1)}, bf16[256,256]{1,0:T(8,128)(2,1)S(1)}, u32[]{:S(2)}, u32[]{:S(2)}) collective-permute-start(bf16[256,256]{1,0:T(8,128)(2,1)S(1)} %pad_maximum_fusion.5), channel_id=1, source_target_pairs={{0,2},{1,5},{2,0},{3,7},{4,6},{5,1},{6,4},{7,3},{8,10},{9,13},{10,... | collective-permute-start | bytes 393224 | tf_op jit(solution)/shard_map/ppermute | solution.py:242
  60.3 2.0 %collective-permute-done.24 = bf16[256,256]{1,0:T(8,128)(2,1)S(1)} collective-permute-done((bf16[256,256]{1,0:T(8,128)(2,1)S(1)}, bf16[256,256]{1,0:T(8,128)(2,1)S(1)}, u32[]{:S(2)}, u32[]{:S(2)}) %collective-permute-start.24) | collective-permute-done | bytes 131104 | tf_op jit(solution)/shard_map/ppermute | solution.py:242
  62.3 2.1 %collective-permute-start.26 = (bf16[512,256]{1,0:T(8,128)(2,1)S(1)}, bf16[512,256]{1,0:T(8,128)(2,1)S(1)}, u32[]{:S(2)}, u32[]{:S(2)}) collective-permute-start(bf16[512,256]{1,0:T(8,128)(2,1)S(1)} %pad_maximum_fusion.2), channel_id=1, source_target_pairs={{0,8},{1,3},{2,10},{3,1},{4,12},{5,7},{6,14},{7,5},{8,0},{9,11},{1... | collective-permute-start | bytes 786440 | tf_op jit(solution)/shard_map/ppermute | solution.py:242
  64.5 2.1 %collective-permute-start.25 = (bf16[512,256]{1,0:T(8,128)(2,1)S(1)}, bf16[512,256]{1,0:T(8,128)(2,1)S(1)}, u32[]{:S(2)}, u32[]{:S(2)}) collective-permute-start(bf16[512,256]{1,0:T(8,128)(2,1)S(1)} %pad_maximum_fusion.3), channel_id=1, source_target_pairs={{0,8},{1,3},{2,10},{3,1},{4,12},{5,7},{6,14},{7,5},{8,0},{9,11},{1... | collective-permute-start | bytes 786440 | tf_op jit(solution)/shard_map/ppermute | solution.py:242
  66.6 1.1 %maximum_select_fusion.1 = (bf16[2,256,512]{2,1,0:T(8,128)(2,1)}, bf16[2,256,512]{2,1,0:T(8,128)(2,1)}) fusion(bf16[1,256,512]{2,1,0:T(8,128)(2,1)S(1)} %bitcast.12, bf16[1,256,512]{2,1,0:T(8,128)(2,1)S(1)} %bitcast.14, pred[512]{0:T(512)(128)(4,1)S(1)} %compare_reduce_fusion, bf16[1,256,512]{2,1,0:T(8,128)(2,1)S(1)} %bitcast.13, ...), kind=kLoop, calls=%fused_computation.3 | loop fusion | flops 1572864 | bytes 2097664 | tf_op jit(solution)/shard_map/jit(_where)/select_n | solution.py:356
  67.7 1.1 %collective-permute-done.26 = bf16[512,256]{1,0:T(8,128)(2,1)S(1)} collective-permute-done((bf16[512,256]{1,0:T(8,128)(2,1)S(1)}, bf16[512,256]{1,0:T(8,128)(2,1)S(1)}, u32[]{:S(2)}, u32[]{:S(2)}) %collective-permute-start.26) | collective-permute-done | bytes 262176 | tf_op jit(solution)/shard_map/ppermute | solution.py:242
  68.8 0.9 %select_convert_fusion.4 = (f32[512,256]{1,0:T(8,128)S(1)}, f32[512,256]{1,0:T(8,128)}) fusion(bf16[512,256]{1,0:T(8,128)(2,1)S(1)} %pad_maximum_fusion.2, bf16[512,256]{1,0:T(8,128)(2,1)S(1)} %collective-permute-done.26, pred[256]{0:T(512)(128)(4,1)S(1)} %get-tuple-element.105), kind=kLoop, calls=%fused_computation.19 | loop fusion | flops 524288 | bytes 1573120 | tf_op jit(solution)/shard_map/convert_element_type | solution.py:360
  69.7 0.9 %pad_maximum_fusion = f32[256,512]{1,0:T(8,128)} fusion(f32[256,256]{1,0:T(8,128)S(1)} %get-tuple-element.120, f32[256,256]{1,0:T(8,128)S(1)} %get-tuple-element.119), kind=kLoop, calls=%fused_computation.4 | loop fusion | flops 131072 | bytes 1048576 | tf_op jit(solution)/shard_map/concatenate | solution.py:361
  70.5 1.0 %collective-permute-done.25 = bf16[512,256]{1,0:T(8,128)(2,1)S(1)} collective-permute-done((bf16[512,256]{1,0:T(8,128)(2,1)S(1)}, bf16[512,256]{1,0:T(8,128)(2,1)S(1)}, u32[]{:S(2)}, u32[]{:S(2)}) %collective-permute-start.25) | collective-permute-done | bytes 262176 | tf_op jit(solution)/shard_map/ppermute | solution.py:242
  71.6 1.0 %select_convert_fusion.2 = (f32[512,256]{1,0:T(8,128)}, f32[512,256]{1,0:T(8,128)}) fusion(bf16[512,256]{1,0:T(8,128)(2,1)S(1)} %pad_maximum_fusion.3, bf16[512,256]{1,0:T(8,128)(2,1)S(1)} %collective-permute-done.25, pred[256]{0:T(512)(128)(4,1)S(1)} %get-tuple-element.105), kind=kLoop, calls=%fused_computation.17 | loop fusion | flops 524288 | bytes 1573120 | tf_op jit(solution)/shard_map/convert_element_type | solution.py:363
  (64 shorter events, 7.7 us)
Async XLA Ops:
  0.6 1.1 %copy-start = (bf16[2,256,512]{2,1,0:T(8,128)(2,1)S(1)}, bf16[2,256,512]{2,1,0:T(8,128)(2,1)}, u32[]{:S(2)}) copy-start(bf16[2,256,512]{2,1,0:T(8,128)(2,1)} %param.9) | copy-start | bytes 1572868
  0.6 15.5 %copy-start.2 = (f32[2]{0:T(128)S(1)}, f32[2]{0:T(128)}, u32[]{:S(2)}) copy-start(f32[2]{0:T(128)} %decay_ref.1) | copy-start | bytes 28
  1.8 5.1 %collective-permute-start.2 = (bf16[512,256]{1,0:T(8,128)(2,1)}, bf16[512,256]{1,0:T(8,128)(2,1)S(1)}, u32[]{:S(2)}, u32[]{:S(2)}) collective-permute-start(bf16[512,256]{1,0:T(8,128)(2,1)} %wq_ref.1), channel_id=1, source_target_pairs={{0,1},{1,0},{2,3},{3,2},{4,5},{5,4},{6,7},{7,6},{8,9},{9,8},{10,11... | collective-permute-start | bytes 786440 | tf_op jit(solution)/shard_map/ppermute | solution.py:25
  2.3 11.7 %collective-permute-start = (bf16[272,512]{1,0:T(8,128)(2,1)S(1)}, bf16[272,512]{1,0:T(8,128)(2,1)S(1)}, u32[]{:S(2)}, u32[]{:S(2)}) collective-permute-start(bf16[272,512]{1,0:T(8,128)(2,1)S(1)} %pad_maximum_fusion.1.parcel_ref.x_ref), channel_id=1, source_target_pairs={{0,2},{2,4},{4,6},{6,8},{8,10},{10,12},{12,14},{14,16},{16,18},{18... | collective-permute-start | bytes 835592 | tf_op jit(solution)/shard_map/ppermute | solution.py:35
  4.8 11.3 %collective-permute-start.1 = (bf16[272,512]{1,0:T(8,128)(2,1)S(1)}, bf16[272,512]{1,0:T(8,128)(2,1)S(1)}, u32[]{:S(2)}, u32[]{:S(2)}) collective-permute-start(bf16[272,512]{1,0:T(8,128)(2,1)S(1)} %pad_maximum_fusion.1.parcel_ref.x_ref), channel_id=1, source_target_pairs={{0,4},{2,6},{4,8},{6,10},{8,12},{10,14},{12,16},{14,18},{16,20},{1... | collective-permute-start | bytes 835592 | tf_op jit(solution)/shard_map/ppermute | solution.py:35
  6.4 2.2 %collective-permute-start.3 = (bf16[512,256]{1,0:T(8,128)(2,1)}, bf16[512,256]{1,0:T(8,128)(2,1)S(1)}, u32[]{:S(2)}, u32[]{:S(2)}) collective-permute-start(bf16[512,256]{1,0:T(8,128)(2,1)} %wk_ref.1), channel_id=1, source_target_pairs={{0,1},{1,0},{2,3},{3,2},{4,5},{5,4},{6,7},{7,6},{8,9},{9,8},{10,11... | collective-permute-start | bytes 786440 | tf_op jit(solution)/shard_map/ppermute | solution.py:25
  6.4 2.6 %collective-permute-start.4 = (bf16[512,256]{1,0:T(8,128)(2,1)}, bf16[512,256]{1,0:T(8,128)(2,1)S(1)}, u32[]{:S(2)}, u32[]{:S(2)}) collective-permute-start(bf16[512,256]{1,0:T(8,128)(2,1)} %wv_ref.1), channel_id=1, source_target_pairs={{0,1},{1,0},{2,3},{3,2},{4,5},{5,4},{6,7},{7,6},{8,9},{9,8},{10,11... | collective-permute-start | bytes 786440 | tf_op jit(solution)/shard_map/ppermute | solution.py:25
  6.9 2.2 %collective-permute-start.5 = (bf16[256,512]{1,0:T(8,128)(2,1)}, bf16[256,512]{1,0:T(8,128)(2,1)S(1)}, u32[]{:S(2)}, u32[]{:S(2)}) collective-permute-start(bf16[256,512]{1,0:T(8,128)(2,1)} %wo_ref.1), channel_id=1, source_target_pairs={{0,1},{1,0},{2,3},{3,2},{4,5},{5,4},{6,7},{7,6},{8,9},{9,8},{10,11... | collective-permute-start | bytes 786440 | tf_op jit(solution)/shard_map/ppermute | solution.py:25
  7.0 0.7 copy-start.1
  8.5 3.3 %collective-permute-start.6 = (f32[2]{0:T(128)}, f32[2]{0:T(128)S(1)}, u32[]{:S(2)}, u32[]{:S(2)}) collective-permute-start(f32[2]{0:T(128)} %decay_ref.1), channel_id=1, source_target_pairs={{0,1},{1,0},{2,3},{3,2},{4,5},{5,4},{6,7},{7,6},{8,9},{9,8},{10,11... | collective-permute-start | bytes 32 | tf_op jit(solution)/shard_map/ppermute | solution.py:25
  20.1 3.2 %collective-permute-start.9 = (f32[1024,256]{1,0:T(8,128)S(1)}, f32[1024,256]{1,0:T(8,128)S(1)}, u32[]{:S(2)}, u32[]{:S(2)}) collective-permute-start(f32[1024,256]{1,0:T(8,128)S(1)} %get-tuple-element.84), channel_id=1, source_target_pairs={{0,1},{1,0},{2,3},{3,2},{4,5},{5,4},{6,7},{7,6},{8,9},{9,8},{10,11... | collective-permute-start | bytes 3145736 | tf_op jit(solution)/shard_map/ppermute | solution.py:25
  22.7 3.1 %collective-permute-start.8 = (f32[1024,256]{1,0:T(8,128)S(1)}, f32[1024,256]{1,0:T(8,128)S(1)}, u32[]{:S(2)}, u32[]{:S(2)}) collective-permute-start(f32[1024,256]{1,0:T(8,128)S(1)} %get-tuple-element.82), channel_id=1, source_target_pairs={{0,1},{1,0},{2,3},{3,2},{4,5},{5,4},{6,7},{7,6},{8,9},{9,8},{10,11... | collective-permute-start | bytes 3145736 | tf_op jit(solution)/shard_map/ppermute | solution.py:25
  23.6 6.6 %collective-permute-start.11 = (bf16[512,256]{1,0:T(8,128)(2,1)S(1)}, bf16[512,256]{1,0:T(8,128)(2,1)S(1)}, u32[]{:S(2)}, u32[]{:S(2)}) collective-permute-start(bf16[512,256]{1,0:T(8,128)(2,1)S(1)} %get-tuple-element.108), channel_id=1, source_target_pairs={{0,8},{1,3},{2,10},{3,1},{4,12},{5,7},{6,14},{7,5},{8,0},{9,11},{1... | collective-permute-start | bytes 786440 | tf_op jit(solution)/shard_map/ppermute | solution.py:242
  25.9 7.0 %collective-permute-start.10 = (bf16[512,256]{1,0:T(8,128)(2,1)S(1)}, bf16[512,256]{1,0:T(8,128)(2,1)S(1)}, u32[]{:S(2)}, u32[]{:S(2)}) collective-permute-start(bf16[512,256]{1,0:T(8,128)(2,1)S(1)} %get-tuple-element.109), channel_id=1, source_target_pairs={{0,8},{1,3},{2,10},{3,1},{4,12},{5,7},{6,14},{7,5},{8,0},{9,11},{1... | collective-permute-start | bytes 786440 | tf_op jit(solution)/shard_map/ppermute | solution.py:242
  29.6 37.0 %collective-permute-start.7 = (bf16[256,512]{1,0:T(8,128)(2,1)S(1)}, bf16[256,512]{1,0:T(8,128)(2,1)S(1)}, u32[]{:S(2)}, u32[]{:S(2)}) collective-permute-start(bf16[256,512]{1,0:T(8,128)(2,1)S(1)} %get-tuple-element.78), channel_id=1, source_target_pairs={{0,1},{1,0},{2,3},{3,2},{4,5},{5,4},{6,7},{7,6},{8,9},{9,8},{10,11... | collective-permute-start | bytes 786440 | tf_op jit(solution)/shard_map/ppermute | solution.py:25
  30.2 5.0 %collective-permute-start.13 = (bf16[256,256]{1,0:T(8,128)(2,1)S(1)}, bf16[256,256]{1,0:T(8,128)(2,1)S(1)}, u32[]{:S(2)}, u32[]{:S(2)}) collective-permute-start(bf16[256,256]{1,0:T(8,128)(2,1)S(1)} %get-tuple-element.112), channel_id=1, source_target_pairs={{0,2},{1,5},{2,0},{3,7},{4,6},{5,1},{6,4},{7,3},{8,10},{9,13},{10,... | collective-permute-start | bytes 393224 | tf_op jit(solution)/shard_map/ppermute | solution.py:242
  33.0 5.0 %collective-permute-start.12 = (bf16[256,256]{1,0:T(8,128)(2,1)S(1)}, bf16[256,256]{1,0:T(8,128)(2,1)S(1)}, u32[]{:S(2)}, u32[]{:S(2)}) collective-permute-start(bf16[256,256]{1,0:T(8,128)(2,1)S(1)} %get-tuple-element.113), channel_id=1, source_target_pairs={{0,2},{1,5},{2,0},{3,7},{4,6},{5,1},{6,4},{7,3},{8,10},{9,13},{10,... | collective-permute-start | bytes 393224 | tf_op jit(solution)/shard_map/ppermute | solution.py:242
  35.3 5.3 %collective-permute-start.18 = (bf16[128,256]{1,0:T(8,128)(2,1)S(1)}, bf16[128,256]{1,0:T(8,128)(2,1)S(1)}, u32[]{:S(2)}, u32[]{:S(2)}) collective-permute-start(bf16[128,256]{1,0:T(8,128)(2,1)S(1)} %select_convert_fusion.9), channel_id=1, source_target_pairs={{0,4},{1,9},{2,6},{3,11},{4,0},{5,13},{6,2},{7,15},{8,12},{9,1},{1... | collective-permute-start | bytes 196616 | tf_op jit(solution)/shard_map/ppermute | solution.py:242
  38.1 7.3 %collective-permute-start.17 = (bf16[128,256]{1,0:T(8,128)(2,1)S(1)}, bf16[128,256]{1,0:T(8,128)(2,1)S(1)}, u32[]{:S(2)}, u32[]{:S(2)}) collective-permute-start(bf16[128,256]{1,0:T(8,128)(2,1)S(1)} %select_convert_fusion.8), channel_id=1, source_target_pairs={{0,4},{1,9},{2,6},{3,11},{4,0},{5,13},{6,2},{7,15},{8,12},{9,1},{1... | collective-permute-start | bytes 196616 | tf_op jit(solution)/shard_map/ppermute | solution.py:242
  40.5 19.6 %collective-permute-start.14 = (bf16[256,512]{1,0:T(8,128)(2,1)S(1)}, bf16[256,512]{1,0:T(8,128)(2,1)S(1)}, u32[]{:S(2)}, u32[]{:S(2)}) collective-permute-start(bf16[256,512]{1,0:T(8,128)(2,1)S(1)} %get-tuple-element.90), channel_id=1, source_target_pairs={{0,1},{2,0},{4,2},{6,4},{8,6},{10,8},{12,10},{14,12},{16,14},{18,1... | collective-permute-start | bytes 786440 | tf_op jit(solution)/shard_map/ppermute | solution.py:35
  40.5 19.6 %collective-permute-start.15 = (bf16[256,512]{1,0:T(8,128)(2,1)S(1)}, bf16[256,512]{1,0:T(8,128)(2,1)S(1)}, u32[]{:S(2)}, u32[]{:S(2)}) collective-permute-start(bf16[256,512]{1,0:T(8,128)(2,1)S(1)} %get-tuple-element.92), channel_id=1, source_target_pairs={{0,3},{2,1},{4,0},{6,2},{8,4},{10,6},{12,8},{14,10},{16,12},{18,14... | collective-permute-start | bytes 786440 | tf_op jit(solution)/shard_map/ppermute | solution.py:35
  40.6 12.2 %collective-permute-start.20 = (bf16[128,256]{1,0:T(8,128)(2,1)S(1)}, bf16[128,256]{1,0:T(8,128)(2,1)S(1)}, u32[]{:S(2)}, u32[]{:S(2)}) collective-permute-start(bf16[128,256]{1,0:T(8,128)(2,1)S(1)} %add_convert_fusion.4), channel_id=1, source_target_pairs={{0,16},{1,17},{2,18},{3,19},{4,20},{5,21},{6,22},{7,23},{8,24},{9,... | collective-permute-start | bytes 196616 | tf_op jit(solution)/shard_map/ppermute | solution.py:261
  45.5 8.1 %collective-permute-start.19 = (bf16[128,256]{1,0:T(8,128)(2,1)S(1)}, bf16[128,256]{1,0:T(8,128)(2,1)S(1)}, u32[]{:S(2)}, u32[]{:S(2)}) collective-permute-start(bf16[128,256]{1,0:T(8,128)(2,1)S(1)} %add_convert_fusion.3), channel_id=1, source_target_pairs={{0,16},{1,17},{2,18},{3,19},{4,20},{5,21},{6,22},{7,23},{8,24},{9,... | collective-permute-start | bytes 196616 | tf_op jit(solution)/shard_map/ppermute | solution.py:261
  52.9 4.3 %collective-permute-start.22 = (bf16[128,256]{1,0:T(8,128)(2,1)S(1)}, bf16[128,256]{1,0:T(8,128)(2,1)S(1)}, u32[]{:S(2)}, u32[]{:S(2)}) collective-permute-start(bf16[128,256]{1,0:T(8,128)(2,1)S(1)} %add_convert_fusion.1), channel_id=1, source_target_pairs={{0,4},{1,9},{2,6},{3,11},{4,0},{5,13},{6,2},{7,15},{8,12},{9,1},{1... | collective-permute-start | bytes 196616 | tf_op jit(solution)/shard_map/ppermute | solution.py:242
  53.6 4.6 %collective-permute-start.21 = (bf16[128,256]{1,0:T(8,128)(2,1)S(1)}, bf16[128,256]{1,0:T(8,128)(2,1)S(1)}, u32[]{:S(2)}, u32[]{:S(2)}) collective-permute-start(bf16[128,256]{1,0:T(8,128)(2,1)S(1)} %add_convert_fusion.2), channel_id=1, source_target_pairs={{0,4},{1,9},{2,6},{3,11},{4,0},{5,13},{6,2},{7,15},{8,12},{9,1},{1... | collective-permute-start | bytes 196616 | tf_op jit(solution)/shard_map/ppermute | solution.py:242
  57.2 5.0 %collective-permute-start.24 = (bf16[256,256]{1,0:T(8,128)(2,1)S(1)}, bf16[256,256]{1,0:T(8,128)(2,1)S(1)}, u32[]{:S(2)}, u32[]{:S(2)}) collective-permute-start(bf16[256,256]{1,0:T(8,128)(2,1)S(1)} %pad_maximum_fusion.4), channel_id=1, source_target_pairs={{0,2},{1,5},{2,0},{3,7},{4,6},{5,1},{6,4},{7,3},{8,10},{9,13},{10,... | collective-permute-start | bytes 393224 | tf_op jit(solution)/shard_map/ppermute | solution.py:242
  58.2 6.2 %collective-permute-start.23 = (bf16[256,256]{1,0:T(8,128)(2,1)S(1)}, bf16[256,256]{1,0:T(8,128)(2,1)S(1)}, u32[]{:S(2)}, u32[]{:S(2)}) collective-permute-start(bf16[256,256]{1,0:T(8,128)(2,1)S(1)} %pad_maximum_fusion.5), channel_id=1, source_target_pairs={{0,2},{1,5},{2,0},{3,7},{4,6},{5,1},{6,4},{7,3},{8,10},{9,13},{10,... | collective-permute-start | bytes 393224 | tf_op jit(solution)/shard_map/ppermute | solution.py:242
  60.2 6.4 %collective-permute-start.16 = (bf16[256,512]{1,0:T(8,128)(2,1)S(1)}, bf16[256,512]{1,0:T(8,128)(2,1)S(1)}, u32[]{:S(2)}, u32[]{:S(2)}) collective-permute-start(bf16[256,512]{1,0:T(8,128)(2,1)S(1)} %add_convert_fusion), channel_id=1, source_target_pairs={{0,1},{1,0},{2,3},{3,2},{4,5},{5,4},{6,7},{7,6},{8,9},{9,8},{10,11... | collective-permute-start | bytes 786440 | tf_op jit(solution)/shard_map/ppermute | solution.py:25
  62.3 6.5 %collective-permute-start.26 = (bf16[512,256]{1,0:T(8,128)(2,1)S(1)}, bf16[512,256]{1,0:T(8,128)(2,1)S(1)}, u32[]{:S(2)}, u32[]{:S(2)}) collective-permute-start(bf16[512,256]{1,0:T(8,128)(2,1)S(1)} %pad_maximum_fusion.2), channel_id=1, source_target_pairs={{0,8},{1,3},{2,10},{3,1},{4,12},{5,7},{6,14},{7,5},{8,0},{9,11},{1... | collective-permute-start | bytes 786440 | tf_op jit(solution)/shard_map/ppermute | solution.py:242
  64.5 7.1 %collective-permute-start.25 = (bf16[512,256]{1,0:T(8,128)(2,1)S(1)}, bf16[512,256]{1,0:T(8,128)(2,1)S(1)}, u32[]{:S(2)}, u32[]{:S(2)}) collective-permute-start(bf16[512,256]{1,0:T(8,128)(2,1)S(1)} %pad_maximum_fusion.3), channel_id=1, source_target_pairs={{0,8},{1,3},{2,10},{3,1},{4,12},{5,7},{6,14},{7,5},{8,0},{9,11},{1... | collective-permute-start | bytes 786440 | tf_op jit(solution)/shard_map/ppermute | solution.py:242

commit v4 on v3

--- a/solution.py
+++ b/solution.py
@@ -39,7 +39,7 @@
     bits = lax.axis_size("tm").bit_length() - 1
     count = min(3, bits)
     first = list(range(count))
-    return first[-1:] + first[:-1], first, list(range(count, bits))
+    return first[1:] + first[:1], first, list(range(count, bits))
 
 
 def partners(bit0, bit1):
@@ -338,8 +338,10 @@
     for step in range(steps):
         sum_a.halve(step, *([sum_b.send] if step else []))
         sum_b.halve(step, sum_a.send)
-    halo_one = shift_blocks(tied(to_one, sum_b.send), -1)
-    halo_two = shift_blocks(tied(to_two, sum_b.send), -2)
+        if step == min(1, steps - 1):
+            halo_one = shift_blocks(tied(to_one, sum_b.send), -1)
+        if step == steps - 1:
+            halo_two = shift_blocks(tied(to_two, sum_b.send), -2)
     sum_a.exchange(sum_b.send)
     sum_b.exchange(sum_a.send)
     for step in reversed(range(steps)):

time: 72.8 us -> 71.9 us (0.988)
  starting transfers between devices: 37.4 us -> 25.3 us
  waiting for transfers between devices: 16.3 us -> 27.4 us
    ppermute x12, waiting for transfers between devices: 9.71 us -> 16.8 us  [passed(): lax.ppermute(x, AXES, partners(*(order[step] for order in self.orders)))]
    ppermute x2, starting transfers between devices: 10.5 us -> 3.57 us  [exchange(): got = lax.ppermute(self.send, AXES, partners(bit, bit))]
    ppermute x12, starting transfers between devices: 20.3 us -> 15.2 us  [passed(): lax.ppermute(x, AXES, partners(*(order[step] for order in self.orders)))]
    ppermute x2, waiting for transfers between devices: 2.27 us -> 6.29 us  [exchange(): got = lax.ppermute(self.send, AXES, partners(bit, bit))]
  transfers between devices with their start and end apart: 27 -> 27, of which waited for: 12 -> 14; matrix products, arithmetic and copies ran while one was open for 5% -> 5% of each run, Pallas kernels for 10% -> 10%
where the time goes in v4:
time: 71.9 us; the launch traced here: 71.7 us
  waiting for transfers between devices  27.4 us (38%)
  starting transfers between devices  25.3 us (35%)
  Pallas kernels  11.4 us (16%)
  other arithmetic  5.64 us (8%)
  local copies, waits for them, and re-layouts  1.11 us (2%)
  between operations  0.89 us (1%)
    ppermute x12, waiting for transfers between devices, passed(): lax.ppermute(x, AXES, partners(*(order[step] for order in self.orders)))  16.8 us
    ppermute x12, starting transfers between devices, passed(): lax.ppermute(x, AXES, partners(*(order[step] for order in self.orders)))  15.2 us
    pallas_call x5, Pallas kernels, call(): pl.pallas_call(kernel, in_specs=[pl.BlockSpec(memory_space=space) for spa...  11.4 us
    ppermute x2, waiting for transfers between devices, exchange(): got = lax.ppermute(self.send, AXES, partners(bit, bit))  6.29 us
    ppermute x4, waiting for transfers between devices, shift_blocks(): return lax.ppermute(x, AXES, route)  4.29 us
    ppermute x4, starting transfers between devices, shift_blocks(): return lax.ppermute(x, AXES, route)  4.08 us
    ppermute x2, starting transfers between devices, exchange(): got = lax.ppermute(self.send, AXES, partners(bit, bit))  3.57 us
    ppermute x9, starting transfers between devices, swap_cores(): return lax.ppermute(x, 'rep', [(0, 1), (1, 0)])  2.37 us
  transfers between devices with their start and end apart: 27, of which 14 were waited for; matrix products, arithmetic and copies ran while one was open for 5% of the time, Pallas kernels for 10%

profile of v4, /device:TPU:0, one launch (start us, length us, event | category | flops | bytes accessed | tf_op | source)
XLA Modules:
  0.0 71.7 jit_solution(8748366769481632067)
XLA Ops:
  2.3 2.6 %collective-permute-start = (bf16[272,512]{1,0:T(8,128)(2,1)S(1)}, bf16[272,512]{1,0:T(8,128)(2,1)S(1)}, u32[]{:S(2)}, u32[]{:S(2)}) collective-permute-start(bf16[272,512]{1,0:T(8,128)(2,1)S(1)} %pad_maximum_fusion.1.parcel_ref.x_ref), channel_id=1, source_target_pairs={{0,2},{2,4},{4,6},{6,8},{8,10},{10,12},{12,14},{14,16},{16,18},{18... | collective-permute-start | bytes 835592 | tf_op jit(solution)/shard_map/ppermute | solution.py:35
  4.8 1.5 %collective-permute-start.1 = (bf16[272,512]{1,0:T(8,128)(2,1)S(1)}, bf16[272,512]{1,0:T(8,128)(2,1)S(1)}, u32[]{:S(2)}, u32[]{:S(2)}) collective-permute-start(bf16[272,512]{1,0:T(8,128)(2,1)S(1)} %pad_maximum_fusion.1.parcel_ref.x_ref), channel_id=1, source_target_pairs={{0,4},{2,6},{4,8},{6,10},{8,12},{10,14},{12,16},{14,18},{16,20},{1... | collective-permute-start | bytes 835592 | tf_op jit(solution)/shard_map/ppermute | solution.py:35
  9.0 2.8 %before.1 = (bf16[256,512]{1,0:T(8,128)(2,1)S(1)}, bf16[256,512]{1,0:T(8,128)(2,1)S(1)}, bf16[256,512]{1,0:T(8,128)(2,1)S(1)}, bf16[256,512]{1,0:T(8,128)(2,1)S(...) custom-call(s32[5]{0:T(128)S(1)} %stack.58.info, ...), custom_call_target="tpu_custom_call" | custom-call | tf_op jit(solution)/shard_map/before/pallas_call | solution.py:65
  11.8 2.1 %collective-permute-done.one_ref = bf16[272,512]{1,0:T(8,128)(2,1)S(1)} collective-permute-done((bf16[272,512]{1,0:T(8,128)(2,1)S(1)}, bf16[272,512]{1,0:T(8,128)(2,1)S(1)}, u32[]{:S(2)}, u32[]{:S(2)}) %collective-permute-start) | collective-permute-done | bytes 278560 | tf_op jit(solution)/shard_map/ppermute | solution.py:35
  14.0 2.2 %collective-permute-done.1.two_ref = bf16[272,512]{1,0:T(8,128)(2,1)S(1)} collective-permute-done((bf16[272,512]{1,0:T(8,128)(2,1)S(1)}, bf16[272,512]{1,0:T(8,128)(2,1)S(1)}, u32[]{:S(2)}, u32[]{:S(2)}) %collective-permute-start.1) | collective-permute-done | bytes 278560 | tf_op jit(solution)/shard_map/ppermute | solution.py:35
  16.1 4.0 %forward.1 = (f32[4,256,768]{2,1,0:T(8,128)S(1)}, bf16[768,512]{1,0:T(8,128)(2,1)S(1)}, bf16[768,512]{1,0:T(8,128)(2,1)S(1)}, f32[1024,256]{1,0:T(8,128)S(1)}, f...) custom-call(f32[2]{0:T(128)S(1)} %copy-done.2, ...), custom_call_target="tpu_custom_call" | custom-call | flops 4294967296 | bytes 4194304 | tf_op jit(solution)/shard_map/forward/pallas_call | solution.py:65
  20.2 2.5 %backward.1 = (f32[1024,256]{1,0:T(8,128)S(1)}, f32[1024,256]{1,0:T(8,128)S(1)}, bf16[256,512]{1,0:T(8,128)(2,1)S(1)}, bf16[768,512]{1,0:T(8,128)(2,1)S(1)}) custom-call(bf16[272,512]{1,0:T(8,128)(2,1)S(1)} %pad_maximum_fusion.1.parcel_ref.x_ref, bf16[272,512]{1,0:T(8,128)(2,1)S(1)} %collective-permute-done.one_ref, ...), custom_call_target="tpu_custom_call" | custom-call | flops 3221225472 | bytes 3145728 | tf_op jit(solution)/shard_map/backward/pallas_call | solution.py:65
  23.6 2.5 %collective-permute-start.11 = (bf16[512,256]{1,0:T(8,128)(2,1)S(1)}, bf16[512,256]{1,0:T(8,128)(2,1)S(1)}, u32[]{:S(2)}, u32[]{:S(2)}) collective-permute-start(bf16[512,256]{1,0:T(8,128)(2,1)S(1)} %get-tuple-element.108), channel_id=1, source_target_pairs={{0,4},{1,3},{2,6},{3,1},{4,0},{5,7},{6,2},{7,5},{8,12},{9,11},{10,... | collective-permute-start | bytes 786440 | tf_op jit(solution)/shard_map/ppermute | solution.py:242
  26.3 2.0 %collective-permute-start.10 = (bf16[512,256]{1,0:T(8,128)(2,1)S(1)}, bf16[512,256]{1,0:T(8,128)(2,1)S(1)}, u32[]{:S(2)}, u32[]{:S(2)}) collective-permute-start(bf16[512,256]{1,0:T(8,128)(2,1)S(1)} %get-tuple-element.109), channel_id=1, source_target_pairs={{0,4},{1,3},{2,6},{3,1},{4,0},{5,7},{6,2},{7,5},{8,12},{9,11},{10,... | collective-permute-start | bytes 786440 | tf_op jit(solution)/shard_map/ppermute | solution.py:242
  28.3 1.3 %tail.1 = (bf16[256,512]{1,0:T(8,128)(2,1)S(1)}, bf16[256,512]{1,0:T(8,128)(2,1)S(1)}, f32[256,512]{1,0:T(8,128)S(1)}, bf16[256,512]{1,0:T(8,128)(2,1)S(1)}) custom-call(bf16[768,512]{1,0:T(8,128)(2,1)S(1)} %get-tuple-element.72.dk_ref, bf16[512,512]{1,0:T(8,128)(2,1)S(1)} %get-tuple-element.66.wk_ref, bf16[768,512]{1,0:T(8,128)(2,1)S(1)} %get-tuple-element.73.dv_ref, ...), custom_call_target="tpu_custom_call" | custom-call | flops 1073741824 | bytes 1048576 | tf_op jit(solution)/shard_map/tail/pallas_call | solution.py:65
  30.5 1.8 %collective-permute-start.14 = (bf16[256,256]{1,0:T(8,128)(2,1)S(1)}, bf16[256,256]{1,0:T(8,128)(2,1)S(1)}, u32[]{:S(2)}, u32[]{:S(2)}) collective-permute-start(bf16[256,256]{1,0:T(8,128)(2,1)S(1)} %get-tuple-element.112), channel_id=1, source_target_pairs={{0,8},{1,5},{2,10},{3,7},{4,12},{5,1},{6,14},{7,3},{8,0},{9,13},{1... | collective-permute-start | bytes 393224 | tf_op jit(solution)/shard_map/ppermute | solution.py:242
  32.3 1.4 %collective-permute-done.10 = bf16[512,256]{1,0:T(8,128)(2,1)S(1)} collective-permute-done((bf16[512,256]{1,0:T(8,128)(2,1)S(1)}, bf16[512,256]{1,0:T(8,128)(2,1)S(1)}, u32[]{:S(2)}, u32[]{:S(2)}) %collective-permute-start.10) | collective-permute-done | bytes 262176 | tf_op jit(solution)/shard_map/ppermute | solution.py:242
  33.7 1.7 %collective-permute-start.13 = (bf16[256,256]{1,0:T(8,128)(2,1)S(1)}, bf16[256,256]{1,0:T(8,128)(2,1)S(1)}, u32[]{:S(2)}, u32[]{:S(2)}) collective-permute-start(bf16[256,256]{1,0:T(8,128)(2,1)S(1)} %get-tuple-element.113), channel_id=1, source_target_pairs={{0,8},{1,5},{2,10},{3,7},{4,12},{5,1},{6,14},{7,3},{8,0},{9,13},{1... | collective-permute-start | bytes 393224 | tf_op jit(solution)/shard_map/ppermute | solution.py:242
  35.6 2.0 %collective-permute-start.18 = (bf16[128,256]{1,0:T(8,128)(2,1)S(1)}, bf16[128,256]{1,0:T(8,128)(2,1)S(1)}, u32[]{:S(2)}, u32[]{:S(2)}) collective-permute-start(bf16[128,256]{1,0:T(8,128)(2,1)S(1)} %select_convert_fusion.9), channel_id=1, source_target_pairs={{0,2},{1,9},{2,0},{3,11},{4,6},{5,13},{6,4},{7,15},{8,10},{9,1},{1... | collective-permute-start | bytes 196616 | tf_op jit(solution)/shard_map/ppermute | solution.py:242
  37.6 1.9 %collective-permute-done.13 = bf16[256,256]{1,0:T(8,128)(2,1)S(1)} collective-permute-done((bf16[256,256]{1,0:T(8,128)(2,1)S(1)}, bf16[256,256]{1,0:T(8,128)(2,1)S(1)}, u32[]{:S(2)}, u32[]{:S(2)}) %collective-permute-start.13) | collective-permute-done | bytes 131104 | tf_op jit(solution)/shard_map/ppermute | solution.py:242
  39.5 1.0 %collective-permute-start.17 = (bf16[128,256]{1,0:T(8,128)(2,1)S(1)}, bf16[128,256]{1,0:T(8,128)(2,1)S(1)}, u32[]{:S(2)}, u32[]{:S(2)}) collective-permute-start(bf16[128,256]{1,0:T(8,128)(2,1)S(1)} %select_convert_fusion.8), channel_id=1, source_target_pairs={{0,2},{1,9},{2,0},{3,11},{4,6},{5,13},{6,4},{7,15},{8,10},{9,1},{1... | collective-permute-start | bytes 196616 | tf_op jit(solution)/shard_map/ppermute | solution.py:242
  40.5 2.6 %collective-permute-done.18 = bf16[128,256]{1,0:T(8,128)(2,1)S(1)} collective-permute-done((bf16[128,256]{1,0:T(8,128)(2,1)S(1)}, bf16[128,256]{1,0:T(8,128)(2,1)S(1)}, u32[]{:S(2)}, u32[]{:S(2)}) %collective-permute-start.18) | collective-permute-done | bytes 65568 | tf_op jit(solution)/shard_map/ppermute | solution.py:242
  43.1 3.1 %collective-permute-start.20 = (bf16[128,256]{1,0:T(8,128)(2,1)S(1)}, bf16[128,256]{1,0:T(8,128)(2,1)S(1)}, u32[]{:S(2)}, u32[]{:S(2)}) collective-permute-start(bf16[128,256]{1,0:T(8,128)(2,1)S(1)} %add_convert_fusion.4), channel_id=1, source_target_pairs={{0,16},{1,17},{2,18},{3,19},{4,20},{5,21},{6,22},{7,23},{8,24},{9,... | collective-permute-start | bytes 196616 | tf_op jit(solution)/shard_map/ppermute | solution.py:261
  46.7 5.1 %collective-permute-done.20 = bf16[128,256]{1,0:T(8,128)(2,1)S(1)} collective-permute-done((bf16[128,256]{1,0:T(8,128)(2,1)S(1)}, bf16[128,256]{1,0:T(8,128)(2,1)S(1)}, u32[]{:S(2)}, u32[]{:S(2)}) %collective-permute-start.20) | collective-permute-done | bytes 65568 | tf_op jit(solution)/shard_map/ppermute | solution.py:261
  51.9 1.2 %collective-permute-done.19 = bf16[128,256]{1,0:T(8,128)(2,1)S(1)} collective-permute-done((bf16[128,256]{1,0:T(8,128)(2,1)S(1)}, bf16[128,256]{1,0:T(8,128)(2,1)S(1)}, u32[]{:S(2)}, u32[]{:S(2)}) %collective-permute-start.19) | collective-permute-done | bytes 65568 | tf_op jit(solution)/shard_map/ppermute | solution.py:261
  53.1 0.9 %collective-permute-start.21 = (bf16[128,256]{1,0:T(8,128)(2,1)S(1)}, bf16[128,256]{1,0:T(8,128)(2,1)S(1)}, u32[]{:S(2)}, u32[]{:S(2)}) collective-permute-start(bf16[128,256]{1,0:T(8,128)(2,1)S(1)} %add_convert_fusion.2), channel_id=1, source_target_pairs={{0,2},{1,9},{2,0},{3,11},{4,6},{5,13},{6,4},{7,15},{8,10},{9,1},{1... | collective-permute-start | bytes 196616 | tf_op jit(solution)/shard_map/ppermute | solution.py:242
  54.0 2.1 %collective-permute-done.22 = bf16[128,256]{1,0:T(8,128)(2,1)S(1)} collective-permute-done((bf16[128,256]{1,0:T(8,128)(2,1)S(1)}, bf16[128,256]{1,0:T(8,128)(2,1)S(1)}, u32[]{:S(2)}, u32[]{:S(2)}) %collective-permute-start.22) | collective-permute-done | bytes 65568 | tf_op jit(solution)/shard_map/ppermute | solution.py:242
  56.2 2.2 %collective-permute-start.24 = (bf16[256,256]{1,0:T(8,128)(2,1)S(1)}, bf16[256,256]{1,0:T(8,128)(2,1)S(1)}, u32[]{:S(2)}, u32[]{:S(2)}) collective-permute-start(bf16[256,256]{1,0:T(8,128)(2,1)S(1)} %pad_maximum_fusion.4), channel_id=1, source_target_pairs={{0,8},{1,5},{2,10},{3,7},{4,12},{5,1},{6,14},{7,3},{8,0},{9,13},{1... | collective-permute-start | bytes 393224 | tf_op jit(solution)/shard_map/ppermute | solution.py:242
  58.4 0.9 %collective-permute-start.23 = (bf16[256,256]{1,0:T(8,128)(2,1)S(1)}, bf16[256,256]{1,0:T(8,128)(2,1)S(1)}, u32[]{:S(2)}, u32[]{:S(2)}) collective-permute-start(bf16[256,256]{1,0:T(8,128)(2,1)S(1)} %pad_maximum_fusion.5), channel_id=1, source_target_pairs={{0,8},{1,5},{2,10},{3,7},{4,12},{5,1},{6,14},{7,3},{8,0},{9,13},{1... | collective-permute-start | bytes 393224 | tf_op jit(solution)/shard_map/ppermute | solution.py:242
  59.5 1.8 %collective-permute-done.24 = bf16[256,256]{1,0:T(8,128)(2,1)S(1)} collective-permute-done((bf16[256,256]{1,0:T(8,128)(2,1)S(1)}, bf16[256,256]{1,0:T(8,128)(2,1)S(1)}, u32[]{:S(2)}, u32[]{:S(2)}) %collective-permute-start.24) | collective-permute-done | bytes 131104 | tf_op jit(solution)/shard_map/ppermute | solution.py:242
  61.5 2.0 %collective-permute-done.23 = bf16[256,256]{1,0:T(8,128)(2,1)S(1)} collective-permute-done((bf16[256,256]{1,0:T(8,128)(2,1)S(1)}, bf16[256,256]{1,0:T(8,128)(2,1)S(1)}, u32[]{:S(2)}, u32[]{:S(2)}) %collective-permute-start.23) | collective-permute-done | bytes 131104 | tf_op jit(solution)/shard_map/ppermute | solution.py:242
  63.6 1.1 %maximum_select_fusion.1 = (bf16[2,256,512]{2,1,0:T(8,128)(2,1)}, bf16[2,256,512]{2,1,0:T(8,128)(2,1)}) fusion(bf16[1,256,512]{2,1,0:T(8,128)(2,1)S(1)} %bitcast.12, bf16[1,256,512]{2,1,0:T(8,128)(2,1)S(1)} %bitcast.14, pred[512]{0:T(512)(128)(4,1)S(1)} %compare_reduce_fusion, bf16[1,256,512]{2,1,0:T(8,128)(2,1)S(1)} %bitcast.13, ...), kind=kLoop, calls=%fused_computation.3 | loop fusion | flops 1572864 | bytes 2097664 | tf_op jit(solution)/shard_map/jit(_where)/select_n | solution.py:358
  64.7 3.1 %collective-permute-done.26 = bf16[512,256]{1,0:T(8,128)(2,1)S(1)} collective-permute-done((bf16[512,256]{1,0:T(8,128)(2,1)S(1)}, bf16[512,256]{1,0:T(8,128)(2,1)S(1)}, u32[]{:S(2)}, u32[]{:S(2)}) %collective-permute-start.26) | collective-permute-done | bytes 262176 | tf_op jit(solution)/shard_map/ppermute | solution.py:242
  67.8 0.9 %select_convert_fusion.4 = (f32[512,256]{1,0:T(8,128)S(1)}, f32[512,256]{1,0:T(8,128)}) fusion(bf16[512,256]{1,0:T(8,128)(2,1)S(1)} %pad_maximum_fusion.2, bf16[512,256]{1,0:T(8,128)(2,1)S(1)} %collective-permute-done.26, pred[256]{0:T(512)(128)(4,1)S(1)} %get-tuple-element.105), kind=kLoop, calls=%fused_computation.19 | loop fusion | flops 524288 | bytes 1573120 | tf_op jit(solution)/shard_map/convert_element_type | solution.py:362
  68.7 0.9 %pad_maximum_fusion = f32[256,512]{1,0:T(8,128)} fusion(f32[256,256]{1,0:T(8,128)S(1)} %get-tuple-element.120, f32[256,256]{1,0:T(8,128)S(1)} %get-tuple-element.119), kind=kLoop, calls=%fused_computation.4 | loop fusion | flops 131072 | bytes 1048576 | tf_op jit(solution)/shard_map/concatenate | solution.py:363
  69.6 1.0 %collective-permute-done.25 = bf16[512,256]{1,0:T(8,128)(2,1)S(1)} collective-permute-done((bf16[512,256]{1,0:T(8,128)(2,1)S(1)}, bf16[512,256]{1,0:T(8,128)(2,1)S(1)}, u32[]{:S(2)}, u32[]{:S(2)}) %collective-permute-start.25) | collective-permute-done | bytes 262176 | tf_op jit(solution)/shard_map/ppermute | solution.py:242
  70.6 1.0 %select_convert_fusion.2 = (f32[512,256]{1,0:T(8,128)}, f32[512,256]{1,0:T(8,128)}) fusion(bf16[512,256]{1,0:T(8,128)(2,1)S(1)} %pad_maximum_fusion.3, bf16[512,256]{1,0:T(8,128)(2,1)S(1)} %collective-permute-done.25, pred[256]{0:T(512)(128)(4,1)S(1)} %get-tuple-element.105), kind=kLoop, calls=%fused_computation.17 | loop fusion | flops 524288 | bytes 1573120 | tf_op jit(solution)/shard_map/convert_element_type | solution.py:365
  (64 shorter events, 7.7 us)
Async XLA Ops:
  0.6 1.1 %copy-start = (bf16[2,256,512]{2,1,0:T(8,128)(2,1)S(1)}, bf16[2,256,512]{2,1,0:T(8,128)(2,1)}, u32[]{:S(2)}) copy-start(bf16[2,256,512]{2,1,0:T(8,128)(2,1)} %param.9) | copy-start | bytes 1572868
  0.6 15.5 %copy-start.2 = (f32[2]{0:T(128)S(1)}, f32[2]{0:T(128)}, u32[]{:S(2)}) copy-start(f32[2]{0:T(128)} %decay_ref.1) | copy-start | bytes 28
  1.8 5.1 %collective-permute-start.2 = (bf16[512,256]{1,0:T(8,128)(2,1)}, bf16[512,256]{1,0:T(8,128)(2,1)S(1)}, u32[]{:S(2)}, u32[]{:S(2)}) collective-permute-start(bf16[512,256]{1,0:T(8,128)(2,1)} %wq_ref.1), channel_id=1, source_target_pairs={{0,1},{1,0},{2,3},{3,2},{4,5},{5,4},{6,7},{7,6},{8,9},{9,8},{10,11... | collective-permute-start | bytes 786440 | tf_op jit(solution)/shard_map/ppermute | solution.py:25
  2.3 11.7 %collective-permute-start = (bf16[272,512]{1,0:T(8,128)(2,1)S(1)}, bf16[272,512]{1,0:T(8,128)(2,1)S(1)}, u32[]{:S(2)}, u32[]{:S(2)}) collective-permute-start(bf16[272,512]{1,0:T(8,128)(2,1)S(1)} %pad_maximum_fusion.1.parcel_ref.x_ref), channel_id=1, source_target_pairs={{0,2},{2,4},{4,6},{6,8},{8,10},{10,12},{12,14},{14,16},{16,18},{18... | collective-permute-start | bytes 835592 | tf_op jit(solution)/shard_map/ppermute | solution.py:35
  4.8 11.3 %collective-permute-start.1 = (bf16[272,512]{1,0:T(8,128)(2,1)S(1)}, bf16[272,512]{1,0:T(8,128)(2,1)S(1)}, u32[]{:S(2)}, u32[]{:S(2)}) collective-permute-start(bf16[272,512]{1,0:T(8,128)(2,1)S(1)} %pad_maximum_fusion.1.parcel_ref.x_ref), channel_id=1, source_target_pairs={{0,4},{2,6},{4,8},{6,10},{8,12},{10,14},{12,16},{14,18},{16,20},{1... | collective-permute-start | bytes 835592 | tf_op jit(solution)/shard_map/ppermute | solution.py:35
  6.4 2.2 %collective-permute-start.3 = (bf16[512,256]{1,0:T(8,128)(2,1)}, bf16[512,256]{1,0:T(8,128)(2,1)S(1)}, u32[]{:S(2)}, u32[]{:S(2)}) collective-permute-start(bf16[512,256]{1,0:T(8,128)(2,1)} %wk_ref.1), channel_id=1, source_target_pairs={{0,1},{1,0},{2,3},{3,2},{4,5},{5,4},{6,7},{7,6},{8,9},{9,8},{10,11... | collective-permute-start | bytes 786440 | tf_op jit(solution)/shard_map/ppermute | solution.py:25
  6.4 2.6 %collective-permute-start.4 = (bf16[512,256]{1,0:T(8,128)(2,1)}, bf16[512,256]{1,0:T(8,128)(2,1)S(1)}, u32[]{:S(2)}, u32[]{:S(2)}) collective-permute-start(bf16[512,256]{1,0:T(8,128)(2,1)} %wv_ref.1), channel_id=1, source_target_pairs={{0,1},{1,0},{2,3},{3,2},{4,5},{5,4},{6,7},{7,6},{8,9},{9,8},{10,11... | collective-permute-start | bytes 786440 | tf_op jit(solution)/shard_map/ppermute | solution.py:25
  6.9 2.2 %collective-permute-start.5 = (bf16[256,512]{1,0:T(8,128)(2,1)}, bf16[256,512]{1,0:T(8,128)(2,1)S(1)}, u32[]{:S(2)}, u32[]{:S(2)}) collective-permute-start(bf16[256,512]{1,0:T(8,128)(2,1)} %wo_ref.1), channel_id=1, source_target_pairs={{0,1},{1,0},{2,3},{3,2},{4,5},{5,4},{6,7},{7,6},{8,9},{9,8},{10,11... | collective-permute-start | bytes 786440 | tf_op jit(solution)/shard_map/ppermute | solution.py:25
  7.0 0.7 copy-start.1
  8.5 3.3 %collective-permute-start.6 = (f32[2]{0:T(128)}, f32[2]{0:T(128)S(1)}, u32[]{:S(2)}, u32[]{:S(2)}) collective-permute-start(f32[2]{0:T(128)} %decay_ref.1), channel_id=1, source_target_pairs={{0,1},{1,0},{2,3},{3,2},{4,5},{5,4},{6,7},{7,6},{8,9},{9,8},{10,11... | collective-permute-start | bytes 32 | tf_op jit(solution)/shard_map/ppermute | solution.py:25
  20.1 3.2 %collective-permute-start.9 = (f32[1024,256]{1,0:T(8,128)S(1)}, f32[1024,256]{1,0:T(8,128)S(1)}, u32[]{:S(2)}, u32[]{:S(2)}) collective-permute-start(f32[1024,256]{1,0:T(8,128)S(1)} %get-tuple-element.84), channel_id=1, source_target_pairs={{0,1},{1,0},{2,3},{3,2},{4,5},{5,4},{6,7},{7,6},{8,9},{9,8},{10,11... | collective-permute-start | bytes 3145736 | tf_op jit(solution)/shard_map/ppermute | solution.py:25
  22.7 3.4 %collective-permute-start.8 = (f32[1024,256]{1,0:T(8,128)S(1)}, f32[1024,256]{1,0:T(8,128)S(1)}, u32[]{:S(2)}, u32[]{:S(2)}) collective-permute-start(f32[1024,256]{1,0:T(8,128)S(1)} %get-tuple-element.82), channel_id=1, source_target_pairs={{0,1},{1,0},{2,3},{3,2},{4,5},{5,4},{6,7},{7,6},{8,9},{9,8},{10,11... | collective-permute-start | bytes 3145736 | tf_op jit(solution)/shard_map/ppermute | solution.py:25
  23.6 6.9 %collective-permute-start.11 = (bf16[512,256]{1,0:T(8,128)(2,1)S(1)}, bf16[512,256]{1,0:T(8,128)(2,1)S(1)}, u32[]{:S(2)}, u32[]{:S(2)}) collective-permute-start(bf16[512,256]{1,0:T(8,128)(2,1)S(1)} %get-tuple-element.108), channel_id=1, source_target_pairs={{0,4},{1,3},{2,6},{3,1},{4,0},{5,7},{6,2},{7,5},{8,12},{9,11},{10,... | collective-permute-start | bytes 786440 | tf_op jit(solution)/shard_map/ppermute | solution.py:242
  26.3 7.4 %collective-permute-start.10 = (bf16[512,256]{1,0:T(8,128)(2,1)S(1)}, bf16[512,256]{1,0:T(8,128)(2,1)S(1)}, u32[]{:S(2)}, u32[]{:S(2)}) collective-permute-start(bf16[512,256]{1,0:T(8,128)(2,1)S(1)} %get-tuple-element.109), channel_id=1, source_target_pairs={{0,4},{1,3},{2,6},{3,1},{4,0},{5,7},{6,2},{7,5},{8,12},{9,11},{10,... | collective-permute-start | bytes 786440 | tf_op jit(solution)/shard_map/ppermute | solution.py:242
  29.6 34.0 %collective-permute-start.7 = (bf16[256,512]{1,0:T(8,128)(2,1)S(1)}, bf16[256,512]{1,0:T(8,128)(2,1)S(1)}, u32[]{:S(2)}, u32[]{:S(2)}) collective-permute-start(bf16[256,512]{1,0:T(8,128)(2,1)S(1)} %get-tuple-element.78), channel_id=1, source_target_pairs={{0,1},{1,0},{2,3},{3,2},{4,5},{5,4},{6,7},{7,6},{8,9},{9,8},{10,11... | collective-permute-start | bytes 786440 | tf_op jit(solution)/shard_map/ppermute | solution.py:25
  30.5 5.0 %collective-permute-start.14 = (bf16[256,256]{1,0:T(8,128)(2,1)S(1)}, bf16[256,256]{1,0:T(8,128)(2,1)S(1)}, u32[]{:S(2)}, u32[]{:S(2)}) collective-permute-start(bf16[256,256]{1,0:T(8,128)(2,1)S(1)} %get-tuple-element.112), channel_id=1, source_target_pairs={{0,8},{1,5},{2,10},{3,7},{4,12},{5,1},{6,14},{7,3},{8,0},{9,13},{1... | collective-permute-start | bytes 393224 | tf_op jit(solution)/shard_map/ppermute | solution.py:242
  33.7 5.7 %collective-permute-start.13 = (bf16[256,256]{1,0:T(8,128)(2,1)S(1)}, bf16[256,256]{1,0:T(8,128)(2,1)S(1)}, u32[]{:S(2)}, u32[]{:S(2)}) collective-permute-start(bf16[256,256]{1,0:T(8,128)(2,1)S(1)} %get-tuple-element.113), channel_id=1, source_target_pairs={{0,8},{1,5},{2,10},{3,7},{4,12},{5,1},{6,14},{7,3},{8,0},{9,13},{1... | collective-permute-start | bytes 393224 | tf_op jit(solution)/shard_map/ppermute | solution.py:242
  35.5 23.8 %collective-permute-start.12 = (bf16[256,512]{1,0:T(8,128)(2,1)S(1)}, bf16[256,512]{1,0:T(8,128)(2,1)S(1)}, u32[]{:S(2)}, u32[]{:S(2)}) collective-permute-start(bf16[256,512]{1,0:T(8,128)(2,1)S(1)} %get-tuple-element.88), channel_id=1, source_target_pairs={{0,1},{2,0},{4,2},{6,4},{8,6},{10,8},{12,10},{14,12},{16,14},{18,1... | collective-permute-start | bytes 786440 | tf_op jit(solution)/shard_map/ppermute | solution.py:35
  35.6 7.5 %collective-permute-start.18 = (bf16[128,256]{1,0:T(8,128)(2,1)S(1)}, bf16[128,256]{1,0:T(8,128)(2,1)S(1)}, u32[]{:S(2)}, u32[]{:S(2)}) collective-permute-start(bf16[128,256]{1,0:T(8,128)(2,1)S(1)} %select_convert_fusion.9), channel_id=1, source_target_pairs={{0,2},{1,9},{2,0},{3,11},{4,6},{5,13},{6,4},{7,15},{8,10},{9,1},{1... | collective-permute-start | bytes 196616 | tf_op jit(solution)/shard_map/ppermute | solution.py:242
  39.5 6.7 %collective-permute-start.17 = (bf16[128,256]{1,0:T(8,128)(2,1)S(1)}, bf16[128,256]{1,0:T(8,128)(2,1)S(1)}, u32[]{:S(2)}, u32[]{:S(2)}) collective-permute-start(bf16[128,256]{1,0:T(8,128)(2,1)S(1)} %select_convert_fusion.8), channel_id=1, source_target_pairs={{0,2},{1,9},{2,0},{3,11},{4,6},{5,13},{6,4},{7,15},{8,10},{9,1},{1... | collective-permute-start | bytes 196616 | tf_op jit(solution)/shard_map/ppermute | solution.py:242
  40.5 18.8 %collective-permute-start.15 = (bf16[256,512]{1,0:T(8,128)(2,1)S(1)}, bf16[256,512]{1,0:T(8,128)(2,1)S(1)}, u32[]{:S(2)}, u32[]{:S(2)}) collective-permute-start(bf16[256,512]{1,0:T(8,128)(2,1)S(1)} %get-tuple-element.92), channel_id=1, source_target_pairs={{0,3},{2,1},{4,0},{6,2},{8,4},{10,6},{12,8},{14,10},{16,12},{18,14... | collective-permute-start | bytes 786440 | tf_op jit(solution)/shard_map/ppermute | solution.py:35
  43.1 8.7 %collective-permute-start.20 = (bf16[128,256]{1,0:T(8,128)(2,1)S(1)}, bf16[128,256]{1,0:T(8,128)(2,1)S(1)}, u32[]{:S(2)}, u32[]{:S(2)}) collective-permute-start(bf16[128,256]{1,0:T(8,128)(2,1)S(1)} %add_convert_fusion.4), channel_id=1, source_target_pairs={{0,16},{1,17},{2,18},{3,19},{4,20},{5,21},{6,22},{7,23},{8,24},{9,... | collective-permute-start | bytes 196616 | tf_op jit(solution)/shard_map/ppermute | solution.py:261
  46.2 6.9 %collective-permute-start.19 = (bf16[128,256]{1,0:T(8,128)(2,1)S(1)}, bf16[128,256]{1,0:T(8,128)(2,1)S(1)}, u32[]{:S(2)}, u32[]{:S(2)}) collective-permute-start(bf16[128,256]{1,0:T(8,128)(2,1)S(1)} %add_convert_fusion.3), channel_id=1, source_target_pairs={{0,16},{1,17},{2,18},{3,19},{4,20},{5,21},{6,22},{7,23},{8,24},{9,... | collective-permute-start | bytes 196616 | tf_op jit(solution)/shard_map/ppermute | solution.py:261
  51.8 4.3 %collective-permute-start.22 = (bf16[128,256]{1,0:T(8,128)(2,1)S(1)}, bf16[128,256]{1,0:T(8,128)(2,1)S(1)}, u32[]{:S(2)}, u32[]{:S(2)}) collective-permute-start(bf16[128,256]{1,0:T(8,128)(2,1)S(1)} %add_convert_fusion.1), channel_id=1, source_target_pairs={{0,2},{1,9},{2,0},{3,11},{4,6},{5,13},{6,4},{7,15},{8,10},{9,1},{1... | collective-permute-start | bytes 196616 | tf_op jit(solution)/shard_map/ppermute | solution.py:242
  53.1 5.3 %collective-permute-start.21 = (bf16[128,256]{1,0:T(8,128)(2,1)S(1)}, bf16[128,256]{1,0:T(8,128)(2,1)S(1)}, u32[]{:S(2)}, u32[]{:S(2)}) collective-permute-start(bf16[128,256]{1,0:T(8,128)(2,1)S(1)} %add_convert_fusion.2), channel_id=1, source_target_pairs={{0,2},{1,9},{2,0},{3,11},{4,6},{5,13},{6,4},{7,15},{8,10},{9,1},{1... | collective-permute-start | bytes 196616 | tf_op jit(solution)/shard_map/ppermute | solution.py:242
  56.2 5.1 %collective-permute-start.24 = (bf16[256,256]{1,0:T(8,128)(2,1)S(1)}, bf16[256,256]{1,0:T(8,128)(2,1)S(1)}, u32[]{:S(2)}, u32[]{:S(2)}) collective-permute-start(bf16[256,256]{1,0:T(8,128)(2,1)S(1)} %pad_maximum_fusion.4), channel_id=1, source_target_pairs={{0,8},{1,5},{2,10},{3,7},{4,12},{5,1},{6,14},{7,3},{8,0},{9,13},{1... | collective-permute-start | bytes 393224 | tf_op jit(solution)/shard_map/ppermute | solution.py:242
  58.4 5.0 %collective-permute-start.23 = (bf16[256,256]{1,0:T(8,128)(2,1)S(1)}, bf16[256,256]{1,0:T(8,128)(2,1)S(1)}, u32[]{:S(2)}, u32[]{:S(2)}) collective-permute-start(bf16[256,256]{1,0:T(8,128)(2,1)S(1)} %pad_maximum_fusion.5), channel_id=1, source_target_pairs={{0,8},{1,5},{2,10},{3,7},{4,12},{5,1},{6,14},{7,3},{8,0},{9,13},{1... | collective-permute-start | bytes 393224 | tf_op jit(solution)/shard_map/ppermute | solution.py:242
  59.4 4.2 %collective-permute-start.16 = (bf16[256,512]{1,0:T(8,128)(2,1)S(1)}, bf16[256,512]{1,0:T(8,128)(2,1)S(1)}, u32[]{:S(2)}, u32[]{:S(2)}) collective-permute-start(bf16[256,512]{1,0:T(8,128)(2,1)S(1)} %add_convert_fusion), channel_id=1, source_target_pairs={{0,1},{1,0},{2,3},{3,2},{4,5},{5,4},{6,7},{7,6},{8,9},{9,8},{10,11... | collective-permute-start | bytes 786440 | tf_op jit(solution)/shard_map/ppermute | solution.py:25
  61.4 6.4 %collective-permute-start.26 = (bf16[512,256]{1,0:T(8,128)(2,1)S(1)}, bf16[512,256]{1,0:T(8,128)(2,1)S(1)}, u32[]{:S(2)}, u32[]{:S(2)}) collective-permute-start(bf16[512,256]{1,0:T(8,128)(2,1)S(1)} %pad_maximum_fusion.2), channel_id=1, source_target_pairs={{0,4},{1,3},{2,6},{3,1},{4,0},{5,7},{6,2},{7,5},{8,12},{9,11},{10,... | collective-permute-start | bytes 786440 | tf_op jit(solution)/shard_map/ppermute | solution.py:242
  63.5 7.1 %collective-permute-start.25 = (bf16[512,256]{1,0:T(8,128)(2,1)S(1)}, bf16[512,256]{1,0:T(8,128)(2,1)S(1)}, u32[]{:S(2)}, u32[]{:S(2)}) collective-permute-start(bf16[512,256]{1,0:T(8,128)(2,1)S(1)} %pad_maximum_fusion.3), channel_id=1, source_target_pairs={{0,4},{1,3},{2,6},{3,1},{4,0},{5,7},{6,2},{7,5},{8,12},{9,11},{10,... | collective-permute-start | bytes 786440 | tf_op jit(solution)/shard_map/ppermute | solution.py:242

commit v5 on v4

--- a/solution.py
+++ b/solution.py
@@ -353,12 +353,14 @@
     grad_own = (to_self + halo_one.astype(F32) + halo_two.astype(F32)).astype(BF)
     on_second = masks[0][None, None] == 1
 
-    def both_blocks(own):
-        other = swap_cores(own)
+    finished = jnp.concatenate([mixed_own, grad_own], 0)
+    others = swap_cores(finished)
+
+    def both_blocks(own, other):
         return jnp.where(on_second, jnp.stack([other, own]), jnp.stack([own, other]))
 
-    mixed = both_blocks(mixed_own)
-    grad_table = both_blocks(grad_own)
+    mixed = both_blocks(mixed_own, others[:blk])
+    grad_table = both_blocks(grad_own, others[blk:])
     grad_value, lines = (part.astype(F32) for part in sum_a.parts)
     grad_out = jnp.concatenate([lines[:cols], lines[cols:]], 1)
     sum_b.placed(0, grad_value, grad_out)

time: 71.9 us -> 73.1 us (1.017)
  waiting for transfers between devices: 27.4 us -> 28.6 us
    ppermute x12, waiting for transfers between devices: 16.8 us -> 18 us  [passed(): lax.ppermute(x, AXES, partners(*(order[step] for order in self.orders)))]
    ppermute x9 -> x8, starting transfers between devices: 2.37 us -> 2.3 us  [swap_cores(): return lax.ppermute(x, 'rep', [(0, 1), (1, 0)])]
  transfers between devices with their start and end apart: 27 -> 26, of which waited for: 14 -> 14; matrix products, arithmetic and copies ran while one was open for 5% -> 5% of each run, Pallas kernels for 10% -> 10%
where the time goes in v5:
time: 73.1 us; the launch traced here: 72.9 us
  waiting for transfers between devices  28.6 us (39%)
  starting transfers between devices  25.2 us (34%)
  Pallas kernels  11.4 us (16%)
  other arithmetic  5.71 us (8%)
  local copies, waits for them, and re-layouts  1.15 us (2%)
  between operations  0.89 us (1%)
    ppermute x12, waiting for transfers between devices, passed(): lax.ppermute(x, AXES, partners(*(order[step] for order in self.orders)))  18 us
    ppermute x12, starting transfers between devices, passed(): lax.ppermute(x, AXES, partners(*(order[step] for order in self.orders)))  15.3 us
    pallas_call x5, Pallas kernels, call(): pl.pallas_call(kernel, in_specs=[pl.BlockSpec(memory_space=space) for spa...  11.4 us
    ppermute x2, waiting for transfers between devices, exchange(): got = lax.ppermute(self.send, AXES, partners(bit, bit))  6.28 us
    ppermute x4, waiting for transfers between devices, shift_blocks(): return lax.ppermute(x, AXES, route)  4.29 us
    ppermute x4, starting transfers between devices, shift_blocks(): return lax.ppermute(x, AXES, route)  4.08 us
    ppermute x2, starting transfers between devices, exchange(): got = lax.ppermute(self.send, AXES, partners(bit, bit))  3.57 us
    ppermute x8, starting transfers between devices, swap_cores(): return lax.ppermute(x, 'rep', [(0, 1), (1, 0)])  2.3 us
  transfers between devices with their start and end apart: 26, of which 14 were waited for; matrix products, arithmetic and copies ran while one was open for 5% of the time, Pallas kernels for 10%

profile of v5, /device:TPU:0, one launch (start us, length us, event | category | flops | bytes accessed | tf_op | source)
XLA Modules:
  0.0 72.9 jit_solution(10077850327219313347)
XLA Ops:
  2.3 2.6 %collective-permute-start = (bf16[272,512]{1,0:T(8,128)(2,1)S(1)}, bf16[272,512]{1,0:T(8,128)(2,1)S(1)}, u32[]{:S(2)}, u32[]{:S(2)}) collective-permute-start(bf16[272,512]{1,0:T(8,128)(2,1)S(1)} %pad_maximum_fusion.2.parcel_ref.x_ref), channel_id=1, source_target_pairs={{0,2},{2,4},{4,6},{6,8},{8,10},{10,12},{12,14},{14,16},{16,18},{18... | collective-permute-start | bytes 835592 | tf_op jit(solution)/shard_map/ppermute | solution.py:35
  4.8 1.5 %collective-permute-start.1 = (bf16[272,512]{1,0:T(8,128)(2,1)S(1)}, bf16[272,512]{1,0:T(8,128)(2,1)S(1)}, u32[]{:S(2)}, u32[]{:S(2)}) collective-permute-start(bf16[272,512]{1,0:T(8,128)(2,1)S(1)} %pad_maximum_fusion.2.parcel_ref.x_ref), channel_id=1, source_target_pairs={{0,4},{2,6},{4,8},{6,10},{8,12},{10,14},{12,16},{14,18},{16,20},{1... | collective-permute-start | bytes 835592 | tf_op jit(solution)/shard_map/ppermute | solution.py:35
  9.0 2.8 %before.1 = (bf16[256,512]{1,0:T(8,128)(2,1)S(1)}, bf16[256,512]{1,0:T(8,128)(2,1)S(1)}, bf16[256,512]{1,0:T(8,128)(2,1)S(1)}, bf16[256,512]{1,0:T(8,128)(2,1)S(...) custom-call(s32[5]{0:T(128)S(1)} %stack.58.info, ...), custom_call_target="tpu_custom_call" | custom-call | tf_op jit(solution)/shard_map/before/pallas_call | solution.py:65
  11.8 2.1 %collective-permute-done.one_ref = bf16[272,512]{1,0:T(8,128)(2,1)S(1)} collective-permute-done((bf16[272,512]{1,0:T(8,128)(2,1)S(1)}, bf16[272,512]{1,0:T(8,128)(2,1)S(1)}, u32[]{:S(2)}, u32[]{:S(2)}) %collective-permute-start) | collective-permute-done | bytes 278560 | tf_op jit(solution)/shard_map/ppermute | solution.py:35
  14.0 2.2 %collective-permute-done.1.two_ref = bf16[272,512]{1,0:T(8,128)(2,1)S(1)} collective-permute-done((bf16[272,512]{1,0:T(8,128)(2,1)S(1)}, bf16[272,512]{1,0:T(8,128)(2,1)S(1)}, u32[]{:S(2)}, u32[]{:S(2)}) %collective-permute-start.1) | collective-permute-done | bytes 278560 | tf_op jit(solution)/shard_map/ppermute | solution.py:35
  16.1 4.0 %forward.1 = (f32[4,256,768]{2,1,0:T(8,128)S(1)}, bf16[768,512]{1,0:T(8,128)(2,1)S(1)}, bf16[768,512]{1,0:T(8,128)(2,1)S(1)}, f32[1024,256]{1,0:T(8,128)S(1)}, f...) custom-call(f32[2]{0:T(128)S(1)} %copy-done.2, ...), custom_call_target="tpu_custom_call" | custom-call | flops 4294967296 | bytes 4194304 | tf_op jit(solution)/shard_map/forward/pallas_call | solution.py:65
  20.2 2.5 %backward.1 = (f32[1024,256]{1,0:T(8,128)S(1)}, f32[1024,256]{1,0:T(8,128)S(1)}, bf16[256,512]{1,0:T(8,128)(2,1)S(1)}, bf16[768,512]{1,0:T(8,128)(2,1)S(1)}) custom-call(bf16[272,512]{1,0:T(8,128)(2,1)S(1)} %pad_maximum_fusion.2.parcel_ref.x_ref, bf16[272,512]{1,0:T(8,128)(2,1)S(1)} %collective-permute-done.one_ref, ...), custom_call_target="tpu_custom_call" | custom-call | flops 3221225472 | bytes 3145728 | tf_op jit(solution)/shard_map/backward/pallas_call | solution.py:65
  23.6 2.5 %collective-permute-start.10 = (bf16[512,256]{1,0:T(8,128)(2,1)S(1)}, bf16[512,256]{1,0:T(8,128)(2,1)S(1)}, u32[]{:S(2)}, u32[]{:S(2)}) collective-permute-start(bf16[512,256]{1,0:T(8,128)(2,1)S(1)} %get-tuple-element.108), channel_id=1, source_target_pairs={{0,4},{1,3},{2,6},{3,1},{4,0},{5,7},{6,2},{7,5},{8,12},{9,11},{10,... | collective-permute-start | bytes 786440 | tf_op jit(solution)/shard_map/ppermute | solution.py:242
  26.3 2.0 %collective-permute-start.9 = (bf16[512,256]{1,0:T(8,128)(2,1)S(1)}, bf16[512,256]{1,0:T(8,128)(2,1)S(1)}, u32[]{:S(2)}, u32[]{:S(2)}) collective-permute-start(bf16[512,256]{1,0:T(8,128)(2,1)S(1)} %get-tuple-element.109), channel_id=1, source_target_pairs={{0,4},{1,3},{2,6},{3,1},{4,0},{5,7},{6,2},{7,5},{8,12},{9,11},{10,... | collective-permute-start | bytes 786440 | tf_op jit(solution)/shard_map/ppermute | solution.py:242
  28.3 1.3 %tail.1 = (bf16[256,512]{1,0:T(8,128)(2,1)S(1)}, bf16[256,512]{1,0:T(8,128)(2,1)S(1)}, f32[256,512]{1,0:T(8,128)S(1)}, bf16[256,512]{1,0:T(8,128)(2,1)S(1)}) custom-call(bf16[768,512]{1,0:T(8,128)(2,1)S(1)} %get-tuple-element.72.dk_ref, bf16[512,512]{1,0:T(8,128)(2,1)S(1)} %get-tuple-element.66.wk_ref, bf16[768,512]{1,0:T(8,128)(2,1)S(1)} %get-tuple-element.73.dv_ref, ...), custom_call_target="tpu_custom_call" | custom-call | flops 1073741824 | bytes 1048576 | tf_op jit(solution)/shard_map/tail/pallas_call | solution.py:65
  29.6 0.9 %collective-permute-done.10 = bf16[512,256]{1,0:T(8,128)(2,1)S(1)} collective-permute-done((bf16[512,256]{1,0:T(8,128)(2,1)S(1)}, bf16[512,256]{1,0:T(8,128)(2,1)S(1)}, u32[]{:S(2)}, u32[]{:S(2)}) %collective-permute-start.10) | collective-permute-done | bytes 262176 | tf_op jit(solution)/shard_map/ppermute | solution.py:242
  30.5 1.8 %collective-permute-start.13 = (bf16[256,256]{1,0:T(8,128)(2,1)S(1)}, bf16[256,256]{1,0:T(8,128)(2,1)S(1)}, u32[]{:S(2)}, u32[]{:S(2)}) collective-permute-start(bf16[256,256]{1,0:T(8,128)(2,1)S(1)} %get-tuple-element.112), channel_id=1, source_target_pairs={{0,8},{1,5},{2,10},{3,7},{4,12},{5,1},{6,14},{7,3},{8,0},{9,13},{1... | collective-permute-start | bytes 393224 | tf_op jit(solution)/shard_map/ppermute | solution.py:242
  32.3 1.5 %collective-permute-done.9 = bf16[512,256]{1,0:T(8,128)(2,1)S(1)} collective-permute-done((bf16[512,256]{1,0:T(8,128)(2,1)S(1)}, bf16[512,256]{1,0:T(8,128)(2,1)S(1)}, u32[]{:S(2)}, u32[]{:S(2)}) %collective-permute-start.9) | collective-permute-done | bytes 262176 | tf_op jit(solution)/shard_map/ppermute | solution.py:242
  33.9 1.6 %collective-permute-start.12 = (bf16[256,256]{1,0:T(8,128)(2,1)S(1)}, bf16[256,256]{1,0:T(8,128)(2,1)S(1)}, u32[]{:S(2)}, u32[]{:S(2)}) collective-permute-start(bf16[256,256]{1,0:T(8,128)(2,1)S(1)} %get-tuple-element.113), channel_id=1, source_target_pairs={{0,8},{1,5},{2,10},{3,7},{4,12},{5,1},{6,14},{7,3},{8,0},{9,13},{1... | collective-permute-start | bytes 393224 | tf_op jit(solution)/shard_map/ppermute | solution.py:242
  35.6 2.0 %collective-permute-start.17 = (bf16[128,256]{1,0:T(8,128)(2,1)S(1)}, bf16[128,256]{1,0:T(8,128)(2,1)S(1)}, u32[]{:S(2)}, u32[]{:S(2)}) collective-permute-start(bf16[128,256]{1,0:T(8,128)(2,1)S(1)} %select_convert_fusion.9), channel_id=1, source_target_pairs={{0,2},{1,9},{2,0},{3,11},{4,6},{5,13},{6,4},{7,15},{8,10},{9,1},{1... | collective-permute-start | bytes 196616 | tf_op jit(solution)/shard_map/ppermute | solution.py:242
  37.6 2.0 %collective-permute-done.12 = bf16[256,256]{1,0:T(8,128)(2,1)S(1)} collective-permute-done((bf16[256,256]{1,0:T(8,128)(2,1)S(1)}, bf16[256,256]{1,0:T(8,128)(2,1)S(1)}, u32[]{:S(2)}, u32[]{:S(2)}) %collective-permute-start.12) | collective-permute-done | bytes 131104 | tf_op jit(solution)/shard_map/ppermute | solution.py:242
  39.7 1.2 %collective-permute-start.16 = (bf16[128,256]{1,0:T(8,128)(2,1)S(1)}, bf16[128,256]{1,0:T(8,128)(2,1)S(1)}, u32[]{:S(2)}, u32[]{:S(2)}) collective-permute-start(bf16[128,256]{1,0:T(8,128)(2,1)S(1)} %select_convert_fusion.8), channel_id=1, source_target_pairs={{0,2},{1,9},{2,0},{3,11},{4,6},{5,13},{6,4},{7,15},{8,10},{9,1},{1... | collective-permute-start | bytes 196616 | tf_op jit(solution)/shard_map/ppermute | solution.py:242
  40.8 2.2 %collective-permute-done.17 = bf16[128,256]{1,0:T(8,128)(2,1)S(1)} collective-permute-done((bf16[128,256]{1,0:T(8,128)(2,1)S(1)}, bf16[128,256]{1,0:T(8,128)(2,1)S(1)}, u32[]{:S(2)}, u32[]{:S(2)}) %collective-permute-start.17) | collective-permute-done | bytes 65568 | tf_op jit(solution)/shard_map/ppermute | solution.py:242
  43.1 3.1 %collective-permute-start.19 = (bf16[128,256]{1,0:T(8,128)(2,1)S(1)}, bf16[128,256]{1,0:T(8,128)(2,1)S(1)}, u32[]{:S(2)}, u32[]{:S(2)}) collective-permute-start(bf16[128,256]{1,0:T(8,128)(2,1)S(1)} %add_convert_fusion.4), channel_id=1, source_target_pairs={{0,16},{1,17},{2,18},{3,19},{4,20},{5,21},{6,22},{7,23},{8,24},{9,... | collective-permute-start | bytes 196616 | tf_op jit(solution)/shard_map/ppermute | solution.py:261
  46.7 5.1 %collective-permute-done.19 = bf16[128,256]{1,0:T(8,128)(2,1)S(1)} collective-permute-done((bf16[128,256]{1,0:T(8,128)(2,1)S(1)}, bf16[128,256]{1,0:T(8,128)(2,1)S(1)}, u32[]{:S(2)}, u32[]{:S(2)}) %collective-permute-start.19) | collective-permute-done | bytes 65568 | tf_op jit(solution)/shard_map/ppermute | solution.py:261
  51.9 1.2 %collective-permute-done.18 = bf16[128,256]{1,0:T(8,128)(2,1)S(1)} collective-permute-done((bf16[128,256]{1,0:T(8,128)(2,1)S(1)}, bf16[128,256]{1,0:T(8,128)(2,1)S(1)}, u32[]{:S(2)}, u32[]{:S(2)}) %collective-permute-start.18) | collective-permute-done | bytes 65568 | tf_op jit(solution)/shard_map/ppermute | solution.py:261
  53.1 0.9 %collective-permute-start.20 = (bf16[128,256]{1,0:T(8,128)(2,1)S(1)}, bf16[128,256]{1,0:T(8,128)(2,1)S(1)}, u32[]{:S(2)}, u32[]{:S(2)}) collective-permute-start(bf16[128,256]{1,0:T(8,128)(2,1)S(1)} %add_convert_fusion.2), channel_id=1, source_target_pairs={{0,2},{1,9},{2,0},{3,11},{4,6},{5,13},{6,4},{7,15},{8,10},{9,1},{1... | collective-permute-start | bytes 196616 | tf_op jit(solution)/shard_map/ppermute | solution.py:242
  54.0 2.1 %collective-permute-done.21 = bf16[128,256]{1,0:T(8,128)(2,1)S(1)} collective-permute-done((bf16[128,256]{1,0:T(8,128)(2,1)S(1)}, bf16[128,256]{1,0:T(8,128)(2,1)S(1)}, u32[]{:S(2)}, u32[]{:S(2)}) %collective-permute-start.21) | collective-permute-done | bytes 65568 | tf_op jit(solution)/shard_map/ppermute | solution.py:242
  56.2 2.2 %collective-permute-start.23 = (bf16[256,256]{1,0:T(8,128)(2,1)S(1)}, bf16[256,256]{1,0:T(8,128)(2,1)S(1)}, u32[]{:S(2)}, u32[]{:S(2)}) collective-permute-start(bf16[256,256]{1,0:T(8,128)(2,1)S(1)} %pad_maximum_fusion.5), channel_id=1, source_target_pairs={{0,8},{1,5},{2,10},{3,7},{4,12},{5,1},{6,14},{7,3},{8,0},{9,13},{1... | collective-permute-start | bytes 393224 | tf_op jit(solution)/shard_map/ppermute | solution.py:242
  58.4 0.9 %collective-permute-start.22 = (bf16[256,256]{1,0:T(8,128)(2,1)S(1)}, bf16[256,256]{1,0:T(8,128)(2,1)S(1)}, u32[]{:S(2)}, u32[]{:S(2)}) collective-permute-start(bf16[256,256]{1,0:T(8,128)(2,1)S(1)} %pad_maximum_fusion.6), channel_id=1, source_target_pairs={{0,8},{1,5},{2,10},{3,7},{4,12},{5,1},{6,14},{7,3},{8,0},{9,13},{1... | collective-permute-start | bytes 393224 | tf_op jit(solution)/shard_map/ppermute | solution.py:242
  59.6 1.8 %collective-permute-done.23 = bf16[256,256]{1,0:T(8,128)(2,1)S(1)} collective-permute-done((bf16[256,256]{1,0:T(8,128)(2,1)S(1)}, bf16[256,256]{1,0:T(8,128)(2,1)S(1)}, u32[]{:S(2)}, u32[]{:S(2)}) %collective-permute-start.23) | collective-permute-done | bytes 131104 | tf_op jit(solution)/shard_map/ppermute | solution.py:242
  61.5 2.0 %collective-permute-done.22 = bf16[256,256]{1,0:T(8,128)(2,1)S(1)} collective-permute-done((bf16[256,256]{1,0:T(8,128)(2,1)S(1)}, bf16[256,256]{1,0:T(8,128)(2,1)S(1)}, u32[]{:S(2)}, u32[]{:S(2)}) %collective-permute-start.22) | collective-permute-done | bytes 131104 | tf_op jit(solution)/shard_map/ppermute | solution.py:242
  63.6 4.2 %collective-permute-done.25 = bf16[512,256]{1,0:T(8,128)(2,1)S(1)} collective-permute-done((bf16[512,256]{1,0:T(8,128)(2,1)S(1)}, bf16[512,256]{1,0:T(8,128)(2,1)S(1)}, u32[]{:S(2)}, u32[]{:S(2)}) %collective-permute-start.25) | collective-permute-done | bytes 262176 | tf_op jit(solution)/shard_map/ppermute | solution.py:242
  67.8 0.9 %select_convert_fusion.4 = (f32[512,256]{1,0:T(8,128)S(1)}, f32[512,256]{1,0:T(8,128)}) fusion(bf16[512,256]{1,0:T(8,128)(2,1)S(1)} %pad_maximum_fusion.3, bf16[512,256]{1,0:T(8,128)(2,1)S(1)} %collective-permute-done.25, pred[256]{0:T(512)(128)(4,1)S(1)} %get-tuple-element.105), kind=kLoop, calls=%fused_computation.22 | loop fusion | flops 524288 | bytes 1573120 | tf_op jit(solution)/shard_map/convert_element_type | solution.py:364
  69.6 1.0 %collective-permute-done.24 = bf16[512,256]{1,0:T(8,128)(2,1)S(1)} collective-permute-done((bf16[512,256]{1,0:T(8,128)(2,1)S(1)}, bf16[512,256]{1,0:T(8,128)(2,1)S(1)}, u32[]{:S(2)}, u32[]{:S(2)}) %collective-permute-start.24) | collective-permute-done | bytes 262176 | tf_op jit(solution)/shard_map/ppermute | solution.py:242
  70.6 1.0 %select_convert_fusion.2 = (f32[512,256]{1,0:T(8,128)}, f32[512,256]{1,0:T(8,128)}) fusion(bf16[512,256]{1,0:T(8,128)(2,1)S(1)} %pad_maximum_fusion.4, bf16[512,256]{1,0:T(8,128)(2,1)S(1)} %collective-permute-done.24, pred[256]{0:T(512)(128)(4,1)S(1)} %get-tuple-element.105), kind=kLoop, calls=%fused_computation.20 | loop fusion | flops 524288 | bytes 1573120 | tf_op jit(solution)/shard_map/convert_element_type | solution.py:367
  71.7 1.2 %maximum_select_fusion.1 = (bf16[2,256,512]{2,1,0:T(8,128)(2,1)}, bf16[2,256,512]{2,1,0:T(8,128)(2,1)}) fusion(bf16[1,256,512]{2,1,0:T(8,128)(2,1)S(1)} %bitcast.14, bf16[1,256,512]{2,1,0:T(8,128)(2,1)S(1)} %get-tuple-element.121, pred[512]{0:T(512)(128)(4,1)S(1)} %compare_reduce_fusion, bf16[1,256,512]{2,1,0:T(8,128)(2,1)S(1)} %get-tuple-element.122, ...), kind=kLoop, calls=%fused_computation.4 | loop fusion | flops 1572864 | bytes 2097664 | tf_op jit(solution)/shard_map/jit(_where)/select_n | solution.py:360
  (64 shorter events, 7.7 us)
Async XLA Ops:
  0.6 1.1 %copy-start = (bf16[2,256,512]{2,1,0:T(8,128)(2,1)S(1)}, bf16[2,256,512]{2,1,0:T(8,128)(2,1)}, u32[]{:S(2)}) copy-start(bf16[2,256,512]{2,1,0:T(8,128)(2,1)} %param.9) | copy-start | bytes 1572868
  0.6 15.5 %copy-start.2 = (f32[2]{0:T(128)S(1)}, f32[2]{0:T(128)}, u32[]{:S(2)}) copy-start(f32[2]{0:T(128)} %decay_ref.1) | copy-start | bytes 28
  1.8 5.1 %collective-permute-start.2 = (bf16[512,256]{1,0:T(8,128)(2,1)}, bf16[512,256]{1,0:T(8,128)(2,1)S(1)}, u32[]{:S(2)}, u32[]{:S(2)}) collective-permute-start(bf16[512,256]{1,0:T(8,128)(2,1)} %wq_ref.1), channel_id=1, source_target_pairs={{0,1},{1,0},{2,3},{3,2},{4,5},{5,4},{6,7},{7,6},{8,9},{9,8},{10,11... | collective-permute-start | bytes 786440 | tf_op jit(solution)/shard_map/ppermute | solution.py:25
  2.3 11.7 %collective-permute-start = (bf16[272,512]{1,0:T(8,128)(2,1)S(1)}, bf16[272,512]{1,0:T(8,128)(2,1)S(1)}, u32[]{:S(2)}, u32[]{:S(2)}) collective-permute-start(bf16[272,512]{1,0:T(8,128)(2,1)S(1)} %pad_maximum_fusion.2.parcel_ref.x_ref), channel_id=1, source_target_pairs={{0,2},{2,4},{4,6},{6,8},{8,10},{10,12},{12,14},{14,16},{16,18},{18... | collective-permute-start | bytes 835592 | tf_op jit(solution)/shard_map/ppermute | solution.py:35
  4.8 11.3 %collective-permute-start.1 = (bf16[272,512]{1,0:T(8,128)(2,1)S(1)}, bf16[272,512]{1,0:T(8,128)(2,1)S(1)}, u32[]{:S(2)}, u32[]{:S(2)}) collective-permute-start(bf16[272,512]{1,0:T(8,128)(2,1)S(1)} %pad_maximum_fusion.2.parcel_ref.x_ref), channel_id=1, source_target_pairs={{0,4},{2,6},{4,8},{6,10},{8,12},{10,14},{12,16},{14,18},{16,20},{1... | collective-permute-start | bytes 835592 | tf_op jit(solution)/shard_map/ppermute | solution.py:35
  6.4 2.2 %collective-permute-start.3 = (bf16[512,256]{1,0:T(8,128)(2,1)}, bf16[512,256]{1,0:T(8,128)(2,1)S(1)}, u32[]{:S(2)}, u32[]{:S(2)}) collective-permute-start(bf16[512,256]{1,0:T(8,128)(2,1)} %wk_ref.1), channel_id=1, source_target_pairs={{0,1},{1,0},{2,3},{3,2},{4,5},{5,4},{6,7},{7,6},{8,9},{9,8},{10,11... | collective-permute-start | bytes 786440 | tf_op jit(solution)/shard_map/ppermute | solution.py:25
  6.4 2.6 %collective-permute-start.4 = (bf16[512,256]{1,0:T(8,128)(2,1)}, bf16[512,256]{1,0:T(8,128)(2,1)S(1)}, u32[]{:S(2)}, u32[]{:S(2)}) collective-permute-start(bf16[512,256]{1,0:T(8,128)(2,1)} %wv_ref.1), channel_id=1, source_target_pairs={{0,1},{1,0},{2,3},{3,2},{4,5},{5,4},{6,7},{7,6},{8,9},{9,8},{10,11... | collective-permute-start | bytes 786440 | tf_op jit(solution)/shard_map/ppermute | solution.py:25
  6.9 2.2 %collective-permute-start.5 = (bf16[256,512]{1,0:T(8,128)(2,1)}, bf16[256,512]{1,0:T(8,128)(2,1)S(1)}, u32[]{:S(2)}, u32[]{:S(2)}) collective-permute-start(bf16[256,512]{1,0:T(8,128)(2,1)} %wo_ref.1), channel_id=1, source_target_pairs={{0,1},{1,0},{2,3},{3,2},{4,5},{5,4},{6,7},{7,6},{8,9},{9,8},{10,11... | collective-permute-start | bytes 786440 | tf_op jit(solution)/shard_map/ppermute | solution.py:25
  7.0 0.7 copy-start.1
  8.5 3.3 %collective-permute-start.6 = (f32[2]{0:T(128)}, f32[2]{0:T(128)S(1)}, u32[]{:S(2)}, u32[]{:S(2)}) collective-permute-start(f32[2]{0:T(128)} %decay_ref.1), channel_id=1, source_target_pairs={{0,1},{1,0},{2,3},{3,2},{4,5},{5,4},{6,7},{7,6},{8,9},{9,8},{10,11... | collective-permute-start | bytes 32 | tf_op jit(solution)/shard_map/ppermute | solution.py:25
  20.1 3.2 %collective-permute-start.8 = (f32[1024,256]{1,0:T(8,128)S(1)}, f32[1024,256]{1,0:T(8,128)S(1)}, u32[]{:S(2)}, u32[]{:S(2)}) collective-permute-start(f32[1024,256]{1,0:T(8,128)S(1)} %get-tuple-element.84), channel_id=1, source_target_pairs={{0,1},{1,0},{2,3},{3,2},{4,5},{5,4},{6,7},{7,6},{8,9},{9,8},{10,11... | collective-permute-start | bytes 3145736 | tf_op jit(solution)/shard_map/ppermute | solution.py:25
  22.7 3.4 %collective-permute-start.7 = (f32[1024,256]{1,0:T(8,128)S(1)}, f32[1024,256]{1,0:T(8,128)S(1)}, u32[]{:S(2)}, u32[]{:S(2)}) collective-permute-start(f32[1024,256]{1,0:T(8,128)S(1)} %get-tuple-element.82), channel_id=1, source_target_pairs={{0,1},{1,0},{2,3},{3,2},{4,5},{5,4},{6,7},{7,6},{8,9},{9,8},{10,11... | collective-permute-start | bytes 3145736 | tf_op jit(solution)/shard_map/ppermute | solution.py:25
  23.6 6.9 %collective-permute-start.10 = (bf16[512,256]{1,0:T(8,128)(2,1)S(1)}, bf16[512,256]{1,0:T(8,128)(2,1)S(1)}, u32[]{:S(2)}, u32[]{:S(2)}) collective-permute-start(bf16[512,256]{1,0:T(8,128)(2,1)S(1)} %get-tuple-element.108), channel_id=1, source_target_pairs={{0,4},{1,3},{2,6},{3,1},{4,0},{5,7},{6,2},{7,5},{8,12},{9,11},{10,... | collective-permute-start | bytes 786440 | tf_op jit(solution)/shard_map/ppermute | solution.py:242
  26.3 7.6 %collective-permute-start.9 = (bf16[512,256]{1,0:T(8,128)(2,1)S(1)}, bf16[512,256]{1,0:T(8,128)(2,1)S(1)}, u32[]{:S(2)}, u32[]{:S(2)}) collective-permute-start(bf16[512,256]{1,0:T(8,128)(2,1)S(1)} %get-tuple-element.109), channel_id=1, source_target_pairs={{0,4},{1,3},{2,6},{3,1},{4,0},{5,7},{6,2},{7,5},{8,12},{9,11},{10,... | collective-permute-start | bytes 786440 | tf_op jit(solution)/shard_map/ppermute | solution.py:242
  30.5 5.0 %collective-permute-start.13 = (bf16[256,256]{1,0:T(8,128)(2,1)S(1)}, bf16[256,256]{1,0:T(8,128)(2,1)S(1)}, u32[]{:S(2)}, u32[]{:S(2)}) collective-permute-start(bf16[256,256]{1,0:T(8,128)(2,1)S(1)} %get-tuple-element.112), channel_id=1, source_target_pairs={{0,8},{1,5},{2,10},{3,7},{4,12},{5,1},{6,14},{7,3},{8,0},{9,13},{1... | collective-permute-start | bytes 393224 | tf_op jit(solution)/shard_map/ppermute | solution.py:242
  33.9 5.7 %collective-permute-start.12 = (bf16[256,256]{1,0:T(8,128)(2,1)S(1)}, bf16[256,256]{1,0:T(8,128)(2,1)S(1)}, u32[]{:S(2)}, u32[]{:S(2)}) collective-permute-start(bf16[256,256]{1,0:T(8,128)(2,1)S(1)} %get-tuple-element.113), channel_id=1, source_target_pairs={{0,8},{1,5},{2,10},{3,7},{4,12},{5,1},{6,14},{7,3},{8,0},{9,13},{1... | collective-permute-start | bytes 393224 | tf_op jit(solution)/shard_map/ppermute | solution.py:242
  35.5 23.8 %collective-permute-start.11 = (bf16[256,512]{1,0:T(8,128)(2,1)S(1)}, bf16[256,512]{1,0:T(8,128)(2,1)S(1)}, u32[]{:S(2)}, u32[]{:S(2)}) collective-permute-start(bf16[256,512]{1,0:T(8,128)(2,1)S(1)} %get-tuple-element.88), channel_id=1, source_target_pairs={{0,1},{2,0},{4,2},{6,4},{8,6},{10,8},{12,10},{14,12},{16,14},{18,1... | collective-permute-start | bytes 786440 | tf_op jit(solution)/shard_map/ppermute | solution.py:35
  35.6 7.5 %collective-permute-start.17 = (bf16[128,256]{1,0:T(8,128)(2,1)S(1)}, bf16[128,256]{1,0:T(8,128)(2,1)S(1)}, u32[]{:S(2)}, u32[]{:S(2)}) collective-permute-start(bf16[128,256]{1,0:T(8,128)(2,1)S(1)} %select_convert_fusion.9), channel_id=1, source_target_pairs={{0,2},{1,9},{2,0},{3,11},{4,6},{5,13},{6,4},{7,15},{8,10},{9,1},{1... | collective-permute-start | bytes 196616 | tf_op jit(solution)/shard_map/ppermute | solution.py:242
  39.7 6.5 %collective-permute-start.16 = (bf16[128,256]{1,0:T(8,128)(2,1)S(1)}, bf16[128,256]{1,0:T(8,128)(2,1)S(1)}, u32[]{:S(2)}, u32[]{:S(2)}) collective-permute-start(bf16[128,256]{1,0:T(8,128)(2,1)S(1)} %select_convert_fusion.8), channel_id=1, source_target_pairs={{0,2},{1,9},{2,0},{3,11},{4,6},{5,13},{6,4},{7,15},{8,10},{9,1},{1... | collective-permute-start | bytes 196616 | tf_op jit(solution)/shard_map/ppermute | solution.py:242
  40.8 18.5 %collective-permute-start.14 = (bf16[256,512]{1,0:T(8,128)(2,1)S(1)}, bf16[256,512]{1,0:T(8,128)(2,1)S(1)}, u32[]{:S(2)}, u32[]{:S(2)}) collective-permute-start(bf16[256,512]{1,0:T(8,128)(2,1)S(1)} %get-tuple-element.92), channel_id=1, source_target_pairs={{0,3},{2,1},{4,0},{6,2},{8,4},{10,6},{12,8},{14,10},{16,12},{18,14... | collective-permute-start | bytes 786440 | tf_op jit(solution)/shard_map/ppermute | solution.py:35
  43.1 8.7 %collective-permute-start.19 = (bf16[128,256]{1,0:T(8,128)(2,1)S(1)}, bf16[128,256]{1,0:T(8,128)(2,1)S(1)}, u32[]{:S(2)}, u32[]{:S(2)}) collective-permute-start(bf16[128,256]{1,0:T(8,128)(2,1)S(1)} %add_convert_fusion.4), channel_id=1, source_target_pairs={{0,16},{1,17},{2,18},{3,19},{4,20},{5,21},{6,22},{7,23},{8,24},{9,... | collective-permute-start | bytes 196616 | tf_op jit(solution)/shard_map/ppermute | solution.py:261
  46.2 6.9 %collective-permute-start.18 = (bf16[128,256]{1,0:T(8,128)(2,1)S(1)}, bf16[128,256]{1,0:T(8,128)(2,1)S(1)}, u32[]{:S(2)}, u32[]{:S(2)}) collective-permute-start(bf16[128,256]{1,0:T(8,128)(2,1)S(1)} %add_convert_fusion.3), channel_id=1, source_target_pairs={{0,16},{1,17},{2,18},{3,19},{4,20},{5,21},{6,22},{7,23},{8,24},{9,... | collective-permute-start | bytes 196616 | tf_op jit(solution)/shard_map/ppermute | solution.py:261
  51.8 4.3 %collective-permute-start.21 = (bf16[128,256]{1,0:T(8,128)(2,1)S(1)}, bf16[128,256]{1,0:T(8,128)(2,1)S(1)}, u32[]{:S(2)}, u32[]{:S(2)}) collective-permute-start(bf16[128,256]{1,0:T(8,128)(2,1)S(1)} %add_convert_fusion.1), channel_id=1, source_target_pairs={{0,2},{1,9},{2,0},{3,11},{4,6},{5,13},{6,4},{7,15},{8,10},{9,1},{1... | collective-permute-start | bytes 196616 | tf_op jit(solution)/shard_map/ppermute | solution.py:242
  53.1 5.3 %collective-permute-start.20 = (bf16[128,256]{1,0:T(8,128)(2,1)S(1)}, bf16[128,256]{1,0:T(8,128)(2,1)S(1)}, u32[]{:S(2)}, u32[]{:S(2)}) collective-permute-start(bf16[128,256]{1,0:T(8,128)(2,1)S(1)} %add_convert_fusion.2), channel_id=1, source_target_pairs={{0,2},{1,9},{2,0},{3,11},{4,6},{5,13},{6,4},{7,15},{8,10},{9,1},{1... | collective-permute-start | bytes 196616 | tf_op jit(solution)/shard_map/ppermute | solution.py:242
  56.2 5.1 %collective-permute-start.23 = (bf16[256,256]{1,0:T(8,128)(2,1)S(1)}, bf16[256,256]{1,0:T(8,128)(2,1)S(1)}, u32[]{:S(2)}, u32[]{:S(2)}) collective-permute-start(bf16[256,256]{1,0:T(8,128)(2,1)S(1)} %pad_maximum_fusion.5), channel_id=1, source_target_pairs={{0,8},{1,5},{2,10},{3,7},{4,12},{5,1},{6,14},{7,3},{8,0},{9,13},{1... | collective-permute-start | bytes 393224 | tf_op jit(solution)/shard_map/ppermute | solution.py:242
  58.4 5.0 %collective-permute-start.22 = (bf16[256,256]{1,0:T(8,128)(2,1)S(1)}, bf16[256,256]{1,0:T(8,128)(2,1)S(1)}, u32[]{:S(2)}, u32[]{:S(2)}) collective-permute-start(bf16[256,256]{1,0:T(8,128)(2,1)S(1)} %pad_maximum_fusion.6), channel_id=1, source_target_pairs={{0,8},{1,5},{2,10},{3,7},{4,12},{5,1},{6,14},{7,3},{8,0},{9,13},{1... | collective-permute-start | bytes 393224 | tf_op jit(solution)/shard_map/ppermute | solution.py:242
  59.5 12.2 %collective-permute-start.15 = (bf16[512,512]{1,0:T(8,128)(2,1)S(1)}, bf16[512,512]{1,0:T(8,128)(2,1)S(1)}, u32[]{:S(2)}, u32[]{:S(2)}) collective-permute-start(bf16[512,512]{1,0:T(8,128)(2,1)S(1)} %pad_maximum_fusion), channel_id=1, source_target_pairs={{0,1},{1,0},{2,3},{3,2},{4,5},{5,4},{6,7},{7,6},{8,9},{9,8},{10,11... | collective-permute-start | bytes 1572872 | tf_op jit(solution)/shard_map/ppermute | solution.py:25
  61.4 6.4 %collective-permute-start.25 = (bf16[512,256]{1,0:T(8,128)(2,1)S(1)}, bf16[512,256]{1,0:T(8,128)(2,1)S(1)}, u32[]{:S(2)}, u32[]{:S(2)}) collective-permute-start(bf16[512,256]{1,0:T(8,128)(2,1)S(1)} %pad_maximum_fusion.3), channel_id=1, source_target_pairs={{0,4},{1,3},{2,6},{3,1},{4,0},{5,7},{6,2},{7,5},{8,12},{9,11},{10,... | collective-permute-start | bytes 786440 | tf_op jit(solution)/shard_map/ppermute | solution.py:242
  63.5 7.1 %collective-permute-start.24 = (bf16[512,256]{1,0:T(8,128)(2,1)S(1)}, bf16[512,256]{1,0:T(8,128)(2,1)S(1)}, u32[]{:S(2)}, u32[]{:S(2)}) collective-permute-start(bf16[512,256]{1,0:T(8,128)(2,1)S(1)} %pad_maximum_fusion.4), channel_id=1, source_target_pairs={{0,4},{1,3},{2,6},{3,1},{4,0},{5,7},{6,2},{7,5},{8,12},{9,11},{10,... | collective-permute-start | bytes 786440 | tf_op jit(solution)/shard_map/ppermute | solution.py:242
